TPU v7x, 32 devices: a whole 2x2x4 slice. The times are simulated.
32 devices in a mesh: dp: 8 (over z, y), context: 4 (over x, core).
Axes of the slice: x: 2, y: 2, z: 4, core: 2. Of those that a mesh axis runs over, the one named last changes fastest.
Arguments:
- tokens: bfloat16 [64, 512, 768], P('dp', 'context'), may hold values from -6 to 6
- cotangent: float32 [64, 512, 768], P('dp', 'context'), may hold values from -6 to 6
- lengths: int32 [64], P('dp'), may hold values from 1 to 512, as said below
- attention_weights: float32 [4, 768, 768], P(None, ('dp', 'context')), may hold values from -0.21875 to 0.21875
- inner_weights: float32 [768, 3072], P(('dp', 'context')), may hold values from -0.21875 to 0.21875
- outer_weights: float32 [3072, 768], P(('dp', 'context')), may hold values from -0.109375 to 0.109375
- inner_bias: float32 [3072], P(('dp', 'context')), may hold values from -3 to 3
- vectors: float32 [8, 768], P(None, ('dp', 'context')), may hold values from -3 to 3, as said below
- attention_first: float32 [4, 768, 768], P(None, ('dp', 'context')), may hold values from -24 to 24
- attention_second: float32 [4, 768, 768], P(None, ('dp', 'context')), may hold values from 1.31072 to 5.24288
- inner_first: float32 [768, 3072], P(('dp', 'context')), may hold values from -56 to 56
- inner_second: float32 [768, 3072], P(('dp', 'context')), may hold values from 6.5536 to 26.2144
- outer_moment_first: float32 [3072, 768], P(('dp', 'context')), may hold values from -64 to 64
- outer_second: float32 [3072, 768], P(('dp', 'context')), may hold values from 9.8304 to 39.3216
- bias_first: float32 [3072], P(('dp', 'context')), may hold values from -48 to 48
- bias_second: float32 [3072], P(('dp', 'context')), may hold values from 5.24288 to 20.97152
- vector_first: float32 [8, 768], P(None, ('dp', 'context')), may hold values from -80 to 80
- vector_second: float32 [8, 768], P(None, ('dp', 'context')), may hold values from 16.384 to 65.536
Outputs:
- output_tokens: bfloat16 [64, 512, 768], P('dp', 'context')
- input_grad: float32 [64, 512, 768], P('dp', 'context')
- attention_grad: float32 [4, 768, 768], P(None, ('dp', 'context'))
- attention_square: float32 [4, 768, 768], P(None, ('dp', 'context'))
- attention_new: float32 [4, 768, 768], P(None, ('dp', 'context'))
- inner_grad: float32 [768, 3072], P(('dp', 'context'))
- inner_square: float32 [768, 3072], P(('dp', 'context'))
- inner_new: float32 [768, 3072], P(('dp', 'context'))
- outer_grad: float32 [3072, 768], P(('dp', 'context'))
- outer_square: float32 [3072, 768], P(('dp', 'context'))
- outer_new: float32 [3072, 768], P(('dp', 'context'))
- bias_grad: float32 [3072], P(('dp', 'context'))
- bias_square: float32 [3072], P(('dp', 'context'))
- bias_new: float32 [3072], P(('dp', 'context'))
- vector_grad: float32 [8, 768], P(None, ('dp', 'context'))
- vector_square: float32 [8, 768], P(None, ('dp', 'context'))
- vector_new: float32 [8, 768], P(None, ('dp', 'context'))
Inputs may be any that keep to these rules, and one draw needn't show every extreme that they name: `lengths`: among the 8 sequences of each index of dp, at least one has length 512. `vectors`: norm gains (rows 4 and 6) lie in 0.5 to 1.5.
All inputs are finite; a program needn't handle non-finite values.
Results may differ from a plain program's by a relative error of at most 0.012.
The roundings to bfloat16 on the way count: a program that leaves them out, or rounds other values in their place, can miss the bound.
Values may be sent and summed in bfloat16 or wider, within the bound.
No kernel may reach another device: no remote copies, remote signals or barrier semaphores. Data moves between devices by JAX's collectives and lax.ppermute only.
A program may use at most 192 MiB of HBM per device.

v0:
```python
import jax
import jax.numpy as jnp
from jax import lax
from jax.sharding import PartitionSpec as P

HEADS = 12
HEAD = 64
STEP = 10


NORM_EPS = 1e-12
BETA_ONE = 0.9
BETA_TWO = 0.999
ADAM_EPS = 1e-06
MATRIX_LEARN_RATE = 0.05
VECTOR_RATE = 0.5
WEIGHT_DECAY = 0.01
MASK_FILL = -1e30


def precise_gelu_activation(value_entries):
    return jax.nn.gelu(value_entries, approximate=False)


def normalize(value_entries, gain_row, shift_row):
    centered = value_entries - jnp.mean(value_entries, axis=-1, keepdims=True)
    variance = jnp.mean(centered * centered, axis=-1, keepdims=True)
    return centered * lax.rsqrt(variance + NORM_EPS) * gain_row + shift_row


def adam_step(weight, gradient, moment_one, moment_two, step_rate, decay_rate):
    first_new = BETA_ONE * moment_one + (1.0 - BETA_ONE) * gradient
    second_new = BETA_TWO * moment_two + (1.0 - BETA_TWO) * gradient * gradient
    first_hat = first_new / (1.0 - BETA_ONE**STEP)
    second_hat = second_new / (1.0 - BETA_TWO**STEP)
    updated = weight - step_rate * (
        first_hat / (jnp.sqrt(second_hat) + ADAM_EPS) + decay_rate * weight
    )
    return (second_new, updated)


def matmul(left, right):
    return jnp.dot(left, right, preferred_element_type=jnp.float32)


def contract_rows(left, right):
    return lax.dot_general(
        left, right, (((0,), (0,)), ((), ())), preferred_element_type=jnp.float32
    )


def times_transpose(left, right):
    return lax.dot_general(
        left, right, (((1,), (1,)), ((), ())), preferred_element_type=jnp.float32
    )


def attend(block_data):
    query_block, key_tile_block, value_block, valid_block = block_data
    scores = jnp.einsum(
        "gqhc,gkhc->ghqk", query_block, key_tile_block, preferred_element_type=jnp.float32
    ) * HEAD ** (-0.5)
    masked = jnp.where(valid_block[:, None, None, :], scores, MASK_FILL)
    row_peak = jnp.max(masked, axis=-1, keepdims=True)
    exponent = jnp.exp(masked - row_peak)
    row_total = jnp.sum(exponent, axis=-1, keepdims=True)
    attention_probability = exponent / row_total
    mixed_heads = jnp.einsum(
        "ghqk,gkhc->gqhc",
        attention_probability.astype(jnp.bfloat16),
        value_block,
        preferred_element_type=jnp.float32,
    )
    return (mixed_heads.astype(jnp.bfloat16), row_peak + jnp.log(row_total))


def attend_query_back(block_data):
    query_block, key_tile_block, value_block, valid_block, normalizer, mixed_grad = block_data
    scores = jnp.einsum(
        "gqhc,gkhc->ghqk", query_block, key_tile_block, preferred_element_type=jnp.float32
    ) * HEAD ** (-0.5)
    attention_probability = jnp.where(
        valid_block[:, None, None, :], jnp.exp(scores - normalizer), 0.0
    )
    prob_grad = jnp.einsum(
        "gqhc,gkhc->ghqk", mixed_grad, value_block, preferred_element_type=jnp.float32
    )
    row_term = jnp.sum(prob_grad * attention_probability, axis=-1, keepdims=True)
    score_low = (attention_probability * (prob_grad - row_term)).astype(jnp.bfloat16)
    query_grad = jnp.einsum(
        "ghqk,gkhc->gqhc", score_low, key_tile_block, preferred_element_type=jnp.float32
    ) * HEAD ** (-0.5)
    return (query_grad, row_term)


def attend_key_back(block_data):
    query_block, key_tile_block, value_block, valid_block, normalizer, row_term, mixed_grad = (
        block_data
    )
    scores = jnp.einsum(
        "gqhc,gkhc->ghqk", query_block, key_tile_block, preferred_element_type=jnp.float32
    ) * HEAD ** (-0.5)
    attention_probability = jnp.where(
        valid_block[:, None, None, :], jnp.exp(scores - normalizer), 0.0
    )
    prob_grad = jnp.einsum(
        "gqhc,gkhc->ghqk", mixed_grad, value_block, preferred_element_type=jnp.float32
    )
    value_grad = jnp.einsum(
        "ghqk,gqhc->gkhc",
        attention_probability.astype(jnp.bfloat16),
        mixed_grad,
        preferred_element_type=jnp.float32,
    )
    score_low = (attention_probability * (prob_grad - row_term)).astype(jnp.bfloat16)
    key_grad = jnp.einsum(
        "ghqk,gqhc->gkhc", score_low, query_block, preferred_element_type=jnp.float32
    ) * HEAD ** (-0.5)
    return (key_grad, value_grad)


def local(
    tokens,
    cotangent,
    lengths,
    attention_weights,
    inner_weights,
    outer_weights,
    inner_bias,
    vectors,
    attention_first,
    attention_second,
    inner_first,
    inner_second,
    outer_moment_first,
    outer_second,
    bias_first,
    bias_second,
    vector_first,
    vector_second,
):
    low_type = jnp.bfloat16
    seq_count, local_len, model_width = tokens.shape
    row_count = seq_count * local_len
    group_size = min(seq_count, 4)
    block_count = seq_count // group_size
    attention_full, inner_full, outer_full, bias_full, vector_full = (
        lax.all_gather(attention_weights.astype(low_type), ("dp", "context"), axis=1, tiled=True),
        lax.all_gather(inner_weights.astype(low_type), ("dp", "context"), axis=0, tiled=True),
        lax.all_gather(outer_weights.astype(low_type), ("dp", "context"), axis=0, tiled=True),
        lax.all_gather(inner_bias.astype(low_type), ("dp", "context"), axis=0, tiled=True),
        lax.all_gather(vectors.astype(low_type), ("dp", "context"), axis=1, tiled=True),
    )
    vector_wide = vector_full.astype(jnp.float32)
    bias_wide = bias_full.astype(jnp.float32)
    token_rows = tokens.reshape(row_count, model_width)
    query_rows = (matmul(token_rows, attention_full[0]) + vector_wide[0]).astype(low_type)
    key_rows = matmul(token_rows, attention_full[1]).astype(low_type)
    value_rows = (matmul(token_rows, attention_full[2]) + vector_wide[1]).astype(low_type)
    key_seq, value_seq = (
        lax.all_gather(
            key_rows.reshape(seq_count, local_len, model_width), "context", axis=1, tiled=True
        ),
        lax.all_gather(
            value_rows.reshape(seq_count, local_len, model_width), "context", axis=1, tiled=True
        ),
    )
    full_len = key_seq.shape[1]
    positions = jnp.arange(full_len, dtype=jnp.int32)
    key_valid = positions[None, :] < lengths[:, None]
    valid_blocks = key_valid.reshape(block_count, group_size, full_len)
    query_blocks = query_rows.reshape(block_count, group_size, local_len, HEADS, HEAD)
    key_blocks = key_seq.reshape(block_count, group_size, full_len, HEADS, HEAD)
    value_blocks = value_seq.reshape(block_count, group_size, full_len, HEADS, HEAD)
    mixed_blocks, normalizer = lax.map(
        attend, (query_blocks, key_blocks, value_blocks, valid_blocks)
    )
    mixed_rows = mixed_blocks.reshape(row_count, model_width)
    branch = matmul(mixed_rows, attention_full[3]) + vector_wide[2]
    first_sum = token_rows.astype(jnp.float32) + branch
    normed, norm_one_back = jax.vjp(normalize, first_sum, vector_wide[4], vector_wide[5])
    normed_low = normed.astype(low_type)
    hidden_pre = matmul(normed_low, inner_full) + bias_wide
    activated, gelu_back = jax.vjp(precise_gelu_activation, hidden_pre)
    activated_low = activated.astype(low_type)
    ffn_out = matmul(activated_low, outer_full) + vector_wide[3]
    second_sum = normed + ffn_out
    result, norm_two_back = jax.vjp(normalize, second_sum, vector_wide[6], vector_wide[7])
    output_tokens = result.astype(low_type).reshape(tokens.shape)
    attention_back, inner_back, outer_back = (
        lax.all_gather(attention_weights.astype(low_type), ("dp", "context"), axis=1, tiled=True),
        lax.all_gather(inner_weights.astype(low_type), ("dp", "context"), axis=0, tiled=True),
        lax.all_gather(outer_weights.astype(low_type), ("dp", "context"), axis=0, tiled=True),
    )
    second_grad, gain_two_grad, shift_two_grad = norm_two_back(
        cotangent.reshape(row_count, model_width)
    )
    ffn_grad_low = second_grad.astype(low_type)
    ffn_bias_grad = jnp.sum(ffn_grad_low.astype(jnp.float32), axis=0)
    outer_grad = contract_rows(activated_low, ffn_grad_low)
    (hidden_grad,) = gelu_back(times_transpose(ffn_grad_low, outer_back))
    hidden_low = hidden_grad.astype(low_type)
    inner_bias_grad = jnp.sum(hidden_low.astype(jnp.float32), axis=0)
    inner_grad = contract_rows(normed_low, hidden_low)
    normed_grad = times_transpose(hidden_low, inner_back) + second_grad
    first_grad, gain_one_grad, shift_one_grad = norm_one_back(normed_grad)
    branch_low = first_grad.astype(low_type)
    branch_bias_grad = jnp.sum(branch_low.astype(jnp.float32), axis=0)
    output_proj_grad = contract_rows(mixed_rows, branch_low)
    mixed_grad = times_transpose(branch_low, attention_back[3]).astype(low_type)
    key_back_seq, value_back_seq = (key_seq, value_seq)
    key_back_blocks = key_back_seq.reshape(block_count, group_size, full_len, HEADS, HEAD)
    value_back_blocks = value_back_seq.reshape(block_count, group_size, full_len, HEADS, HEAD)
    mixed_grad_blocks = mixed_grad.reshape(block_count, group_size, local_len, HEADS, HEAD)
    query_grad, row_terms = lax.map(
        attend_query_back,
        (
            query_blocks,
            key_back_blocks,
            value_back_blocks,
            valid_blocks,
            normalizer,
            mixed_grad_blocks,
        ),
    )
    query_whole, mixed_grad_whole = (
        lax.all_gather(
            query_rows.reshape(seq_count, local_len, model_width), "context", axis=1, tiled=True
        ),
        lax.all_gather(
            mixed_grad.reshape(seq_count, local_len, model_width), "context", axis=1, tiled=True
        ),
    )
    normalizer_whole, row_term_whole = (
        lax.all_gather(
            normalizer.reshape(seq_count, HEADS, local_len), "context", axis=2, tiled=True
        ),
        lax.all_gather(
            row_terms.reshape(seq_count, HEADS, local_len), "context", axis=2, tiled=True
        ),
    )
    local_start = lax.axis_index("context") * local_len
    local_positions = local_start + jnp.arange(local_len, dtype=jnp.int32)
    local_valid = (local_positions[None, :] < lengths[:, None]).reshape(
        block_count, group_size, local_len
    )
    key_grad, value_grad = lax.map(
        attend_key_back,
        (
            query_whole.reshape(block_count, group_size, full_len, HEADS, HEAD),
            key_rows.reshape(block_count, group_size, local_len, HEADS, HEAD),
            value_rows.reshape(block_count, group_size, local_len, HEADS, HEAD),
            local_valid,
            normalizer_whole.reshape(block_count, group_size, HEADS, full_len, 1),
            row_term_whole.reshape(block_count, group_size, HEADS, full_len, 1),
            mixed_grad_whole.reshape(block_count, group_size, full_len, HEADS, HEAD),
        ),
    )
    key_sum = key_grad.reshape(seq_count, local_len, model_width)
    value_sum = value_grad.reshape(seq_count, local_len, model_width)
    query_low = query_grad.reshape(row_count, model_width).astype(low_type)
    key_low = key_sum.reshape(row_count, model_width).astype(low_type)
    value_low = value_sum.reshape(row_count, model_width).astype(low_type)
    attention_grad = jnp.stack(
        [
            contract_rows(token_rows, query_low),
            contract_rows(token_rows, key_low),
            contract_rows(token_rows, value_low),
            output_proj_grad,
        ]
    )
    input_grad = (
        first_grad
        + times_transpose(query_low, attention_back[0])
        + times_transpose(key_low, attention_back[1])
        + times_transpose(value_low, attention_back[2])
    )
    vector_grad = jnp.stack(
        [
            jnp.sum(query_low.astype(jnp.float32), axis=0),
            jnp.sum(value_low.astype(jnp.float32), axis=0),
            branch_bias_grad,
            ffn_bias_grad,
            gain_one_grad,
            shift_one_grad,
            gain_two_grad,
            shift_two_grad,
        ]
    )
    attention_total, inner_total, outer_total, bias_total, vector_total = (
        lax.psum_scatter(attention_grad, ("dp", "context"), scatter_dimension=1, tiled=True),
        lax.psum_scatter(inner_grad, ("dp", "context"), scatter_dimension=0, tiled=True),
        lax.psum_scatter(outer_grad, ("dp", "context"), scatter_dimension=0, tiled=True),
        lax.psum_scatter(inner_bias_grad, ("dp", "context"), scatter_dimension=0, tiled=True),
        lax.psum_scatter(vector_grad, ("dp", "context"), scatter_dimension=1, tiled=True),
    )
    attention_square, attention_new = adam_step(
        attention_weights,
        attention_total,
        attention_first,
        attention_second,
        MATRIX_LEARN_RATE,
        WEIGHT_DECAY,
    )
    inner_square, inner_new = adam_step(
        inner_weights, inner_total, inner_first, inner_second, MATRIX_LEARN_RATE, WEIGHT_DECAY
    )
    outer_square, outer_new = adam_step(
        outer_weights,
        outer_total,
        outer_moment_first,
        outer_second,
        MATRIX_LEARN_RATE,
        WEIGHT_DECAY,
    )
    bias_square, bias_new = adam_step(
        inner_bias, bias_total, bias_first, bias_second, VECTOR_RATE, 0.0
    )
    vector_square, vector_new = adam_step(
        vectors, vector_total, vector_first, vector_second, VECTOR_RATE, 0.0
    )
    return (
        output_tokens,
        input_grad.reshape(tokens.shape),
        attention_total,
        attention_square,
        attention_new,
        inner_total,
        inner_square,
        inner_new,
        outer_total,
        outer_square,
        outer_new,
        bias_total,
        bias_square,
        bias_new,
        vector_total,
        vector_square,
        vector_new,
    )


def solution(mesh):
    placed = (
        P("dp", "context", None),
        P("dp", "context", None),
        P("dp"),
        P(None, ("dp", "context"), None),
        P(("dp", "context"), None),
        P(("dp", "context"), None),
        P(("dp", "context")),
        P(None, ("dp", "context")),
        P(None, ("dp", "context"), None),
        P(None, ("dp", "context"), None),
        P(("dp", "context"), None),
        P(("dp", "context"), None),
        P(("dp", "context"), None),
        P(("dp", "context"), None),
        P(("dp", "context")),
        P(("dp", "context")),
        P(None, ("dp", "context")),
        P(None, ("dp", "context")),
    )
    return jax.shard_map(
        local,
        mesh=mesh,
        in_specs=placed,
        out_specs=(
            P("dp", "context", None),
            P("dp", "context", None),
            P(None, ("dp", "context"), None),
            P(None, ("dp", "context"), None),
            P(None, ("dp", "context"), None),
            P(("dp", "context"), None),
            P(("dp", "context"), None),
            P(("dp", "context"), None),
            P(("dp", "context"), None),
            P(("dp", "context"), None),
            P(("dp", "context"), None),
            P(("dp", "context")),
            P(("dp", "context")),
            P(("dp", "context")),
            P(None, ("dp", "context")),
            P(None, ("dp", "context")),
            P(None, ("dp", "context")),
        ),
        check_vma=False,
    )
```

profile of v0, /device:TPU:0, one launch (start us, length us, event | category | flops | bytes accessed | tf_op | source)
XLA Modules:
  0.0 900.2 jit_solution(14538578683455312996)
XLA Ops:
  9.6 43.8 %all-gather = bf16[32,24,8]{1,2,0:T(8,128)(2,1)S(1)} all-gather(bf16[1,24,8]{1,2,0:T(8,128)(2,1)S(1)} %convert_bitcast_fusion), channel_id=1, replica_groups=mesh['dp'=8,'context'=4] {'dp','context'}, dimensions={0}, use_global_device_ids=true | all-gather | bytes 12672 | tf_op jit(solution)/shard_map/all_gather | solution.py:152
  54.4 23.5 %all-gather.9.cloned.1.call-done = bf16[4,768,768]{2,1,0:T(8,128)(2,1)} async-done(((bf16[4,24,768]{2,1,0:T(8,128)(2,1)}), bf16[4,768,768]{2,1,0:T(8,128)(2,1)}) %all-gather.9.cloned.1.call-update) | async-done | bytes 4718608 | tf_op jit(solution)/shard_map/all_gather | solution.py:148
  88.5 40.2 %all-reduce = bf16[3072]{0:T(1024)(128)(2,1)S(1)} all-reduce(bf16[3072]{0:T(1024)(128)(2,1)S(1)} %dynamic-update-slice), channel_id=1, replica_groups=mesh['dp'=8,'context'=4] {'dp','context'}, use_global_device_ids=true, to_apply=%add | all-reduce | flops 3072 | bytes 12288
  137.9 8.7 copy.106
  146.6 30.6 %all-gather.13.cloned.1.call-done = bf16[8,512,768]{2,1,0:T(8,128)(2,1)} async-done(((bf16[8,128,768]{2,1,0:T(8,128)(2,1)}), bf16[8,512,768]{2,1,0:T(8,128)(2,1)}) %all-gather.13.cloned.1.call-update) | async-done | bytes 6291472 | tf_op jit(solution)/shard_map/all_gather | solution.py:161
  177.2 8.7 copy.108
  185.8 27.6 %while.36 = (s32[]{:T(128)}, bf16[2,4,128,12,64]{2,1,0,4,3:T(4,128)(2,1)S(1)}, f32[2,4,12,128,1]{3,2,1,4,0:T(8,128)S(1)}, bf16[2,4,512,12,64]{2,4,3,1,0:T(8,128)...) while((s32[]{:T(128)}, ...), condition=%wide.region_3.4_spmd, body=%wide.region_0.3_spmd.sunk | while | flops 843442176 | bytes 72600696 | solution.py:175
  224.1 20.1 %all-gather.15.cloned.1.call-done = bf16[768,3072]{1,0:T(8,128)(2,1)} async-done(((bf16[24,3072]{1,0:T(8,128)(2,1)}), bf16[768,3072]{1,0:T(8,128)(2,1)}) %all-gather.15.cloned.1.call-update) | async-done | bytes 4718608 | tf_op jit(solution)/shard_map/all_gather | solution.py:149
  244.2 38.3 %multiply_convert_fusion.8 = (bf16[1024,3072]{1,0:T(8,128)(2,1)}, f32[1024,3072]{1,0:T(8,128)}, f32[1024,3072]{1,0:T(8,128)}) fusion(f32[3072]{0:T(1024)S(1)} %copy-done.48, bf16[768,3072]{1,0:T(8,128)(2,1)} %all-gather.15.cloned.1.call-done, f32[1024,768]{1,0:T(8,128)} %copy-done.4, f32[768]{0:T(1024)S(1)} %copy-done.39, f32[768]{0:T(1024)S(1)} %copy-done.38, ...), kind=kOutput, calls=%fused_computation.89 | convolution fusion | flops 5043388416 | bytes 39348224 | tf_op jit(solution)/shard_map/dot_general | solution.py:43
  282.6 27.4 %all-gather.17.cloned.1.call-done = bf16[3072,768]{1,0:T(8,128)(2,1)} async-done(((bf16[96,768]{1,0:T(8,128)(2,1)}), bf16[3072,768]{1,0:T(8,128)(2,1)}) %all-gather.17.cloned.1.call-update) | async-done | bytes 4718608 | tf_op jit(solution)/shard_map/all_gather | solution.py:150
  310.0 8.8 fusion.108
  328.2 18.9 %convert_reduce_fusion = (f32[3072]{0:T(1024)}, bf16[1024,3072]{1,0:T(8,128)(2,1)}) fusion(f32[1024,3072]{1,0:T(8,128)} %get-tuple-element.423, bf16[1024,768]{1,0:T(8,128)(2,1)} %get-tuple-element.408, bf16[3072,768]{1,0:T(8,128)(2,1)} %all-gather.17.cloned.1.call-done, f32[1024,3072]{1,0:T(8,128)} %get-tuple-element.435, f32[3072]{0:T(1024)S(1)} %copy-done.48), kind=kOutput, calls=%fused_computation.87 | convolution fusion | flops 4885312512 | bytes 37773312 | tf_op jit(solution)/shard_map/dot_general | solution.py:53
  347.0 10.2 %multiply_reduce_fusion.1 = (f32[768]{0:T(1024)}, f32[1024]{0:T(1024)S(1)}, f32[768]{0:T(1024)}, f32[1024,768]{1,0:T(8,128)S(1)}) fusion(f32[1024,768]{1,0:T(8,128)S(1)} %copy-done.5, f32[1024]{0:T(1024)S(1)} %fusion.92, f32[1024]{0:T(1024)S(1)} %broadcast_multiply_fusion.1, f32[768]{0:T(1024)S(1)} %copy-done.38, f32[1024,768]{1,0:T(8,128)S(1)} %get-tuple-element.421, ...), kind=kOutput, calls=%fused_computation.109 | convolution fusion | flops 4839699456 | bytes 20472832 | tf_op jit(solution)/shard_map/dot_general | solution.py:53
  364.4 10.2 %fusion.109 = f32[3072,768]{1,0:T(8,128)} fusion(bf16[1024,3072]{1,0:T(8,128)(2,1)} %get-tuple-element.422, bf16[1024,768]{1,0:T(8,128)(2,1)} %get-tuple-element.408), kind=kOutput, calls=%fused_computation.186 | convolution fusion | flops 4831838208 | bytes 17301504 | tf_op jit(solution)/shard_map/dot_general | solution.py:47
  395.3 10.8 %fusion.95 = f32[768,3072]{1,0:T(8,128)} fusion(bf16[1024,3072]{1,0:T(8,128)(2,1)} %get-tuple-element.440, f32[1024,768]{1,0:T(8,128)S(1)} %copy-done.5, f32[768]{0:T(1024)S(1)} %copy-done.39, f32[768]{0:T(1024)S(1)} %copy-done.38, f32[1024]{0:T(1024)S(1)} %fusion.92, f32[1024]{0:T(1024)S(1)} %broadcast_multiply_fusion.1), kind=kOutput, calls=%fused_computation.180 | convolution fusion | flops 4835770368 | bytes 18888704 | tf_op jit(solution)/shard_map/dot_general | solution.py:47
  408.5 43.9 %while.37 = (s32[]{:T(128)}, bf16[2,4,128,12,64]{2,4,3,1,0:T(8,128)(2,1)}, f32[2,4,12,128,1]{3,2,1,4,0:T(8,128)S(1)}, bf16[2,4,512,12,64]{2,4,3,1,0:T(8,128)(2,1...) while((s32[]{:T(128)}, ...), condition=%wide.region_14.15_spmd, body=%wide.region_12.14_spmd.sunk | while | flops 1242949632 | bytes 77294200 | solution.py:215
  412.8 8.4 multiply_reduce_fusion.7
  421.2 9.2 %bitcast_dynamic-update-slice_fusion.11 = bf16[2,4,128,12,64]{2,4,3,1,0:T(8,128)(2,1)} fusion(bf16[2,4,128,12,64]{2,4,3,1,0:T(8,128)(2,1)} %get-tuple-element.651, s32[]{:T(128)} %get-tuple-element.650, f32[4,12,128,512]{3,2,1,0:T(8,128)} %get-tuple-element.600, f32[4,12,128,512]{3,2,1,0:T(8,128)S(1)} %fusion.158, ...), kind=kOutput, calls=%fused_computation.35.clone.1 | convolution fusion | flops 421920768 | bytes 29936640 | tf_op jit(solution)/shard_map/while/body/eval_jaxpr/ghqk,gkhc->gqhc/dot_general | solution.py:90
  434.6 8.5 multiply_reduce_fusion.7
  443.1 9.3 %bitcast_dynamic-update-slice_fusion.11 = bf16[2,4,128,12,64]{2,4,3,1,0:T(8,128)(2,1)} fusion(bf16[2,4,128,12,64]{2,4,3,1,0:T(8,128)(2,1)} %get-tuple-element.651, s32[]{:T(128)} %get-tuple-element.650, f32[4,12,128,512]{3,2,1,0:T(8,128)} %get-tuple-element.600, f32[4,12,128,512]{3,2,1,0:T(8,128)S(1)} %fusion.158, ...), kind=kOutput, calls=%fused_computation.35.clone.1 | convolution fusion | flops 421920768 | bytes 29936640 | tf_op jit(solution)/shard_map/while/body/eval_jaxpr/ghqk,gkhc->gqhc/dot_general | solution.py:90
  457.4 8.8 copy.115
  466.2 7.3 all_gather.46
  473.5 7.6 all_gather.44
  488.4 9.1 %copy.117 = bf16[8,512,768]{1,2,0:T(8,128)(2,1)} copy(bf16[8,512,768]{2,1,0:T(8,128)(2,1)} %all-gather.21.cloned.1.call-done) | data formatting | bytes 12582912 | tf_op jit(solution)/shard_map/all_gather | solution.py:230
  500.6 54.2 %while.38 = (s32[]{:T(128)}, bf16[2,4,128,12,64]{2,4,3,1,0:T(8,128)(2,1)}, bf16[2,4,128,12,64]{2,4,3,1,0:T(8,128)(2,1)}, bf16[2,4,512,12,64]{2,4,3,1,0:T(8,128)(...) while((s32[]{:T(128)}, ...), condition=%wide.region_16.17_spmd, body=%wide.region_15.16_spmd.sunk | while | flops 1642463232 | bytes 140711184 | solution.py:247
  506.6 6.5 bitcast_dynamic-update-slice_fusion.14
  514.3 13.4 %bitcast_dynamic-update-slice_fusion.13 = bf16[2,4,128,12,64]{2,4,3,1,0:T(8,128)(2,1)} fusion(bf16[2,4,128,12,64]{2,4,3,1,0:T(8,128)(2,1)} %get-tuple-element.682, s32[]{:T(128)} %get-tuple-element.681, f32[4,12,512,128]{3,2,1,0:T(8,128)} %copy-done, f32[4,12,512]{2,1,0:T(8,128)S(1)} %get-tuple-element.613, ...), kind=kOutput, calls=%fused_computation.69.clone.1 | convolution fusion | flops 824573952 | bytes 21432320 | tf_op jit(solution)/shard_map/while/body/eval_jaxpr/ghqk,gqhc->gkhc/dot_general | solution.py:116
  541.4 13.5 %bitcast_dynamic-update-slice_fusion.13 = bf16[2,4,128,12,64]{2,4,3,1,0:T(8,128)(2,1)} fusion(bf16[2,4,128,12,64]{2,4,3,1,0:T(8,128)(2,1)} %get-tuple-element.682, s32[]{:T(128)} %get-tuple-element.681, f32[4,12,512,128]{3,2,1,0:T(8,128)} %copy-done, f32[4,12,512]{2,1,0:T(8,128)S(1)} %get-tuple-element.613, ...), kind=kOutput, calls=%fused_computation.69.clone.1 | convolution fusion | flops 824573952 | bytes 21432320 | tf_op jit(solution)/shard_map/while/body/eval_jaxpr/ghqk,gqhc->gkhc/dot_general | solution.py:116
  577.2 12.3 %copy.124 = f32[4,768,768]{2,0,1:T(4,128)} copy(f32[4,768,768]{1,2,0:T(8,128)} %pad_maximum_fusion) | data formatting | bytes 18874368 | tf_op jit(solution)/shard_map/stack | solution.py:264
  597.7 42.7 %all-reduce.4 = (f32[3072]{0:T(1024)S(1)}, f32[8,768]{1,0:T(8,128)S(1)}) all-reduce(f32[3072]{0:T(1024)S(1)} %copy-done.49, f32[8,768]{1,0:T(8,128)S(1)} %stack.43), channel_id=5, replica_groups=mesh['dp'=8,'context'=4] {'dp','context'}, use_global_device_ids=true, to_apply=%region_21.22.clone | all-reduce | flops 9216 | bytes 73728
  652.3 43.2 %reduce-scatter.4.cloned.1.call-done = f32[24,3072]{1,0:T(8,128)} async-done(((f32[768,3072]{1,0:T(8,128)}), f32[24,3072]{1,0:T(8,128)}) %reduce-scatter.4.cloned.1.call-update) | async-done | bytes 294928 | tf_op jit(solution)/shard_map/reduce_scatter | solution.py:292
  697.8 193.4 %all-reduce.7.cloned.1.call-done = f32[4,768,768]{2,0,1:T(4,128)} async-done(((f32[4,768,768]{2,0,1:T(4,128)}), f32[4,768,768]{2,0,1:T(4,128)}) %all-reduce.7.cloned.1.call-update) | async-done | bytes 9437200
  (291 shorter events, 191.1 us)
Async XLA Ops:
  7.2 70.8 %all-gather.9.cloned.1.call-start = ((), (), s32[]{:S(2)}) async-start(), calls=%async_computation.2 | async-start | bytes 4866048 | tf_op jit(solution)/shard_map/all_gather | solution.py:148
  8.9 129.0 %all-gather.11.cloned.1.call-start = ((), (), s32[]{:S(2)}) async-start(), calls=%async_computation.3 | async-start | bytes 7864320 | tf_op jit(solution)/shard_map/all_gather | solution.py:164
  82.5 94.7 %all-gather.13.cloned.1.call-start = ((), (), s32[]{:S(2)}) async-start(), calls=%async_computation.4 | async-start | bytes 7864320 | tf_op jit(solution)/shard_map/all_gather | solution.py:161
  86.6 157.6 %all-gather.15.cloned.1.call-start = ((), (), s32[]{:S(2)}) async-start(), calls=%async_computation.5 | async-start | bytes 4866048 | tf_op jit(solution)/shard_map/all_gather | solution.py:149
  87.3 222.6 %all-gather.17.cloned.1.call-start = ((), (), s32[]{:S(2)}) async-start(), calls=%async_computation.6 | async-start | bytes 4866048 | tf_op jit(solution)/shard_map/all_gather | solution.py:150
  88.1 369.3 %all-gather.19.cloned.1.call-start = ((), (), s32[]{:S(2)}) async-start(), calls=%async_computation.7 | async-start | bytes 7864320 | tf_op jit(solution)/shard_map/all_gather | solution.py:227
  88.2 44.3 %copy-start.56 = (s32[2,4]{1,0:T(2,128)}, s32[2,4]{1,0:T(2,128)S(1)}, u32[]{:S(2)}) copy-start(s32[2,4]{1,0:T(2,128)S(1)} %lt.40) | copy-start | bytes 100
  137.6 350.8 %all-gather.21.cloned.1.call-start = ((), (), s32[]{:S(2)}) async-start(), calls=%async_computation.8 | async-start | bytes 7864320 | tf_op jit(solution)/shard_map/all_gather | solution.py:230
  146.6 39.3 %copy-start.25 = (bf16[2,4,128,12,64]{2,1,0,4,3:T(4,128)(2,1)S(1)}, bf16[2,4,128,12,64]{2,1,0,4,3:T(4,128)(2,1)}, u32[]{:S(2)}) copy-start(bf16[2,4,128,12,64]{2,1,0,4,3:T(4,128)(2,1)} %custom-call) | copy-start | bytes 4718596
  214.6 7.3 copy-start.2
  214.6 7.3 copy-start.28
  214.6 7.3 copy-start.36
  221.9 22.3 %copy-start.38 = (f32[768]{0:T(1024)S(1)}, f32[768]{0:T(1024)}, u32[]{:S(2)}) copy-start(f32[768]{0:T(1024)} %get-tuple-element.343) | copy-start | bytes 9220
  221.9 22.3 %copy-start.39 = (f32[768]{0:T(1024)S(1)}, f32[768]{0:T(1024)}, u32[]{:S(2)}) copy-start(f32[768]{0:T(1024)} %get-tuple-element.342) | copy-start | bytes 9220
  221.9 22.3 %copy-start.48 = (f32[3072]{0:T(1024)S(1)}, f32[3072]{0:T(1024)}, u32[]{:S(2)}) copy-start(f32[3072]{0:T(1024)} %convert_element_type.125) | copy-start | bytes 36868
  244.2 65.7 %copy-start.5 = (f32[1024,768]{1,0:T(8,128)S(1)}, f32[1024,768]{1,0:T(8,128)}, u32[]{:S(2)}) copy-start(f32[1024,768]{1,0:T(8,128)} %copy-done.4) | copy-start | bytes 9437188
  244.2 65.7 %copy-start.50 = (f32[768]{0:T(1024)S(1)}, f32[768]{0:T(1024)}, u32[]{:S(2)}) copy-start(f32[768]{0:T(1024)} %get-tuple-element.341) | copy-start | bytes 9220
  364.4 285.6 %reduce-scatter.6.cloned.1.call-start = ((), (), s32[]{:S(2)}) async-start(), calls=%async_computation.10 | async-start | bytes 9732096 | tf_op jit(solution)/shard_map/reduce_scatter | solution.py:293
  374.7 320.8 %reduce-scatter.4.cloned.1.call-start = ((), (), s32[]{:S(2)}) async-start(), calls=%async_computation.9 | async-start | bytes 9732096 | tf_op jit(solution)/shard_map/reduce_scatter | solution.py:292
  406.1 485.1 %all-reduce.7.cloned.1.call-start = ((), (), s32[]{:S(2)}) async-start(), calls=%async_computation.11 | async-start | bytes 18874368
  457.4 23.7 %copy-start.22 = (bf16[1024,768]{0,1:T(8,128)(2,1)S(1)}, bf16[1024,768]{0,1:T(8,128)(2,1)}, u32[]{:S(2)}) copy-start(bf16[1024,768]{0,1:T(8,128)(2,1)} %copy-done.21) | copy-start | bytes 4718596
  506.5 6.7 copy-start
  554.9 6.8 copy-start.18
  593.7 46.6 %copy-start.60 = (f32[96]{0:T(128)S(1)}, f32[96]{0:T(128)}, u32[]{:S(2)}) copy-start(f32[96]{0:T(128)} %param.30) | copy-start | bytes 1156
  593.8 46.6 %copy-start.61 = (f32[96]{0:T(128)S(1)}, f32[96]{0:T(128)}, u32[]{:S(2)}) copy-start(f32[96]{0:T(128)} %param.38) | copy-start | bytes 1156
  593.8 46.6 %copy-start.62 = (f32[96]{0:T(128)S(1)}, f32[96]{0:T(128)}, u32[]{:S(2)}) copy-start(f32[96]{0:T(128)} %param.39) | copy-start | bytes 1156
  593.8 47.2 %copy-start.46 = (f32[8,24]{1,0:T(8,128)S(1)}, f32[8,24]{1,0:T(8,128)}, u32[]{:S(2)}) copy-start(f32[8,24]{1,0:T(8,128)} %param.31) | copy-start | bytes 2308
  593.8 47.2 %copy-start.52 = (f32[8,24]{1,0:T(8,128)S(1)}, f32[8,24]{1,0:T(8,128)}, u32[]{:S(2)}) copy-start(f32[8,24]{1,0:T(8,128)} %param.40) | copy-start | bytes 2308
  593.8 47.2 %copy-start.53 = (f32[8,24]{1,0:T(8,128)S(1)}, f32[8,24]{1,0:T(8,128)}, u32[]{:S(2)}) copy-start(f32[8,24]{1,0:T(8,128)} %param.41) | copy-start | bytes 2308
  650.0 242.1 %copy-start.33 = (f32[4,24,768]{2,1,0:T(8,128)S(1)}, f32[4,24,768]{2,1,0:T(8,128)}, u32[]{:S(2)}) copy-start(f32[4,24,768]{2,1,0:T(8,128)} %param.27) | copy-start | bytes 884740
  650.0 242.1 %copy-start.34 = (f32[4,24,768]{2,1,0:T(8,128)S(1)}, f32[4,24,768]{2,1,0:T(8,128)}, u32[]{:S(2)}) copy-start(f32[4,24,768]{2,1,0:T(8,128)} %param.32) | copy-start | bytes 884740
  650.0 242.1 %copy-start.35 = (f32[4,24,768]{2,1,0:T(8,128)S(1)}, f32[4,24,768]{2,1,0:T(8,128)}, u32[]{:S(2)}) copy-start(f32[4,24,768]{2,1,0:T(8,128)} %param.33) | copy-start | bytes 884740
  (53 other events, 191.2 us)
Sparse Core Ops, SparseCore 0:
  11.5 66.3 all-gather.8
  82.5 46.4 all-gather.10
  130.6 46.5 all-gather.12
  180.5 63.6 all-gather.14
  247.5 62.3 all-gather.16
  311.4 45.1 all-gather.18
  364.5 44.9 all-gather.20
  416.0 135.7 reduce-scatter.5
  559.3 136.1 reduce-scatter.3
  701.1 189.9 all-reduce.6
where the time goes:
time: 907 us; the launch traced here: 900 us
  waiting for transfers between devices  338 us (37%)
  matrix products  251 us (28%)
  blocking collectives  142 us (16%)
  local copies, waits for them, and re-layouts  118 us (13%)
  other arithmetic  35.4 us (4%)
  between operations  15.2 us (2%)
    unnamed x11, waiting for transfers between devices  194 us
    unnamed x2, blocking collectives  82.8 us
    dot_general x6, matrix products, matmul(): return jnp.dot(left, right, preferred_element_type=jnp.float32)  62.7 us
    dot_general x6, matrix products, times_transpose(): lax.dot_general(left, right, (((1,), (1,)), ((), ())), preferred_element_...  45.1 us
    all_gather x1, blocking collectives, local(): lax.all_gather(vectors.astype(low_type), ('dp', 'context'), axis=1, tiled...  43.8 us
    reduce_scatter x1, waiting for transfers between devices, local(): lax.psum_scatter(inner_grad, ('dp', 'context'), scatter_dimension=0, tile...  43.2 us
    dot_general x6, matrix products, contract_rows(): lax.dot_general(left, right, (((0,), (0,)), ((), ())), preferred_element_...  33.1 us
    all_gather x1, waiting for transfers between devices, local(): lax.all_gather(key_rows.reshape(seq_count, local_len, model_width), 'cont...  30.6 us
  transfers between devices with their start and end apart: 10, of which 6 were waited for; matrix products, arithmetic and copies ran while one was open for 43% of the time, Pallas kernels for 0%

commit v1 on v0

v1 whole, which is shorter than its diff:
```python
import jax
import jax.numpy as jnp
from jax import lax
from jax.sharding import PartitionSpec as P

HEADS = 12
HEAD = 64
STEP = 10

NORM_EPS = 1e-12
BETA_ONE = 0.9
BETA_TWO = 0.999
ADAM_EPS = 1e-06
MATRIX_LEARN_RATE = 0.05
VECTOR_RATE = 0.5
WEIGHT_DECAY = 0.01
MASK_FILL = -1e30

BOTH = ("dp", "context")
LOW = jnp.bfloat16
WIDE = jnp.float32


def adam_step(weight, gradient, moment_one, moment_two, step_rate, decay_rate):
    first_new = BETA_ONE * moment_one + (1.0 - BETA_ONE) * gradient
    second_new = BETA_TWO * moment_two + (1.0 - BETA_TWO) * gradient * gradient
    first_hat = first_new / (1.0 - BETA_ONE**STEP)
    second_hat = second_new / (1.0 - BETA_TWO**STEP)
    updated = weight - step_rate * (
        first_hat / (jnp.sqrt(second_hat) + ADAM_EPS) + decay_rate * weight
    )
    return (second_new, updated)


def matmul(left, right):
    return jnp.dot(left, right, preferred_element_type=WIDE)


def contract_rows(left, right):
    return lax.dot_general(left, right, (((0,), (0,)), ((), ())), preferred_element_type=WIDE)


def times_transpose(left, right):
    return lax.dot_general(left, right, (((1,), (1,)), ((), ())), preferred_element_type=WIDE)


def swap_bit(value, bit, count):
    return lax.ppermute(value, BOTH, [(i, i ^ (1 << bit)) for i in range(count)])


def my_bit(bit):
    return (lax.axis_index(BOTH) >> bit) & 1


def join(mine, other, bit, axis):
    flag = my_bit(bit) == 1
    return jnp.where(
        flag, jnp.stack([other, mine], axis=axis), jnp.stack([mine, other], axis=axis)
    )


def gather_all(shard, count):
    bits = count.bit_length() - 1
    held = shard
    for place, bit in enumerate(range(bits - 1, 2, -1)):
        held = join(held, swap_bit(held, bit, count), bit, place)
    place = bits - 3
    half = shard.shape[1] // 2
    first, second = held[..., :half], held[..., half:]
    first = join(first, swap_bit(first, 2, count), 2, place)
    second = join(second, swap_bit(second, 1, count), 1, place)
    first = join(first, swap_bit(first, 1, count), 1, place + 1)
    second = join(second, swap_bit(second, 2, count), 2, place)
    held = jnp.concatenate([first, second], axis=-1)
    held = join(held, swap_bit(held, 0, count), 0, place + 2)
    return held.reshape((count,) + shard.shape)


def halve(partial, bit, axis, count):
    mine = my_bit(bit)
    sent = lax.dynamic_index_in_dim(partial, 1 - mine, axis, keepdims=False)
    kept = lax.dynamic_index_in_dim(partial, mine, axis, keepdims=False)
    return kept.astype(WIDE) + swap_bit(sent, bit, count).astype(WIDE)


def reduce_shards(partial, count, kind=LOW):
    bits = count.bit_length() - 1
    rows, columns = partial.shape[1:]
    partial = partial.astype(kind).reshape((2,) * bits + (rows, columns))
    partial = halve(partial, 0, bits - 1, count).astype(kind)
    half = columns // 2
    first, second = partial[..., :half], partial[..., half:]
    place = bits - 3
    first = halve(first, 1, place + 1, count).astype(kind)
    second = halve(second, 2, place, count).astype(kind)
    first = halve(first, 2, place, count).astype(kind)
    second = halve(second, 1, place, count).astype(kind)
    partial = jnp.concatenate([first, second], axis=-1)
    for place, bit in reversed(list(enumerate(range(bits - 1, 2, -1)))):
        partial = halve(partial, bit, place, count)
        if place:
            partial = partial.astype(kind)
    return partial


def swap_context(value, offset, parts):
    return lax.ppermute(value, "context", [(i, i ^ offset) for i in range(parts)])


def to_sequences(value, parts):
    seqs, here, width = value.shape
    own = seqs // parts
    me = lax.axis_index("context")
    whole = jnp.zeros((own, parts * here, width), value.dtype)
    for offset in range(parts):
        peer = me ^ offset
        block = lax.dynamic_slice_in_dim(value, peer * own, own, 0)
        if offset:
            block = swap_context(block, offset, parts)
        whole = lax.dynamic_update_slice_in_dim(whole, block, peer * here, 1)
    return whole


def to_positions(value, parts):
    own, length, width = value.shape
    here = length // parts
    me = lax.axis_index("context")
    whole = jnp.zeros((own * parts, here, width), value.dtype)
    for offset in range(parts):
        peer = me ^ offset
        block = lax.dynamic_slice_in_dim(value, peer * here, here, 1)
        if offset:
            block = swap_context(block, offset, parts)
        whole = lax.dynamic_update_slice_in_dim(whole, block, peer * own, 0)
    return whole


def norm_stats(value):
    centered = value - jnp.mean(value, axis=-1, keepdims=True)
    variance = jnp.mean(centered * centered, axis=-1, keepdims=True)
    scale = lax.rsqrt(variance + NORM_EPS)
    return centered * scale, scale


def norm_back(grad, gain, unit, scale):
    scaled = grad * gain
    return scale * (
        scaled
        - jnp.mean(scaled, axis=-1, keepdims=True)
        - unit * jnp.mean(scaled * unit, axis=-1, keepdims=True)
    )


def split_heads(rows, seqs):
    return rows.reshape(seqs, -1, HEADS, HEAD)


def attend(query, key, value, valid):
    seqs = valid.shape[0]
    scores = jnp.einsum(
        "gqhc,gkhc->ghqk",
        split_heads(query, seqs),
        split_heads(key, seqs),
        preferred_element_type=WIDE,
    ) * HEAD ** (-0.5)
    masked = jnp.where(valid[:, None, None, :], scores, MASK_FILL)
    peak = jnp.max(masked, axis=-1, keepdims=True)
    exponent = jnp.exp(masked - peak)
    total = jnp.sum(exponent, axis=-1, keepdims=True)
    prob = exponent / total
    mixed = jnp.einsum(
        "ghqk,gkhc->gqhc", prob.astype(LOW), split_heads(value, seqs), preferred_element_type=WIDE
    )
    return mixed.astype(LOW).reshape(query.shape), peak + jnp.log(total)


def attend_back(query, key, value, valid, normalizer, mixed_grad):
    seqs = valid.shape[0]
    shape = query.shape
    query, key, value, mixed_grad = (
        split_heads(query, seqs),
        split_heads(key, seqs),
        split_heads(value, seqs),
        split_heads(mixed_grad, seqs),
    )
    scores = jnp.einsum("gqhc,gkhc->ghqk", query, key, preferred_element_type=WIDE) * HEAD ** (
        -0.5
    )
    prob = jnp.where(valid[:, None, None, :], jnp.exp(scores - normalizer), 0.0)
    prob_grad = jnp.einsum("gqhc,gkhc->ghqk", mixed_grad, value, preferred_element_type=WIDE)
    row_term = jnp.sum(prob_grad * prob, axis=-1, keepdims=True)
    score_low = (prob * (prob_grad - row_term)).astype(LOW)
    query_grad = jnp.einsum(
        "ghqk,gkhc->gqhc", score_low, key, preferred_element_type=WIDE
    ) * HEAD ** (-0.5)
    key_grad = jnp.einsum(
        "ghqk,gqhc->gkhc", score_low, query, preferred_element_type=WIDE
    ) * HEAD ** (-0.5)
    value_grad = jnp.einsum(
        "ghqk,gqhc->gkhc", prob.astype(LOW), mixed_grad, preferred_element_type=WIDE
    )
    return tuple(g.astype(LOW).reshape(shape) for g in (query_grad, key_grad, value_grad))


def local(
    tokens,
    cotangent,
    lengths,
    attention_weights,
    inner_weights,
    outer_weights,
    inner_bias,
    vectors,
    attention_first,
    attention_second,
    inner_first,
    inner_second,
    outer_moment_first,
    outer_second,
    bias_first,
    bias_second,
    vector_first,
    vector_second,
):
    parts = lax.axis_size("context")
    count = lax.axis_size("dp") * parts
    seq_count, local_len, width = tokens.shape
    hidden = inner_weights.shape[1]
    full_len = local_len * parts
    own_seqs = seq_count // parts
    rows = own_seqs * full_len
    att_rows, vec_cols, bias_cols = (
        attention_weights.shape[1],
        vectors.shape[1],
        inner_bias.shape[0],
    )

    small = jnp.concatenate([vectors.reshape(-1), inner_bias]).astype(LOW)
    small_size = small.shape[0]
    small = jnp.pad(small, (0, width - small_size)).reshape(1, width)
    att_shard = jnp.concatenate(
        [attention_weights.astype(LOW).reshape(4 * att_rows, width), small], axis=0
    )
    token_rows = to_sequences(tokens, parts).reshape(rows, width)
    att_all = gather_all(att_shard, count)
    inner_full = gather_all(inner_weights.astype(LOW), count).reshape(width, hidden)
    outer_full = gather_all(outer_weights.astype(LOW), count).reshape(hidden, width)
    cot_rows = to_sequences(cotangent.astype(LOW), parts).reshape(rows, width).astype(WIDE)

    attention_full = (
        att_all[:, : 4 * att_rows]
        .reshape(count, 4, att_rows, width)
        .transpose(1, 0, 2, 3)
        .reshape(4, width, width)
    )
    small_all = att_all[:, 4 * att_rows, :small_size].astype(WIDE)
    vec = (
        small_all[:, : 8 * vec_cols].reshape(count, 8, vec_cols).transpose(1, 0, 2).reshape(8, -1)
    )
    bias = small_all[:, 8 * vec_cols :].reshape(1, -1)

    me = lax.axis_index("context")
    own_lengths = lax.dynamic_slice_in_dim(lengths, me * own_seqs, own_seqs, 0)
    valid = jnp.arange(full_len, dtype=jnp.int32)[None, :] < own_lengths[:, None]

    query = (matmul(token_rows, attention_full[0]) + vec[0]).astype(LOW)
    key = matmul(token_rows, attention_full[1]).astype(LOW)
    value = (matmul(token_rows, attention_full[2]) + vec[1]).astype(LOW)
    mixed, normalizer = attend(query, key, value, valid)
    first_sum = token_rows.astype(WIDE) + matmul(mixed, attention_full[3]) + vec[2]
    unit_one, scale_one = norm_stats(first_sum)
    normed = unit_one * vec[4] + vec[5]
    normed_low = normed.astype(LOW)
    hidden_pre = matmul(normed_low, inner_full) + bias
    activated, gelu_back = jax.vjp(lambda v: jax.nn.gelu(v, approximate=False), hidden_pre)
    activated = activated.astype(LOW)
    second_sum = normed + matmul(activated, outer_full) + vec[3]
    unit_two, scale_two = norm_stats(second_sum)
    result = (unit_two * vec[6] + vec[7]).astype(LOW)
    output_tokens = to_positions(result.reshape(own_seqs, full_len, width), parts)

    second_grad = norm_back(cot_rows, vec[6], unit_two, scale_two)
    ffn_low = second_grad.astype(LOW)
    outer_grad = contract_rows(activated, ffn_low)
    outer_total = reduce_shards(outer_grad.reshape(count, -1, width), count)
    (hidden_grad,) = gelu_back(times_transpose(ffn_low, outer_full))
    hidden_low = hidden_grad.astype(LOW)
    inner_grad = contract_rows(normed_low, hidden_low)
    inner_total = reduce_shards(inner_grad.reshape(count, -1, hidden), count)
    normed_grad = times_transpose(hidden_low, inner_full) + second_grad
    first_grad = norm_back(normed_grad, vec[4], unit_one, scale_one)
    branch_low = first_grad.astype(LOW)
    proj_grad = contract_rows(mixed, branch_low)
    mixed_grad = times_transpose(branch_low, attention_full[3]).astype(LOW)
    query_low, key_low, value_low = attend_back(query, key, value, valid, normalizer, mixed_grad)

    att_grad = jnp.stack(
        [
            contract_rows(token_rows, query_low),
            contract_rows(token_rows, key_low),
            contract_rows(token_rows, value_low),
            proj_grad,
        ]
    )
    att_grad = (
        att_grad.astype(LOW)
        .reshape(4, count, att_rows, width)
        .transpose(1, 0, 2, 3)
        .reshape(count, 4 * att_rows, width)
    )
    attention_total = reduce_shards(att_grad, count).reshape(4, att_rows, width)

    vector_grad = jnp.stack(
        [
            jnp.sum(query_low.astype(WIDE), axis=0),
            jnp.sum(value_low.astype(WIDE), axis=0),
            jnp.sum(branch_low.astype(WIDE), axis=0),
            jnp.sum(ffn_low.astype(WIDE), axis=0),
            jnp.sum(normed_grad * unit_one, axis=0),
            jnp.sum(normed_grad, axis=0),
            jnp.sum(cot_rows * unit_two, axis=0),
            jnp.sum(cot_rows, axis=0),
        ]
    )
    small_grad = jnp.concatenate(
        [
            vector_grad.reshape(8, count, vec_cols).transpose(1, 0, 2).reshape(count, -1),
            jnp.sum(hidden_low.astype(WIDE), axis=0).reshape(count, bias_cols),
        ],
        axis=1,
    )
    small_total = reduce_shards(small_grad[:, None, :], count, WIDE).reshape(-1)
    vector_total = small_total[: 8 * vec_cols].reshape(8, vec_cols)
    bias_total = small_total[8 * vec_cols :]

    input_grad = (
        first_grad
        + times_transpose(query_low, attention_full[0])
        + times_transpose(key_low, attention_full[1])
        + times_transpose(value_low, attention_full[2])
    )
    input_grad = to_positions(
        input_grad.astype(LOW).reshape(own_seqs, full_len, width), parts
    ).astype(WIDE)

    attention_square, attention_new = adam_step(
        attention_weights,
        attention_total,
        attention_first,
        attention_second,
        MATRIX_LEARN_RATE,
        WEIGHT_DECAY,
    )
    inner_square, inner_new = adam_step(
        inner_weights, inner_total, inner_first, inner_second, MATRIX_LEARN_RATE, WEIGHT_DECAY
    )
    outer_square, outer_new = adam_step(
        outer_weights,
        outer_total,
        outer_moment_first,
        outer_second,
        MATRIX_LEARN_RATE,
        WEIGHT_DECAY,
    )
    bias_square, bias_new = adam_step(
        inner_bias, bias_total, bias_first, bias_second, VECTOR_RATE, 0.0
    )
    vector_square, vector_new = adam_step(
        vectors, vector_total, vector_first, vector_second, VECTOR_RATE, 0.0
    )
    return (
        output_tokens,
        input_grad,
        attention_total,
        attention_square,
        attention_new,
        inner_total,
        inner_square,
        inner_new,
        outer_total,
        outer_square,
        outer_new,
        bias_total,
        bias_square,
        bias_new,
        vector_total,
        vector_square,
        vector_new,
    )


def solution(mesh):
    rows3 = P("dp", "context", None)
    mid3 = P(None, BOTH, None)
    row2 = P(BOTH, None)
    col2 = P(None, BOTH)
    one = P(BOTH)
    return jax.shard_map(
        local,
        mesh=mesh,
        in_specs=(rows3, rows3, P("dp"), mid3, row2, row2, one, col2)
        + (mid3, mid3, row2, row2, row2, row2, one, one, col2, col2),
        out_specs=(rows3, rows3)
        + (mid3,) * 3
        + (row2,) * 6
        + (one,) * 3
        + (col2,) * 3,
        check_vma=False,
    )
```

time: 907 us -> 651 us (0.72)
  waiting for transfers between devices: 338 us -> 166 us
  blocking collectives: 142 us -> 0 us
  other arithmetic: 35.4 us -> 111 us
  starting transfers between devices: 0.63 us -> 66.2 us
  matrix products: 251 us -> 193 us
  local copies, waits for them, and re-layouts: 118 us -> 103 us
  between operations: 15.2 us -> 2.82 us
    unnamed x11 -> x0, waiting for transfers between devices: 194 us -> none
    ppermute x0 -> x61, waiting for transfers between devices: none -> 166 us  [the longest x49 124 us: swap_bit(): return lax.ppermute(value, BOTH, [(i, i ^ 1 << bit) for i in range(count)])]
    all_gather x7 -> x0, waiting for transfers between devices: 102 us -> none  [the longest x1 30.6 us: local(): lax.all_gather(key_rows.reshape(seq_count, local_len, model_width), 'cont...]
    unnamed x2 -> x0, blocking collectives: 82.8 us -> none
    ppermute x0 -> x61, starting transfers between devices: none -> 66.2 us  [the longest x49 60.4 us: swap_bit(): return lax.ppermute(value, BOTH, [(i, i ^ 1 << bit) for i in range(count)])]
    all_gather x3 -> x0, blocking collectives: 58.7 us -> none  [the longest x1 43.8 us: local(): lax.all_gather(vectors.astype(low_type), ('dp', 'context'), axis=1, tiled...]
    dot_general x22 -> x12, matrix products: 172 us -> 124 us  [the longest x6 54.2 us: matmul(): return jnp.dot(left, right, preferred_element_type=WIDE)]
    reduce_scatter x2 -> x0, waiting for transfers between devices: 43.2 us -> none  [the longest x1 43.2 us: local(): lax.psum_scatter(inner_grad, ('dp', 'context'), scatter_dimension=0, tile...]
  transfers between devices with their start and end apart: 10 -> 61, of which waited for: 6 -> 28; matrix products, arithmetic and copies ran while one was open for 43% -> 14% of each run, Pallas kernels for 0% -> 0%
where the time goes in v1:
time: 651 us; the launch traced here: 640 us
  matrix products  193 us (30%)
  waiting for transfers between devices  166 us (25%)
  other arithmetic  111 us (17%)
  local copies, waits for them, and re-layouts  103 us (16%)
  starting transfers between devices  66.2 us (10%)
    ppermute x49, waiting for transfers between devices, swap_bit(): return lax.ppermute(value, BOTH, [(i, i ^ 1 << bit) for i in range(count)])  124 us
    ppermute x49, starting transfers between devices, swap_bit(): return lax.ppermute(value, BOTH, [(i, i ^ 1 << bit) for i in range(count)])  60.4 us
    dot_general x6, matrix products, matmul(): return jnp.dot(left, right, preferred_element_type=WIDE)  54.2 us
    dot_general x6, matrix products, times_transpose(): lax.dot_general(left, right, (((1,), (1,)), ((), ())), preferred_element_...  42.8 us
    ppermute x12, waiting for transfers between devices, swap_context(): lax.ppermute(value, 'context', [(i, i ^ offset) for i in range(parts)])  41.8 us
    select_n x28, other arithmetic, join(): jnp.where(flag, jnp.stack([other, mine], axis=axis), jnp.stack([mine, oth...  32.8 us
    dot_general x6, matrix products, contract_rows(): lax.dot_general(left, right, (((0,), (0,)), ((), ())), preferred_element_...  26.2 us
    convert_element_type x1, other arithmetic, attend_back(): score_low = (prob * (prob_grad - row_term)).astype(LOW)  21.6 us
  transfers between devices with their start and end apart: 61, of which 28 were waited for; matrix products, arithmetic and copies ran while one was open for 14% of the time, Pallas kernels for 0%

profile of v1, /device:TPU:0, one launch (start us, length us, event | category | flops | bytes accessed | tf_op | source)
XLA Modules:
  0.0 640.4 jit_solution(5587852920378140639)
XLA Ops:
  30.2 11.3 %collective-permute-done.18 = bf16[2,96,768]{2,1,0:T(8,128)(2,1)S(1)} collective-permute-done((bf16[2,96,768]{2,1,0:T(8,128)(2,1)S(1)}, bf16[2,96,768]{2,1,0:T(8,128)(2,1)S(1)}, u32[]{:S(2)}, u32[]{:S(2)}) %collective-permute-start.18) | collective-permute-done | bytes 294944 | tf_op jit(solution)/shard_map/ppermute | solution.py:48
  69.0 7.3 %collective-permute-done.22 = bf16[2,2,2,96,384]{4,3,1,0,2:T(8,128)(2,1)S(1)} collective-permute-done((bf16[2,2,2,96,384]{4,3,1,0,2:T(8,128)(2,1)S(1)}, bf16[2,2,2,96,384]{4,3,1,0,2:T(8,128)(2,1)S(1)}, u32[]{:S(2)}, u32[]{:S(2)}) %collective-permute-start.22) | collective-permute-done | bytes 589856 | tf_op jit(solution)/shard_map/ppermute | solution.py:48
  80.2 8.7 %collective-permute-done.15 = bf16[2,2,2,24,1536]{4,3,1,0,2:T(8,128)(2,1)S(1)} collective-permute-done((bf16[2,2,2,24,1536]{4,3,1,0,2:T(8,128)(2,1)S(1)}, bf16[2,2,2,24,1536]{4,3,1,0,2:T(8,128)(2,1)S(1)}, u32[]{:S(2)}, u32[]{:S(2)}) %collective-permute-start.15) | collective-permute-done | bytes 589856 | tf_op jit(solution)/shard_map/ppermute | solution.py:48
  91.6 6.6 %collective-permute-done.8 = bf16[2,2,2,97,384]{4,0,3,1,2:T(2,128)(2,1)S(1)} collective-permute-done((bf16[2,2,2,97,384]{4,0,3,1,2:T(2,128)(2,1)S(1)}, bf16[2,2,2,97,384]{4,0,3,1,2:T(2,128)(2,1)S(1)}, u32[]{:S(2)}, u32[]{:S(2)}) %collective-permute-start.8) | collective-permute-done | bytes 596000 | tf_op jit(solution)/shard_map/ppermute | solution.py:48
  107.8 9.3 %collective-permute-done.28 = bf16[2,128,768]{2,1,0:T(8,128)(2,1)S(1)} collective-permute-done((bf16[2,128,768]{2,1,0:T(8,128)(2,1)S(1)}, bf16[2,128,768]{2,1,0:T(8,128)(2,1)S(1)}, u32[]{:S(2)}, u32[]{:S(2)}) %collective-permute-start.28) | collective-permute-done | bytes 393248 | tf_op jit(solution)/shard_map/ppermute | solution.py:107
  120.0 11.0 %collective-permute-done.1 = bf16[2,128,768]{2,1,0:T(8,128)(2,1)} collective-permute-done((bf16[2,128,768]{2,1,0:T(8,128)(2,1)}, bf16[2,128,768]{2,1,0:T(8,128)(2,1)}, u32[]{:S(2)}, u32[]{:S(2)}) %collective-permute-start.1) | collective-permute-done | bytes 393248 | tf_op jit(solution)/shard_map/ppermute | solution.py:107
  137.6 7.7 %collective-permute-done.2 = bf16[2,128,768]{2,1,0:T(8,128)(2,1)S(1)} collective-permute-done((bf16[2,128,768]{2,1,0:T(8,128)(2,1)}, bf16[2,128,768]{2,1,0:T(8,128)(2,1)S(1)}, u32[]{:S(2)}, u32[]{:S(2)}) %collective-permute-start.2) | collective-permute-done | bytes 393248 | tf_op jit(solution)/shard_map/ppermute | solution.py:107
  151.2 5.7 maximum_select_fusion.1
  156.9 5.6 maximum_select_fusion
  166.0 8.5 %broadcast_select_fusion = bf16[2,2,2,2,2,97,768]{6,3,5,2,1,0,4:T(2,128)(2,1)} fusion(pred[]{:T(512)S(6)} %eq.10, bf16[2,2,2,2,1,97,768]{6,3,5,2,1,0,4:T(2,128)(2,1)S(1)} %bitcast.411, bf16[2,2,2,2,1,97,768]{6,3,5,2,1,0,4:T(2,128)(2,1)S(1)} %bitcast.412), kind=kLoop, calls=%fused_computation.29 | loop fusion | flops 7151616 | bytes 9535489 | tf_op jit(solution)/shard_map/jit(_where)/select_n | solution.py:57
  174.5 9.5 %copy.105 = bf16[2,2,2,2,2,97,768]{6,4,3,2,1,0,5:T(2,128)(2,1)} copy(bf16[2,2,2,2,2,97,768]{6,3,5,2,1,0,4:T(2,128)(2,1)} %broadcast_select_fusion) | data formatting | bytes 9535488 | tf_op jit(solution)/shard_map/jit(_where)/select_n | solution.py:57
  184.1 10.9 %select_n.445 = bf16[32,97,768]{2,0,1:T(8,128)(2,1)} reshape(bf16[2,2,2,2,2,97,768]{6,4,3,2,1,0,5:T(2,128)(2,1)} %copy.105) | data formatting | bytes 9535488 | tf_op jit(solution)/shard_map/jit(_where)/select_n | solution.py:57
  234.8 11.2 %select_reduce_fusion = (f32[2,12,512]{2,1,0:T(8,128)S(1)}, f32[2,12,512,512]{2,3,1,0:T(8,128)}) fusion(pred[2,512]{1,0:T(4,128)(4,1)S(1)} %iota_compare_fusion.1, bf16[2,512,12,64]{1,0,3,2:T(2,128)(2,1)S(1)} %reshape.870, bf16[2,512,12,64]{1,0,3,2:T(2,128)(2,1)S(1)} %reshape.869), kind=kOutput, calls=%fused_computation.5 | convolution fusion | flops 824168448 | bytes 28361728 | tf_op jit(solution)/shard_map/gqhc,gkhc->ghqk/dot_general | solution.py:160
  246.0 11.2 %fusion = f32[2,12,512]{2,1,0:T(8,128)S(1)} fusion(f32[2,12,512,512]{2,3,1,0:T(8,128)} %get-tuple-element.114, f32[2,12,512]{2,1,0:T(8,128)S(1)} %get-tuple-element.113, pred[2,512]{1,0:T(4,128)(4,1)S(1)} %iota_compare_fusion.1), kind=kLoop, calls=%fused_computation.6 | loop fusion | flops 25153536 | bytes 25265152 | tf_op jit(solution)/shard_map/reduce_sum | solution.py:169
  257.9 11.8 %fusion.52 = bf16[2,512,12,64]{1,3,2,0:T(8,128)(2,1)S(1)} fusion(f32[2,12,512,512]{2,3,1,0:T(8,128)} %get-tuple-element.114, f32[2,12,512]{2,1,0:T(8,128)S(1)} %fusion, f32[2,12,512]{2,1,0:T(8,128)S(1)} %get-tuple-element.113, pred[2,512]{1,0:T(4,128)(4,1)S(1)} %iota_compare_fusion.1, bf16[2,512,12,64]{1,0,3,2:T(2,128)(2,1)S(1)} %copy-done.20), kind=kOutput, calls=%fused_computation.107 | convolution fusion | flops 837550080 | bytes 28410880 | tf_op jit(solution)/shard_map/ghqk,gkhc->gqhc/dot_general | solution.py:171
  274.6 35.0 %multiply_convert_fusion.1 = (bf16[1024,3072]{1,0:T(8,128)(2,1)S(1)}, f32[1024,3072]{1,0:T(8,128)}, f32[1024,3072]{1,0:T(8,128)}) fusion(f32[3072]{0:T(1024)S(1)} %add.495, bf16[768,3072]{1,0:T(8,128)(2,1)S(1)} %bitcast.430, f32[1024,768]{1,0:T(8,128)S(1)} %get-tuple-element.53, f32[768]{0:T(1024)S(1)} %add.492, f32[768]{0:T(1024)S(1)} %mul.455, ...), kind=kOutput, calls=%fused_computation.12 | convolution fusion | flops 5043388416 | bytes 39348224 | tf_op jit(solution)/shard_map/dot_general | solution.py:36
  320.2 7.0 %convolution_convert_fusion = bf16[3072,768]{1,0:T(8,128)(2,1)} fusion(bf16[1024,3072]{1,0:T(8,128)(2,1)S(1)} %get-tuple-element.50, f32[1024,768]{1,0:T(8,128)S(1)} %get-tuple-element.39), kind=kOutput, calls=%fused_computation.30 | convolution fusion | flops 4834983936 | bytes 14155776 | tf_op jit(solution)/shard_map/dot_general | solution.py:40
  327.2 19.0 %convert_reduce_fusion = (f32[3072]{0:T(1024)S(1)}, bf16[1024,3072]{1,0:T(8,128)(2,1)}) fusion(f32[1024,3072]{1,0:T(8,128)} %get-tuple-element.51, bf16[3072,768]{1,0:T(8,128)(2,1)} %bitcast.431, f32[1024,768]{1,0:T(8,128)} %copy-done.25, f32[1024,3072]{1,0:T(8,128)} %get-tuple-element.115, f32[3072]{0:T(1024)S(1)} %add.495), kind=kOutput, calls=%fused_computation.10 | convolution fusion | flops 4886098944 | bytes 39346176 | tf_op jit(solution)/shard_map/dot_general | solution.py:44
  346.3 10.2 %multiply_reduce_fusion.1 = (f32[768]{0:T(1024)S(1)}, f32[1024]{0:T(1024)S(1)}, f32[1024]{0:T(1024)S(1)}, f32[768]{0:T(1024)S(1)}, f32[1024,768]{1,0:T(8,128)S(1)}) fusion(f32[1024,768]{1,0:T(8,128)S(1)} %get-tuple-element.53, f32[1024]{0:T(1024)S(1)} %add_rsqrt_fusion.1, f32[1024]{0:T(1024)S(1)} %broadcast_multiply_fusion.4, f32[768]{0:T(1024)S(1)} %mul.455, ...), kind=kOutput, calls=%fused_computation.53 | convolution fusion | flops 4839698432 | bytes 20472832 | tf_op jit(solution)/shard_map/dot_general | solution.py:44
  356.5 8.0 %convolution_convert_fusion.1 = bf16[768,3072]{1,0:T(8,128)(2,1)} fusion(bf16[1024,3072]{1,0:T(8,128)(2,1)S(1)} %copy-done.65, f32[1024,768]{1,0:T(8,128)S(1)} %get-tuple-element.53, f32[768]{0:T(1024)S(1)} %add.492, f32[768]{0:T(1024)S(1)} %mul.455, f32[1024]{0:T(1024)S(1)} %add_rsqrt_fusion.1, f32[1024]{0:T(1024)S(1)} %broadcast_multiply_fusion.4), kind=kOutput, calls=%fused_computation.31 | convolution fusion | flops 4838129664 | bytes 14170112 | tf_op jit(solution)/shard_map/dot_general | solution.py:40
  370.7 12.3 %convert_reduce_fusion.4 = (f32[12,64]{1,0:T(8,128)S(1)}, bf16[2,512,12,64]{1,3,2,0:T(8,128)(2,1)}) fusion(f32[2,12,512,512]{2,3,1,0:T(8,128)} %get-tuple-element.114, f32[2,12,512]{2,1,0:T(8,128)S(1)} %copy-done.42, pred[2,512]{1,0:T(4,128)(4,1)S(1)} %copy-done.55, bf16[2,512,12,64]{1,0,3,2:T(2,128)(2,1)S(1)} %reshape.873), kind=kOutput, calls=%fused_computation.56 | convolution fusion | flops 832830720 | bytes 28364800 | tf_op jit(solution)/shard_map/ghqk,gqhc->gkhc/dot_general | solution.py:199
  383.1 18.5 %multiply_reduce_fusion = (f32[2,12,512]{2,1,0:T(8,128)S(1)}, f32[2,12,512,512]{2,3,1,0:T(8,128)}) fusion(f32[2,12,512,512]{2,3,1,0:T(8,128)} %get-tuple-element.114, f32[2,12,512]{2,1,0:T(8,128)S(1)} %copy-done.42, pred[2,512]{1,0:T(4,128)(4,1)S(1)} %copy-done.55, bf16[2,512,12,64]{1,0,3,2:T(2,128)(2,1)S(1)} %copy-done.21, ...), kind=kOutput, calls=%fused_computation.1 | convolution fusion | flops 836751360 | bytes 53576704 | tf_op jit(solution)/shard_map/gqhc,gkhc->ghqk/dot_general | solution.py:190
  401.6 21.6 %multiply_convert_fusion = bf16[2,12,512,512]{2,3,1,0:T(8,128)(2,1)} fusion(f32[2,12,512,512]{2,3,1,0:T(8,128)} %get-tuple-element.120, f32[2,12,512,512]{2,3,1,0:T(8,128)} %get-tuple-element.114, f32[2,12,512]{2,1,0:T(8,128)S(1)} %get-tuple-element.119, f32[2,12,512]{2,1,0:T(8,128)S(1)} %copy-done.42, pred[2,512]{1,0:T(4,128)(4,1)S(1)} %copy-done.55), kind=kLoop, calls=%fused_computation | loop fusion | flops 37748736 | bytes 63013888 | tf_op jit(solution)/shard_map/convert_element_type | solution.py:192
  423.2 8.6 %fusion.51 = bf16[2,512,12,64]{1,3,2,0:T(8,128)(2,1)S(1)} fusion(bf16[2,12,512,512]{2,3,1,0:T(8,128)(2,1)} %multiply_convert_fusion, bf16[2,512,12,64]{1,0,3,2:T(2,128)(2,1)S(1)} %copy-done.6), kind=kOutput, calls=%fused_computation.106 | convolution fusion | flops 806879232 | bytes 15728640 | tf_op jit(solution)/shard_map/ghqk,gqhc->gkhc/dot_general | solution.py:196
  431.8 6.8 %convert_reduce_fusion.5 = (f32[12,64]{1,0:T(8,128)S(1)}, bf16[2,512,12,64]{1,3,2,0:T(8,128)(2,1)S(1)}) fusion(bf16[2,12,512,512]{2,3,1,0:T(8,128)(2,1)} %multiply_convert_fusion, bf16[2,512,12,64]{1,0,3,2:T(2,128)(2,1)S(1)} %copy-done.3), kind=kOutput, calls=%fused_computation.57 | convolution fusion | flops 808451328 | bytes 15731712 | tf_op jit(solution)/shard_map/ghqk,gkhc->gqhc/dot_general | solution.py:193
  493.2 14.0 %collective-permute-done.55 = f32[2,2,2,1,144]{4,3,2,1,0:T(1,128)S(1)} collective-permute-done((f32[2,2,2,1,144]{4,3,2,1,0:T(1,128)S(1)}, f32[2,2,2,1,144]{4,3,2,1,0:T(1,128)S(1)}, u32[]{:S(2)}, u32[]{:S(2)}) %collective-permute-start.55) | collective-permute-done | bytes 4640 | tf_op jit(solution)/shard_map/ppermute | solution.py:48
  539.7 6.5 %collective-permute-done.26 = bf16[2,128,768]{2,1,0:T(8,128)(2,1)S(1)} collective-permute-done((bf16[2,128,768]{2,1,0:T(8,128)(2,1)}, bf16[2,128,768]{2,1,0:T(8,128)(2,1)S(1)}, u32[]{:S(2)}, u32[]{:S(2)}) %collective-permute-start.26) | collective-permute-done | bytes 393248 | tf_op jit(solution)/shard_map/ppermute | solution.py:107
  560.0 6.0 collective-permute-done.48
  568.6 10.0 %collective-permute-done.41 = bf16[2,2,2,24,1536]{4,3,0,1,2:T(8,128)(2,1)S(1)} collective-permute-done((bf16[2,2,2,24,1536]{4,3,0,1,2:T(8,128)(2,1)S(1)}, bf16[2,2,2,24,1536]{4,3,0,1,2:T(8,128)(2,1)S(1)}, u32[]{:S(2)}, u32[]{:S(2)}) %collective-permute-start.41) | collective-permute-done | bytes 589856 | tf_op jit(solution)/shard_map/ppermute | solution.py:48
  581.2 10.7 %collective-permute-done.36 = bf16[2,2,2,96,384]{4,3,2,1,0:T(8,128)(2,1)S(1)} collective-permute-done((bf16[2,2,2,96,384]{4,3,2,1,0:T(8,128)(2,1)S(1)}, bf16[2,2,2,96,384]{4,3,2,1,0:T(8,128)(2,1)S(1)}, u32[]{:S(2)}, u32[]{:S(2)}) %collective-permute-start.36) | collective-permute-done | bytes 589856 | tf_op jit(solution)/shard_map/ppermute | solution.py:48
  615.2 8.5 %collective-permute-done.38 = bf16[2,96,768]{2,1,0:T(8,128)(2,1)S(1)} collective-permute-done((bf16[2,96,768]{2,1,0:T(8,128)(2,1)S(1)}, bf16[2,96,768]{2,1,0:T(8,128)(2,1)S(1)}, u32[]{:S(2)}, u32[]{:S(2)}) %collective-permute-start.38) | collective-permute-done | bytes 294944 | tf_op jit(solution)/shard_map/ppermute | solution.py:48
  627.0 10.1 %collective-permute-done.39 = bf16[96,768]{1,0:T(8,128)(2,1)S(1)} collective-permute-done((bf16[96,768]{1,0:T(8,128)(2,1)S(1)}, bf16[96,768]{1,0:T(8,128)(2,1)S(1)}, u32[]{:S(2)}, u32[]{:S(2)}) %collective-permute-start.39) | collective-permute-done | bytes 147488 | tf_op jit(solution)/shard_map/ppermute | solution.py:48
  (492 shorter events, 288.3 us)
Async XLA Ops:
  2.3 23.0 %collective-permute-start.17 = (bf16[96,768]{1,0:T(8,128)(2,1)}, bf16[96,768]{1,0:T(8,128)(2,1)S(1)}, u32[]{:S(2)}, u32[]{:S(2)}) collective-permute-start(bf16[96,768]{1,0:T(8,128)(2,1)} %convert_element_type.392), channel_id=1, source_target_pairs={{0,16},{1,17},{2,18},{3,19},{4,20},{5,21},{6,22},{7,23},{8,24},{9,... | collective-permute-start | bytes 442376 | tf_op jit(solution)/shard_map/ppermute | solution.py:48
  11.2 17.3 %collective-permute-start.3 = (bf16[97,768]{1,0:T(8,128)(2,1)}, bf16[97,768]{1,0:T(8,128)(2,1)S(1)}, u32[]{:S(2)}, u32[]{:S(2)}) collective-permute-start(bf16[97,768]{1,0:T(8,128)(2,1)} %get-tuple-element.110), channel_id=1, source_target_pairs={{0,16},{1,17},{2,18},{3,19},{4,20},{5,21},{6,22},{7,23},{8,24},{9,... | collective-permute-start | bytes 446984 | tf_op jit(solution)/shard_map/ppermute | solution.py:48
  25.3 20.0 %collective-permute-start.11 = (bf16[2,24,3072]{2,1,0:T(8,128)(2,1)S(1)}, bf16[2,24,3072]{2,1,0:T(8,128)(2,1)S(1)}, u32[]{:S(2)}, u32[]{:S(2)}) collective-permute-start(bf16[2,24,3072]{2,1,0:T(8,128)(2,1)S(1)} %maximum_select_fusion.17), channel_id=1, source_target_pairs={{0,8},{1,9},{2,10},{3,11},{4,12},{5,13},{6,14},{7,15},{8,0},{9,1},... | collective-permute-start | bytes 884744 | tf_op jit(solution)/shard_map/ppermute | solution.py:48
  28.8 17.4 %collective-permute-start.4 = (bf16[2,97,768]{2,1,0:T(8,128)(2,1)S(1)}, bf16[2,97,768]{2,1,0:T(8,128)(2,1)S(1)}, u32[]{:S(2)}, u32[]{:S(2)}) collective-permute-start(bf16[2,97,768]{2,1,0:T(8,128)(2,1)S(1)} %maximum_select_fusion.16), channel_id=1, source_target_pairs={{0,8},{1,9},{2,10},{3,11},{4,12},{5,13},{6,14},{7,15},{8,0},{9,1},... | collective-permute-start | bytes 893960 | tf_op jit(solution)/shard_map/ppermute | solution.py:48
  52.6 25.2 %collective-permute-start.20 = (bf16[2,2,2,96,384]{4,3,1,0,2:T(8,128)(2,1)S(1)}, bf16[2,2,2,96,384]{4,3,1,0,2:T(8,128)(2,1)S(1)}, u32[]{:S(2)}, u32[]{:S(2)}) collective-permute-start(bf16[2,2,2,96,384]{4,3,1,0,2:T(8,128)(2,1)S(1)} %maximum_select_fusion.12), channel_id=1, source_target_pairs={{0,2},{1,3},{2,0},{3,1},{4,6},{5,7},{6,4},{7,5},{8,10},{9,11},{10,... | collective-permute-start | bytes 1769480 | tf_op jit(solution)/shard_map/ppermute | solution.py:48
  57.3 19.0 %collective-permute-start.22 = (bf16[2,2,2,96,384]{4,3,1,0,2:T(8,128)(2,1)S(1)}, bf16[2,2,2,96,384]{4,3,1,0,2:T(8,128)(2,1)S(1)}, u32[]{:S(2)}, u32[]{:S(2)}) collective-permute-start(bf16[2,2,2,96,384]{4,3,1,0,2:T(8,128)(2,1)S(1)} %maximum_select_fusion.14), channel_id=1, source_target_pairs={{0,4},{1,5},{2,6},{3,7},{4,0},{5,1},{6,2},{7,3},{8,12},{9,13},{10,... | collective-permute-start | bytes 1769480 | tf_op jit(solution)/shard_map/ppermute | solution.py:48
  58.9 30.2 %collective-permute-start.13 = (bf16[2,2,2,24,1536]{4,3,1,0,2:T(8,128)(2,1)S(1)}, bf16[2,2,2,24,1536]{4,3,1,0,2:T(8,128)(2,1)S(1)}, u32[]{:S(2)}, u32[]{:S(2)}) collective-permute-start(bf16[2,2,2,24,1536]{4,3,1,0,2:T(8,128)(2,1)S(1)} %maximum_select_fusion.7), channel_id=1, source_target_pairs={{0,2},{1,3},{2,0},{3,1},{4,6},{5,7},{6,4},{7,5},{8,10},{9,11},{10,... | collective-permute-start | bytes 1769480 | tf_op jit(solution)/shard_map/ppermute | solution.py:48
  63.0 25.9 %collective-permute-start.15 = (bf16[2,2,2,24,1536]{4,3,1,0,2:T(8,128)(2,1)S(1)}, bf16[2,2,2,24,1536]{4,3,1,0,2:T(8,128)(2,1)S(1)}, u32[]{:S(2)}, u32[]{:S(2)}) collective-permute-start(bf16[2,2,2,24,1536]{4,3,1,0,2:T(8,128)(2,1)S(1)} %maximum_select_fusion.9), channel_id=1, source_target_pairs={{0,4},{1,5},{2,6},{3,7},{4,0},{5,1},{6,2},{7,3},{8,12},{9,13},{10,... | collective-permute-start | bytes 1769480 | tf_op jit(solution)/shard_map/ppermute | solution.py:48
  65.1 33.0 %collective-permute-start.8 = (bf16[2,2,2,97,384]{4,0,3,1,2:T(2,128)(2,1)S(1)}, bf16[2,2,2,97,384]{4,0,3,1,2:T(2,128)(2,1)S(1)}, u32[]{:S(2)}, u32[]{:S(2)}) collective-permute-start(bf16[2,2,2,97,384]{4,0,3,1,2:T(2,128)(2,1)S(1)} %broadcast_select_fusion.4), channel_id=1, source_target_pairs={{0,4},{1,5},{2,6},{3,7},{4,0},{5,1},{6,2},{7,3},{8,12},{9,13},{10,... | collective-permute-start | bytes 1787912 | tf_op jit(solution)/shard_map/ppermute | solution.py:48
  76.3 23.6 %collective-permute-start.6 = (bf16[2,2,2,97,384]{4,0,3,1,2:T(2,128)(2,1)S(1)}, bf16[2,2,2,97,384]{4,0,3,1,2:T(2,128)(2,1)S(1)}, u32[]{:S(2)}, u32[]{:S(2)}) collective-permute-start(bf16[2,2,2,97,384]{4,0,3,1,2:T(2,128)(2,1)S(1)} %broadcast_select_fusion.7), channel_id=1, source_target_pairs={{0,2},{1,3},{2,0},{3,1},{4,6},{5,7},{6,4},{7,5},{8,10},{9,11},{10,... | collective-permute-start | bytes 1787912 | tf_op jit(solution)/shard_map/ppermute | solution.py:48
  80.2 70.9 %collective-permute-start.23 = (bf16[2,2,2,2,96,768]{5,4,3,2,1,0:T(8,128)(2,1)}, bf16[2,2,2,2,96,768]{5,4,3,2,1,0:T(8,128)(2,1)}, u32[]{:S(2)}, u32[]{:S(2)}) collective-permute-start(bf16[2,2,2,2,96,768]{5,4,3,2,1,0:T(8,128)(2,1)} %get-tuple-element.69), channel_id=1, source_target_pairs={{0,1},{1,0},{2,3},{3,2},{4,5},{5,4},{6,7},{7,6},{8,9},{9,8},{10,11... | collective-permute-start | bytes 7077896 | tf_op jit(solution)/shard_map/ppermute | solution.py:48
  91.6 65.3 %collective-permute-start.16 = (bf16[2,2,2,2,24,3072]{5,4,3,2,1,0:T(8,128)(2,1)}, bf16[2,2,2,2,24,3072]{5,4,3,2,1,0:T(8,128)(2,1)}, u32[]{:S(2)}, u32[]{:S(2)}) collective-permute-start(bf16[2,2,2,2,24,3072]{5,4,3,2,1,0:T(8,128)(2,1)} %get-tuple-element.71), channel_id=1, source_target_pairs={{0,1},{1,0},{2,3},{3,2},{4,5},{5,4},{6,7},{7,6},{8,9},{9,8},{10,11... | collective-permute-start | bytes 7077896 | tf_op jit(solution)/shard_map/ppermute | solution.py:48
  105.3 57.2 %collective-permute-start.9 = (bf16[2,2,2,2,97,768]{5,0,4,1,3,2:T(2,128)(2,1)}, bf16[2,2,2,2,97,768]{5,0,4,1,3,2:T(2,128)(2,1)}, u32[]{:S(2)}, u32[]{:S(2)}) collective-permute-start(bf16[2,2,2,2,97,768]{5,0,4,1,3,2:T(2,128)(2,1)} %pad_maximum_fusion), channel_id=1, source_target_pairs={{0,1},{1,0},{2,3},{3,2},{4,5},{5,4},{6,7},{7,6},{8,9},{9,8},{10,11... | collective-permute-start | bytes 7151624 | tf_op jit(solution)/shard_map/ppermute | solution.py:48
  119.6 18.0 %collective-permute-start.29 = (bf16[2,128,768]{2,1,0:T(8,128)(2,1)S(1)}, bf16[2,128,768]{2,1,0:T(8,128)(2,1)S(1)}, u32[]{:S(2)}, u32[]{:S(2)}) collective-permute-start(bf16[2,128,768]{2,1,0:T(8,128)(2,1)S(1)} %get-tuple-element.77), channel_id=1, source_target_pairs={{0,3},{1,2},{2,1},{3,0},{4,7},{5,6},{6,5},{7,4},{8,11},{9,10},{10,... | collective-permute-start | bytes 1179656 | tf_op jit(solution)/shard_map/ppermute | solution.py:107
  476.7 69.6 %collective-permute-start.47 = (bf16[2,2,2,2,96,768]{5,4,0,1,3,2:T(8,128)(2,1)}, bf16[2,2,2,2,96,768]{5,4,0,1,3,2:T(8,128)(2,1)}, u32[]{:S(2)}, u32[]{:S(2)}) collective-permute-start(bf16[2,2,2,2,96,768]{5,4,0,1,3,2:T(8,128)(2,1)} %bitcast.397), channel_id=1, source_target_pairs={{0,1},{1,0},{2,3},{3,2},{4,5},{5,4},{6,7},{7,6},{8,9},{9,8},{10,11... | collective-permute-start | bytes 7077896 | tf_op jit(solution)/shard_map/ppermute | solution.py:48
  477.7 74.3 %collective-permute-start.40 = (bf16[2,2,2,2,24,3072]{5,4,0,1,3,2:T(8,128)(2,1)}, bf16[2,2,2,2,24,3072]{5,4,0,1,3,2:T(8,128)(2,1)}, u32[]{:S(2)}, u32[]{:S(2)}) collective-permute-start(bf16[2,2,2,2,24,3072]{5,4,0,1,3,2:T(8,128)(2,1)} %bitcast.398), channel_id=1, source_target_pairs={{0,1},{1,0},{2,3},{3,2},{4,5},{5,4},{6,7},{7,6},{8,9},{9,8},{10,11... | collective-permute-start | bytes 7077896 | tf_op jit(solution)/shard_map/ppermute | solution.py:48
  486.9 38.8 %collective-permute-start.32 = (bf16[2,128,768]{2,1,0:T(8,128)(2,1)}, bf16[2,128,768]{2,1,0:T(8,128)(2,1)}, u32[]{:S(2)}, u32[]{:S(2)}) collective-permute-start(bf16[2,128,768]{2,1,0:T(8,128)(2,1)} %get-tuple-element.73), channel_id=1, source_target_pairs={{0,3},{1,2},{2,1},{3,0},{4,7},{5,6},{6,5},{7,4},{8,11},{9,10},{10,... | collective-permute-start | bytes 1179656 | tf_op jit(solution)/shard_map/ppermute | solution.py:107
  487.2 41.8 %collective-permute-start.31 = (bf16[2,128,768]{2,1,0:T(8,128)(2,1)S(1)}, bf16[2,128,768]{2,1,0:T(8,128)(2,1)}, u32[]{:S(2)}, u32[]{:S(2)}) collective-permute-start(bf16[2,128,768]{2,1,0:T(8,128)(2,1)S(1)} %get-tuple-element.74), channel_id=1, source_target_pairs={{0,2},{1,3},{2,0},{3,1},{4,6},{5,7},{6,4},{7,5},{8,10},{9,11},{10,... | collective-permute-start | bytes 1179656 | tf_op jit(solution)/shard_map/ppermute | solution.py:107
  529.1 17.1 %collective-permute-start.26 = (bf16[2,128,768]{2,1,0:T(8,128)(2,1)}, bf16[2,128,768]{2,1,0:T(8,128)(2,1)S(1)}, u32[]{:S(2)}, u32[]{:S(2)}) collective-permute-start(bf16[2,128,768]{2,1,0:T(8,128)(2,1)} %get-tuple-element.81), channel_id=1, source_target_pairs={{0,3},{1,2},{2,1},{3,0},{4,7},{5,6},{6,5},{7,4},{8,11},{9,10},{10,... | collective-permute-start | bytes 1179656 | tf_op jit(solution)/shard_map/ppermute | solution.py:107
  534.0 23.4 %collective-permute-start.33 = (bf16[2,2,2,2,96,768]{5,4,3,2,1,0:T(8,128)(2,1)S(1)}, bf16[2,2,2,2,96,768]{5,4,3,2,1,0:T(8,128)(2,1)S(1)}, u32[]{:S(2)}, u32[]{:S(2)}) collective-permute-start(bf16[2,2,2,2,96,768]{5,4,3,2,1,0:T(8,128)(2,1)S(1)} %copy-done.26), channel_id=1, source_target_pairs={{0,1},{1,0},{2,3},{3,2},{4,5},{5,4},{6,7},{7,6},{8,9},{9,8},{10,11... | collective-permute-start | bytes 7077896 | tf_op jit(solution)/shard_map/ppermute | solution.py:48
  549.7 16.3 %collective-permute-start.48 = (bf16[2,2,2,96,384]{4,3,0,1,2:T(8,128)(2,1)S(1)}, bf16[2,2,2,96,384]{4,3,0,1,2:T(8,128)(2,1)S(1)}, u32[]{:S(2)}, u32[]{:S(2)}) collective-permute-start(bf16[2,2,2,96,384]{4,3,0,1,2:T(8,128)(2,1)S(1)} %dynamic-slice_bitcast_fusion.2), channel_id=1, source_target_pairs={{0,2},{1,3},{2,0},{3,1},{4,6},{5,7},{6,4},{7,5},{8,10},{9,11},{10,... | collective-permute-start | bytes 1769480 | tf_op jit(solution)/shard_map/ppermute | solution.py:48
  550.4 16.3 %collective-permute-start.50 = (bf16[2,2,2,96,384]{4,3,0,1,2:T(8,128)(2,1)S(1)}, bf16[2,2,2,96,384]{4,3,0,1,2:T(8,128)(2,1)S(1)}, u32[]{:S(2)}, u32[]{:S(2)}) collective-permute-start(bf16[2,2,2,96,384]{4,3,0,1,2:T(8,128)(2,1)S(1)} %dynamic-slice_bitcast_fusion.1), channel_id=1, source_target_pairs={{0,4},{1,5},{2,6},{3,7},{4,0},{5,1},{6,2},{7,3},{8,12},{9,13},{10,... | collective-permute-start | bytes 1769480 | tf_op jit(solution)/shard_map/ppermute | solution.py:48
  555.0 23.6 %collective-permute-start.41 = (bf16[2,2,2,24,1536]{4,3,0,1,2:T(8,128)(2,1)S(1)}, bf16[2,2,2,24,1536]{4,3,0,1,2:T(8,128)(2,1)S(1)}, u32[]{:S(2)}, u32[]{:S(2)}) collective-permute-start(bf16[2,2,2,24,1536]{4,3,0,1,2:T(8,128)(2,1)S(1)} %dynamic-slice_bitcast_fusion.4), channel_id=1, source_target_pairs={{0,2},{1,3},{2,0},{3,1},{4,6},{5,7},{6,4},{7,5},{8,10},{9,11},{10,... | collective-permute-start | bytes 1769480 | tf_op jit(solution)/shard_map/ppermute | solution.py:48
  556.5 22.9 %collective-permute-start.43 = (bf16[2,2,2,24,1536]{4,3,0,1,2:T(8,128)(2,1)S(1)}, bf16[2,2,2,24,1536]{4,3,0,1,2:T(8,128)(2,1)S(1)}, u32[]{:S(2)}, u32[]{:S(2)}) collective-permute-start(bf16[2,2,2,24,1536]{4,3,0,1,2:T(8,128)(2,1)S(1)} %dynamic-slice_bitcast_fusion.3), channel_id=1, source_target_pairs={{0,4},{1,5},{2,6},{3,7},{4,0},{5,1},{6,2},{7,3},{8,12},{9,13},{10,... | collective-permute-start | bytes 1769480 | tf_op jit(solution)/shard_map/ppermute | solution.py:48
  558.7 33.2 %collective-permute-start.36 = (bf16[2,2,2,96,384]{4,3,2,1,0:T(8,128)(2,1)S(1)}, bf16[2,2,2,96,384]{4,3,2,1,0:T(8,128)(2,1)S(1)}, u32[]{:S(2)}, u32[]{:S(2)}) collective-permute-start(bf16[2,2,2,96,384]{4,3,2,1,0:T(8,128)(2,1)S(1)} %dynamic-slice_bitcast_fusion.5), channel_id=1, source_target_pairs={{0,4},{1,5},{2,6},{3,7},{4,0},{5,1},{6,2},{7,3},{8,12},{9,13},{10,... | collective-permute-start | bytes 1769480 | tf_op jit(solution)/shard_map/ppermute | solution.py:48
  566.0 27.6 %collective-permute-start.34 = (bf16[2,2,2,96,384]{4,3,1,0,2:T(8,128)(2,1)S(1)}, bf16[2,2,2,96,384]{4,3,1,0,2:T(8,128)(2,1)S(1)}, u32[]{:S(2)}, u32[]{:S(2)}) collective-permute-start(bf16[2,2,2,96,384]{4,3,1,0,2:T(8,128)(2,1)S(1)} %bitcast.479), channel_id=1, source_target_pairs={{0,2},{1,3},{2,0},{3,1},{4,6},{5,7},{6,4},{7,5},{8,10},{9,11},{10,... | collective-permute-start | bytes 1769480 | tf_op jit(solution)/shard_map/ppermute | solution.py:48
  566.8 31.5 %collective-permute-start.49 = (bf16[2,2,96,384]{3,2,0,1:T(8,128)(2,1)S(1)}, bf16[2,2,96,384]{3,2,0,1:T(8,128)(2,1)S(1)}, u32[]{:S(2)}, u32[]{:S(2)}) collective-permute-start(bf16[2,2,96,384]{3,2,0,1:T(8,128)(2,1)S(1)} %dynamic-slice_bitcast_fusion.7), channel_id=1, source_target_pairs={{0,4},{1,5},{2,6},{3,7},{4,0},{5,1},{6,2},{7,3},{8,12},{9,13},{10,... | collective-permute-start | bytes 884744 | tf_op jit(solution)/shard_map/ppermute | solution.py:48
  578.6 21.3 %collective-permute-start.51 = (bf16[2,2,96,384]{3,2,0,1:T(8,128)(2,1)S(1)}, bf16[2,2,96,384]{3,2,0,1:T(8,128)(2,1)S(1)}, u32[]{:S(2)}, u32[]{:S(2)}) collective-permute-start(bf16[2,2,96,384]{3,2,0,1:T(8,128)(2,1)S(1)} %dynamic-slice_bitcast_fusion.6), channel_id=1, source_target_pairs={{0,2},{1,3},{2,0},{3,1},{4,6},{5,7},{6,4},{7,5},{8,10},{9,11},{10,... | collective-permute-start | bytes 884744 | tf_op jit(solution)/shard_map/ppermute | solution.py:48
  579.4 25.1 %collective-permute-start.42 = (bf16[2,2,24,1536]{3,2,0,1:T(8,128)(2,1)S(1)}, bf16[2,2,24,1536]{3,2,0,1:T(8,128)(2,1)S(1)}, u32[]{:S(2)}, u32[]{:S(2)}) collective-permute-start(bf16[2,2,24,1536]{3,2,0,1:T(8,128)(2,1)S(1)} %dynamic-slice_bitcast_fusion.9), channel_id=1, source_target_pairs={{0,4},{1,5},{2,6},{3,7},{4,0},{5,1},{6,2},{7,3},{8,12},{9,13},{10,... | collective-permute-start | bytes 884744 | tf_op jit(solution)/shard_map/ppermute | solution.py:48
  593.5 16.5 %collective-permute-start.37 = (bf16[2,2,96,384]{3,2,1,0:T(8,128)(2,1)S(1)}, bf16[2,2,96,384]{3,2,1,0:T(8,128)(2,1)S(1)}, u32[]{:S(2)}, u32[]{:S(2)}) collective-permute-start(bf16[2,2,96,384]{3,2,1,0:T(8,128)(2,1)S(1)} %dynamic-slice_bitcast_fusion.10), channel_id=1, source_target_pairs={{0,2},{1,3},{2,0},{3,1},{4,6},{5,7},{6,4},{7,5},{8,10},{9,11},{10,... | collective-permute-start | bytes 884744 | tf_op jit(solution)/shard_map/ppermute | solution.py:48
  604.8 21.0 %collective-permute-start.45 = (bf16[2,24,3072]{2,1,0:T(8,128)(2,1)S(1)}, bf16[2,24,3072]{2,1,0:T(8,128)(2,1)S(1)}, u32[]{:S(2)}, u32[]{:S(2)}) collective-permute-start(bf16[2,24,3072]{2,1,0:T(8,128)(2,1)S(1)} %fusion.98), channel_id=1, source_target_pairs={{0,8},{1,9},{2,10},{3,11},{4,12},{5,13},{6,14},{7,15},{8,0},{9,1},... | collective-permute-start | bytes 884744 | tf_op jit(solution)/shard_map/ppermute | solution.py:48
  612.2 24.9 %collective-permute-start.53 = (bf16[96,768]{1,0:T(8,128)(2,1)S(1)}, bf16[96,768]{1,0:T(8,128)(2,1)S(1)}, u32[]{:S(2)}, u32[]{:S(2)}) collective-permute-start(bf16[96,768]{1,0:T(8,128)(2,1)S(1)} %dynamic-slice_bitcast_fusion.12), channel_id=1, source_target_pairs={{0,16},{1,17},{2,18},{3,19},{4,20},{5,21},{6,22},{7,23},{8,24},{9,... | collective-permute-start | bytes 442376 | tf_op jit(solution)/shard_map/ppermute | solution.py:48
  (105 other events, 1218.2 us)

commit v2 on v1

v2 whole, which is shorter than its diff:
```python
import functools

import jax
import jax.numpy as jnp
import numpy as np
from jax import lax
from jax.experimental import pallas as pl
from jax.experimental.pallas import tpu as pltpu
from jax.sharding import Mesh, PartitionSpec as P

HEADS = 12
HEAD = 64
PAIR = 2 * HEAD
PAIRS = HEADS // 2
STEP = 10

NORM_EPS = 1e-12
BETA_ONE = 0.9
BETA_TWO = 0.999
ADAM_EPS = 1e-06
MATRIX_LEARN_RATE = 0.05
VECTOR_RATE = 0.5
WEIGHT_DECAY = 0.01
MASK_FILL = -1e30
SCORE_SCALE = HEAD ** (-0.5)
ROOT_HALF = 0.5**0.5
DENSITY = 0.3989422804014327

CHIPS = ("dp_hi", "dp_lo", "ctx_hi")
SIDE = "ctx_lo"
ALL = CHIPS + (SIDE,)
CONTEXT = ("ctx_hi", "ctx_lo")
LOW = jnp.bfloat16
WIDE = jnp.float32
VMEM_BYTES = 60 * 1024 * 1024


def adam_step(weight, gradient, moment_one, moment_two, step_rate, decay_rate):
    first_new = BETA_ONE * moment_one + (1.0 - BETA_ONE) * gradient
    second_new = BETA_TWO * moment_two + (1.0 - BETA_TWO) * gradient * gradient
    first_hat = first_new / (1.0 - BETA_ONE**STEP)
    second_hat = second_new / (1.0 - BETA_TWO**STEP)
    updated = weight - step_rate * (
        first_hat / (jnp.sqrt(second_hat) + ADAM_EPS) + decay_rate * weight
    )
    return (second_new, updated)


def matmul(left, right):
    return jnp.dot(left, right, preferred_element_type=WIDE)


def contract_rows(left, right):
    return lax.dot_general(left, right, (((0,), (0,)), ((), ())), preferred_element_type=WIDE)


def times_transpose(left, right):
    return lax.dot_general(left, right, (((1,), (1,)), ((), ())), preferred_element_type=WIDE)


def flip(value):
    return value.astype(WIDE).T


def norm_stats(value):
    centered = value - jnp.mean(value, axis=-1, keepdims=True)
    variance = jnp.mean(centered * centered, axis=-1, keepdims=True)
    scale = lax.rsqrt(variance + NORM_EPS)
    return centered * scale, scale


def norm_back(grad, gain, unit, scale):
    scaled = grad * gain
    return scale * (
        scaled
        - jnp.mean(scaled, axis=-1, keepdims=True)
        - unit * jnp.mean(scaled * unit, axis=-1, keepdims=True)
    )


def load_matrices(picks, side, mine, other, target, sems):
    rows, half = target.shape[2], mine.shape[2]
    copies = []
    for place, pick in enumerate(picks):
        for which, source in enumerate((mine, other)):
            start = pl.multiple_of((side if which == 0 else 1 - side) * half, half)
            copies.append(
                pltpu.make_async_copy(
                    source.at[:, pl.ds(pick * rows, rows), :],
                    target.at[place, :, :, pl.ds(start, half)],
                    sems.at[2 * place + which],
                )
            )
    return copies


def load_halves(side, mine, other, target, sems, first):
    half = mine.shape[1]
    copies = []
    for which, source in enumerate((mine, other)):
        start = pl.multiple_of((side if which == 0 else 1 - side) * half, half)
        copies.append(
            pltpu.make_async_copy(source, target.at[:, pl.ds(start, half)], sems.at[first + which])
        )
    return copies


def half_slices(side, half):
    return [
        pl.ds(pl.multiple_of(side * half, half), half),
        pl.ds(pl.multiple_of((1 - side) * half, half), half),
    ]


def matrix_of(scratch, place):
    _, blocks, rows, width = scratch.shape
    return scratch[place].reshape(blocks * rows, width)


def head_masks():
    lane = lax.broadcasted_iota(jnp.int32, (1, PAIR), 1)
    return [lane < HEAD, lane >= HEAD]


def only(value, mask):
    return jnp.where(mask, value, 0.0).astype(LOW)


def attend_kernel(
    lengths,
    sides,
    tokens,
    vec,
    mine,
    other,
    query_out,
    key_out,
    value_out,
    mixed_out,
    sum_out,
    norm_out,
    weights,
    value_flip,
    mixed_flip,
    sems,
):
    step = pl.program_id(0)
    copies = load_matrices(range(4), sides[0], mine, other, weights, sems)

    @pl.when(step == 0)
    def _():
        for copy in copies:
            copy.start()
        for copy in copies:
            copy.wait()

    length = lengths[step]
    rows = tokens[...]
    query_out[...] = (matmul(rows, matrix_of(weights, 0)) + vec[0:1, :]).astype(LOW)
    key_out[...] = matmul(rows, matrix_of(weights, 1)).astype(LOW)
    value_low = (matmul(rows, matrix_of(weights, 2)) + vec[1:2, :]).astype(LOW)
    value_out[...] = value_low
    value_flip[...] = flip(value_low).astype(LOW)
    size = tokens.shape[0]
    key_valid = lax.broadcasted_iota(jnp.int32, (size, size), 0) < length
    masks = head_masks()

    def one_pair(pair, carry):
        lanes = pl.ds(pl.multiple_of(pair * PAIR, PAIR), PAIR)
        keys = key_out[:, lanes]
        queries = query_out[:, lanes].astype(WIDE) * SCORE_SCALE
        mixed, norms = [], []
        for head in range(2):
            scores = times_transpose(keys, only(queries, masks[head]))
            scores = jnp.where(key_valid, scores, MASK_FILL)
            peak = jnp.max(scores, axis=0, keepdims=True)
            exponent = jnp.exp(scores - peak)
            total = jnp.sum(exponent, axis=0, keepdims=True)
            prob = (exponent * (1.0 / total)).astype(LOW)
            start = pl.multiple_of(pair * PAIR + head * HEAD, HEAD)
            mixed.append(matmul(value_flip[pl.ds(start, HEAD), :], prob))
            norms.append(peak + jnp.log(total))
        mixed_flip[lanes, :] = jnp.concatenate(mixed, axis=0)
        norm_out[0, pair] = jnp.concatenate(norms, axis=0)
        return carry

    lax.fori_loop(0, PAIRS, one_pair, 0)
    mixed_low = mixed_flip[...].T.astype(LOW)
    mixed_out[...] = mixed_low
    sum_out[...] = (
        rows.astype(WIDE) + matmul(mixed_low, matrix_of(weights, 3)) + vec[2:3, :]
    )


def ffn_kernel(
    sides,
    first_sum,
    cotangent,
    vec,
    bias,
    inner_mine,
    inner_other,
    outer_mine,
    outer_other,
    result_out,
    second_out,
    hidden_out,
    keep_out,
    send_out,
    vec_grad,
    bias_grad,
    inner,
    outer,
    total,
    activated,
    slope,
    sems,
):
    step = pl.program_id(0)
    side = sides[0]
    copies = load_halves(side, inner_mine, inner_other, inner, sems, 0) + load_halves(
        side, outer_mine, outer_other, outer, sems, 2
    )

    @pl.when(step == 0)
    def _():
        for copy in copies:
            copy.start()
        vec_grad[...] = jnp.zeros_like(vec_grad)
        bias_grad[...] = jnp.zeros_like(bias_grad)
        total[...] = jnp.zeros_like(total)
        for copy in copies:
            copy.wait()

    unit, _ = norm_stats(first_sum[...])
    normed = unit * vec[4:5, :] + vec[5:6, :]
    normed_low = normed.astype(LOW)
    hidden = inner.shape[1]
    chunk = inner.shape[0]
    second = normed + vec[3:4, :]
    for start in range(0, hidden, chunk):
        part = slice(start, start + chunk)
        pre = matmul(normed_low, inner[:, part]) + bias[:, part]
        cdf = 0.5 * (1.0 + lax.erf(pre * ROOT_HALF))
        active = (pre * cdf).astype(LOW)
        activated[:, part] = active
        slope[:, part] = cdf + pre * (DENSITY * jnp.exp(-0.5 * pre * pre))
        second = second + matmul(active, outer[part, :])
    unit_two, scale_two = norm_stats(second)
    result_out[...] = (unit_two * vec[6:7, :] + vec[7:8, :]).astype(LOW)
    grad = cotangent[...].astype(WIDE)
    second_grad = norm_back(grad, vec[6:7, :], unit_two, scale_two)
    second_out[...] = second_grad
    grad_low = second_grad.astype(LOW)
    vec_grad[3:4, :] += jnp.sum(grad_low.astype(WIDE), axis=0, keepdims=True)
    vec_grad[6:7, :] += jnp.sum(grad * unit_two, axis=0, keepdims=True)
    vec_grad[7:8, :] += jnp.sum(grad, axis=0, keepdims=True)
    for start in range(0, hidden, chunk):
        part = slice(start, start + chunk)
        back = times_transpose(grad_low, outer[part, :])
        hidden_low = (back * slope[:, part]).astype(LOW)
        hidden_out[:, part] = hidden_low
        bias_grad[:, part] += jnp.sum(hidden_low.astype(WIDE), axis=0, keepdims=True)
        total[part, :] += contract_rows(activated[:, part], grad_low)

    @pl.when(step == pl.num_programs(0) - 1)
    def _():
        mine, theirs = half_slices(side, keep_out.shape[1])
        keep_out[...] = total[:, mine].astype(LOW)
        send_out[...] = total[:, theirs].astype(LOW)


def inner_kernel(
    sides,
    first_sum,
    second_grad,
    hidden_low,
    mixed,
    vec,
    inner_mine,
    inner_other,
    att_mine,
    att_other,
    first_out,
    mixed_grad_out,
    keep_out,
    send_out,
    vec_grad,
    inner,
    project,
    total,
    project_total,
    sems,
):
    step = pl.program_id(0)
    side = sides[0]
    copies = load_halves(side, inner_mine, inner_other, inner, sems, 2) + load_matrices(
        (3,), side, att_mine, att_other, project, sems
    )

    @pl.when(step == 0)
    def _():
        for copy in copies:
            copy.start()
        vec_grad[...] = jnp.zeros_like(vec_grad)
        total[...] = jnp.zeros_like(total)
        project_total[...] = jnp.zeros_like(project_total)
        for copy in copies:
            copy.wait()

    unit, scale = norm_stats(first_sum[...])
    normed_low = (unit * vec[4:5, :] + vec[5:6, :]).astype(LOW)
    normed_flip = flip(normed_low).astype(LOW)
    hidden = inner.shape[1]
    chunk = inner.shape[0]
    grad = second_grad[...]
    for start in range(0, hidden, chunk):
        part = slice(start, start + chunk)
        grad = grad + times_transpose(hidden_low[:, part], inner[:, part])
        total[:, part] += matmul(normed_flip, hidden_low[:, part])
    first_grad = norm_back(grad, vec[4:5, :], unit, scale)
    first_out[...] = first_grad
    branch = first_grad.astype(LOW)
    vec_grad[2:3, :] += jnp.sum(branch.astype(WIDE), axis=0, keepdims=True)
    vec_grad[4:5, :] += jnp.sum(grad * unit, axis=0, keepdims=True)
    vec_grad[5:6, :] += jnp.sum(grad, axis=0, keepdims=True)
    mixed_grad_out[...] = times_transpose(branch, matrix_of(project, 0)).astype(LOW)
    project_total[...] += contract_rows(mixed[...], branch)

    @pl.when(step == pl.num_programs(0) - 1)
    def _():
        half = inner_mine.shape[1]
        for out, wide, narrow in zip(
            (keep_out, send_out),
            half_slices(side, half),
            half_slices(side, att_mine.shape[2]),
        ):
            out[:, :half] = total[:, wide].astype(LOW)
            out[:, half:] = project_total[:, narrow].astype(LOW)


def attend_back_kernel(
    lengths,
    sides,
    tokens,
    query,
    key,
    value,
    mixed_grad,
    normalizer,
    query_out,
    key_out,
    value_out,
    keep_out,
    send_out,
    vec_grad,
    key_flip,
    query_flip,
    total,
):
    step = pl.program_id(0)
    side = sides[0]

    @pl.when(step == 0)
    def _():
        vec_grad[...] = jnp.zeros_like(vec_grad)
        total[...] = jnp.zeros_like(total)

    length = lengths[step]
    size = tokens.shape[0]
    key_flip[...] = flip(key[...]).astype(LOW)
    key_valid = lax.broadcasted_iota(jnp.int32, (size, size), 0) < length
    masks = head_masks()

    def one_pair(pair, carry):
        lanes = pl.ds(pl.multiple_of(pair * PAIR, PAIR), PAIR)
        keys = key[:, lanes]
        values = value[:, lanes]
        queries = query[:, lanes].astype(WIDE) * SCORE_SCALE
        grads = mixed_grad[:, lanes].astype(WIDE)
        norms = normalizer[0, pair]
        query_parts, key_part, value_part = [], 0.0, 0.0
        for head in range(2):
            own_query = only(queries, masks[head])
            own_grad = only(grads, masks[head])
            scores = times_transpose(keys, own_query)
            prob = jnp.where(key_valid, jnp.exp(scores - norms[head : head + 1, :]), 0.0)
            prob_grad = times_transpose(values, own_grad)
            row_term = jnp.sum(prob_grad * prob, axis=0, keepdims=True)
            score_low = (prob * (prob_grad - row_term)).astype(LOW)
            value_part = value_part + matmul(prob.astype(LOW), own_grad)
            key_part = key_part + matmul(score_low, own_query)
            start = pl.multiple_of(pair * PAIR + head * HEAD, HEAD)
            query_parts.append(matmul(key_flip[pl.ds(start, HEAD), :], score_low))
        query_flip[lanes, :] = jnp.concatenate(query_parts, axis=0) * SCORE_SCALE
        key_out[:, lanes] = key_part.astype(LOW)
        value_out[:, lanes] = value_part.astype(LOW)
        return carry

    lax.fori_loop(0, PAIRS, one_pair, 0)
    query_out[...] = query_flip[...].T.astype(LOW)
    token_flip = flip(tokens[...]).astype(LOW)
    for place, grads in enumerate((query_out, key_out, value_out)):
        total[place] += matmul(token_flip, grads[...])
    vec_grad[0:1, :] += jnp.sum(query_out[...].astype(WIDE), axis=0, keepdims=True)
    vec_grad[1:2, :] += jnp.sum(value_out[...].astype(WIDE), axis=0, keepdims=True)

    @pl.when(step == pl.num_programs(0) - 1)
    def _():
        blocks, _, rows, half = keep_out.shape
        for out, part in zip((keep_out, send_out), half_slices(side, half)):
            for place in range(3):
                out[:, place] = total[place, :, part].astype(LOW).reshape(blocks, rows, half)


def input_kernel(
    sides, first_grad, query, key, value, mine, other, grad_out, weights, sems
):
    copies = load_matrices(range(3), sides[0], mine, other, weights, sems)

    @pl.when(pl.program_id(0) == 0)
    def _():
        for copy in copies:
            copy.start()
        for copy in copies:
            copy.wait()

    grad = first_grad[...]
    for place, grads in enumerate((query, key, value)):
        grad = grad + times_transpose(grads[...], matrix_of(weights, place))
    grad_out[...] = grad.astype(grad_out.dtype)


def call(kernel, grid, inputs, outputs, scratch, flops, moved):
    return pl.pallas_call(
        kernel,
        grid=(grid,),
        in_specs=[spec for _, spec in inputs],
        out_specs=[spec for _, _, spec in outputs],
        out_shape=[jax.ShapeDtypeStruct(shape, kind) for shape, kind, _ in outputs],
        scratch_shapes=scratch,
        compiler_params=pltpu.CompilerParams(
            dimension_semantics=("arbitrary",), vmem_limit_bytes=VMEM_BYTES
        ),
        cost_estimate=pl.CostEstimate(flops=flops, bytes_accessed=moved, transcendentals=0),
    )(*[array for array, _ in inputs])


SCALARS = pl.BlockSpec(memory_space=pltpu.SMEM)
WHERE_IT_IS = pl.BlockSpec(memory_space=pl.ANY)


def tiles(rows, width):
    return pl.BlockSpec((rows, width), lambda i: (i, 0))


def whole(*shape):
    return pl.BlockSpec(shape, lambda i: (0,) * len(shape))


def swap_side(value):
    return lax.ppermute(value, SIDE, [(0, 1), (1, 0)])


def split_columns(value, side):
    half = value.shape[-1] // 2
    mine = lax.dynamic_slice_in_dim(value, side * half, half, value.ndim - 1)
    theirs = lax.dynamic_slice_in_dim(value, (1 - side) * half, half, value.ndim - 1)
    return mine, theirs


def in_order(mine, theirs, side, axis):
    return jnp.where(
        side == 0,
        jnp.concatenate([mine, theirs], axis=axis),
        jnp.concatenate([theirs, mine], axis=axis),
    )


def gather_half(shard, side):
    mine, theirs = split_columns(shard, side)
    pair = in_order(mine, swap_side(theirs), side, shard.ndim - 2)
    return pair


def own_rows(total, side):
    rows = total.shape[-2] // 2
    axis = total.ndim - 2
    mine = lax.dynamic_slice_in_dim(total, side * rows, rows, axis)
    theirs = lax.dynamic_slice_in_dim(total, (1 - side) * rows, rows, axis)
    return mine, swap_side(theirs)


def bit_of(bit):
    return (lax.axis_index(ALL) >> bit) & 1


def halve(partial, bit, axis, count):
    mine = bit_of(bit)
    sent = lax.dynamic_index_in_dim(partial, 1 - mine, axis, keepdims=False)
    kept = lax.dynamic_index_in_dim(partial, mine, axis, keepdims=False)
    return kept + lax.ppermute(sent, ALL, [(i, i ^ (1 << bit)) for i in range(count)])


def reduce_small(partial, count):
    bits = count.bit_length() - 1
    partial = partial.reshape((2,) * bits + partial.shape[1:])
    for bit in range(bits):
        partial = halve(partial, bit, bits - 1 - bit, count)
    return partial


def swap_context(value, offset, parts):
    return lax.ppermute(value, CONTEXT, [(i, i ^ offset) for i in range(parts)])


def to_sequences(value, parts):
    seqs, here, width = value.shape
    own = seqs // parts
    me = lax.axis_index(CONTEXT)
    full = jnp.zeros((own, parts * here, width), value.dtype)
    for offset in range(parts):
        peer = me ^ offset
        block = lax.dynamic_slice_in_dim(value, peer * own, own, 0)
        if offset:
            block = swap_context(block, offset, parts)
        full = lax.dynamic_update_slice_in_dim(full, block, peer * here, 1)
    return full


def to_positions(value, parts):
    own, length, width = value.shape
    here = length // parts
    me = lax.axis_index(CONTEXT)
    full = jnp.zeros((own * parts, here, width), value.dtype)
    for offset in range(parts):
        peer = me ^ offset
        block = lax.dynamic_slice_in_dim(value, peer * here, here, 1)
        if offset:
            block = swap_context(block, offset, parts)
        full = lax.dynamic_update_slice_in_dim(full, block, peer * own, 0)
    return full


def local(
    tokens,
    cotangent,
    lengths,
    attention_weights,
    inner_weights,
    outer_weights,
    inner_bias,
    vectors,
    attention_first,
    attention_second,
    inner_first,
    inner_second,
    outer_moment_first,
    outer_second,
    bias_first,
    bias_second,
    vector_first,
    vector_second,
):
    parts = lax.axis_size(CONTEXT)
    chips = lax.axis_size(CHIPS)
    count = 2 * chips
    side = lax.axis_index(SIDE)
    sides = jnp.reshape(side, (1,)).astype(jnp.int32)
    seq_count, local_len, width = tokens.shape
    hidden = inner_weights.shape[1]
    full_len = local_len * parts
    own_seqs = seq_count // parts
    rows = own_seqs * full_len
    att_rows, vec_cols, bias_cols = (
        attention_weights.shape[1],
        vectors.shape[1],
        inner_bias.shape[0],
    )
    half = width // 2
    hidden_half = hidden // 2
    pair_rows = 2 * att_rows
    tall = 16

    small = jnp.concatenate([vectors.reshape(-1), inner_bias]).astype(LOW)
    small_size = small.shape[0]
    small = jnp.pad(small.reshape(1, -1), ((0, tall - 1), (0, half - small_size)))
    att_pair = gather_half(attention_weights.astype(LOW), side).reshape(4 * pair_rows, half)
    att_mine = lax.all_gather(
        jnp.concatenate([att_pair, small], axis=0), CHIPS, axis=0, tiled=False
    )
    att_other = swap_side(att_mine)
    inner_mine = lax.all_gather(
        gather_half(inner_weights.astype(LOW), side), CHIPS, axis=0, tiled=True
    )
    inner_other = swap_side(inner_mine)
    outer_mine = lax.all_gather(
        gather_half(outer_weights.astype(LOW), side), CHIPS, axis=0, tiled=True
    )
    outer_other = swap_side(outer_mine)

    small_all = in_order(
        att_mine[:, None, 4 * pair_rows, :small_size],
        att_other[:, None, 4 * pair_rows, :small_size],
        side,
        1,
    ).reshape(count, small_size)
    small_all = small_all.astype(WIDE)
    vec = (
        small_all[:, : 8 * vec_cols].reshape(count, 8, vec_cols).transpose(1, 0, 2).reshape(8, -1)
    )
    bias = small_all[:, 8 * vec_cols :].reshape(1, -1)
    if pair_rows % tall:
        blocks, block_rows = 1, width

        def lay_out(value):
            value = value[:, : 4 * pair_rows].reshape(chips, 4, pair_rows, half)
            return value.transpose(1, 0, 2, 3).reshape(1, 4 * width, half)

        att_mine, att_other = lay_out(att_mine), lay_out(att_other)
    else:
        blocks, block_rows = chips, pair_rows

    token_rows = to_sequences(tokens, parts).reshape(rows, width)
    cot_rows = to_sequences(cotangent.astype(LOW), parts).reshape(rows, width)
    own_lengths = lax.dynamic_slice_in_dim(lengths, lax.axis_index(CONTEXT) * own_seqs, own_seqs)

    seq_tile = tiles(full_len, width)
    norm_spec = pl.BlockSpec((1, PAIRS, 2, full_len), lambda i: (i, 0, 0, 0))
    norm_shape = (own_seqs, PAIRS, 2, full_len)
    low_rows = ((rows, width), LOW, seq_tile)
    vec_spec = whole(8, width)
    square = 2 * rows * width * width
    attend_flops = 8 * rows * full_len * width

    query, key, value, mixed, first_sum, normalizer = call(
        attend_kernel,
        own_seqs,
        [
            (own_lengths, SCALARS),
            (sides, SCALARS),
            (token_rows, seq_tile),
            (vec, vec_spec),
            (att_mine, WHERE_IT_IS),
            (att_other, WHERE_IT_IS),
        ],
        [low_rows] * 4
        + [((rows, width), WIDE, seq_tile), (norm_shape, WIDE, norm_spec)],
        [
            pltpu.VMEM((4, blocks, block_rows, width), LOW),
            pltpu.VMEM((width, full_len), LOW),
            pltpu.VMEM((width, full_len), WIDE),
            pltpu.SemaphoreType.DMA((8,)),
        ],
        4 * square + 2 * attend_flops,
        20 * rows * width,
    )

    tile = 256
    row_tile = tiles(tile, width)
    hidden_tile = tiles(tile, hidden)
    result, second_grad, hidden_low, outer_keep, outer_send, vec_ffn, bias_grad = call(
        ffn_kernel,
        rows // tile,
        [
            (sides, SCALARS),
            (first_sum, row_tile),
            (cot_rows, row_tile),
            (vec, vec_spec),
            (bias, whole(1, hidden)),
            (inner_mine, WHERE_IT_IS),
            (inner_other, WHERE_IT_IS),
            (outer_mine, WHERE_IT_IS),
            (outer_other, WHERE_IT_IS),
        ],
        [
            ((rows, width), LOW, row_tile),
            ((rows, width), WIDE, row_tile),
            ((rows, hidden), LOW, hidden_tile),
            ((hidden, half), LOW, whole(hidden, half)),
            ((hidden, half), LOW, whole(hidden, half)),
            ((8, width), WIDE, vec_spec),
            ((1, hidden), WIDE, whole(1, hidden)),
        ],
        [
            pltpu.VMEM((width, hidden), LOW),
            pltpu.VMEM((hidden, width), LOW),
            pltpu.VMEM((hidden, width), WIDE),
            pltpu.VMEM((tile, hidden), LOW),
            pltpu.VMEM((tile, hidden), WIDE),
            pltpu.SemaphoreType.DMA((4,)),
        ],
        16 * square + 60 * rows * hidden,
        30 * rows * width,
    )
    outer_sum = lax.psum_scatter(
        outer_keep + swap_side(outer_send), CHIPS, scatter_dimension=0, tiled=True
    )
    output_tokens = to_positions(result.reshape(own_seqs, full_len, width), parts)

    first_grad, mixed_grad, inner_keep, inner_send, vec_mid = call(
        inner_kernel,
        rows // tile,
        [
            (sides, SCALARS),
            (first_sum, row_tile),
            (second_grad, row_tile),
            (hidden_low, hidden_tile),
            (mixed, row_tile),
            (vec, vec_spec),
            (inner_mine, WHERE_IT_IS),
            (inner_other, WHERE_IT_IS),
            (att_mine, WHERE_IT_IS),
            (att_other, WHERE_IT_IS),
        ],
        [
            ((rows, width), WIDE, row_tile),
            ((rows, width), LOW, row_tile),
            ((width, hidden_half + half), LOW, whole(width, hidden_half + half)),
            ((width, hidden_half + half), LOW, whole(width, hidden_half + half)),
            ((8, width), WIDE, vec_spec),
        ],
        [
            pltpu.VMEM((width, hidden), LOW),
            pltpu.VMEM((1, blocks, block_rows, width), LOW),
            pltpu.VMEM((width, hidden), WIDE),
            pltpu.VMEM((width, width), WIDE),
            pltpu.SemaphoreType.DMA((4,)),
        ],
        10 * square,
        26 * rows * width,
    )
    inner_sum = lax.psum_scatter(
        inner_keep + swap_side(inner_send), CHIPS, scatter_dimension=0, tiled=True
    )

    att_shape = (blocks, 3, block_rows, half)
    query_low, key_low, value_low, att_keep, att_send, vec_att = call(
        attend_back_kernel,
        own_seqs,
        [
            (own_lengths, SCALARS),
            (sides, SCALARS),
            (token_rows, seq_tile),
            (query, seq_tile),
            (key, seq_tile),
            (value, seq_tile),
            (mixed_grad, seq_tile),
            (normalizer, norm_spec),
        ],
        [low_rows] * 3
        + [
            (att_shape, LOW, whole(*att_shape)),
            (att_shape, LOW, whole(*att_shape)),
            ((8, width), WIDE, vec_spec),
        ],
        [
            pltpu.VMEM((width, full_len), LOW),
            pltpu.VMEM((width, full_len), WIDE),
            pltpu.VMEM((3, width, width), WIDE),
        ],
        3 * square + 5 * attend_flops,
        20 * rows * width,
    )
    att_partial = att_keep + swap_side(att_send)
    if blocks != chips:
        att_partial = att_partial.reshape(3, chips, pair_rows, half).transpose(1, 0, 2, 3)
    att_sum = lax.psum_scatter(att_partial, CHIPS, scatter_dimension=0, tiled=True)
    att_sum = att_sum.reshape(3, pair_rows, half)

    vector_grad = vec_ffn + vec_mid + vec_att
    small_grad = jnp.concatenate(
        [
            vector_grad.reshape(8, count, vec_cols).transpose(1, 0, 2).reshape(count, -1),
            bias_grad.reshape(count, bias_cols),
        ],
        axis=1,
    )
    small_total = reduce_small(small_grad, count)
    vector_total = small_total[: 8 * vec_cols].reshape(8, vec_cols)
    bias_total = small_total[8 * vec_cols :]

    (input_grad,) = call(
        input_kernel,
        own_seqs,
        [
            (sides, SCALARS),
            (first_grad, seq_tile),
            (query_low, seq_tile),
            (key_low, seq_tile),
            (value_low, seq_tile),
            (att_mine, WHERE_IT_IS),
            (att_other, WHERE_IT_IS),
        ],
        [((rows, width), LOW, seq_tile)],
        [
            pltpu.VMEM((3, blocks, block_rows, width), LOW),
            pltpu.SemaphoreType.DMA((6,)),
        ],
        3 * square,
        12 * rows * width,
    )
    input_grad = to_positions(input_grad.reshape(own_seqs, full_len, width), parts).astype(WIDE)

    outer_total = in_order(*own_rows(outer_sum, side), side, 1).astype(WIDE)
    inner_here, inner_there = own_rows(inner_sum, side)
    inner_total = in_order(
        inner_here[:, :hidden_half], inner_there[:, :hidden_half], side, 1
    ).astype(WIDE)
    project_total = in_order(
        inner_here[:, hidden_half:], inner_there[:, hidden_half:], side, 1
    )
    attention_total = jnp.concatenate(
        [in_order(*own_rows(att_sum, side), side, 2), project_total[None]], axis=0
    ).astype(WIDE)

    attention_square, attention_new = adam_step(
        attention_weights,
        attention_total,
        attention_first,
        attention_second,
        MATRIX_LEARN_RATE,
        WEIGHT_DECAY,
    )
    inner_square, inner_new = adam_step(
        inner_weights, inner_total, inner_first, inner_second, MATRIX_LEARN_RATE, WEIGHT_DECAY
    )
    outer_square, outer_new = adam_step(
        outer_weights,
        outer_total,
        outer_moment_first,
        outer_second,
        MATRIX_LEARN_RATE,
        WEIGHT_DECAY,
    )
    bias_square, bias_new = adam_step(
        inner_bias, bias_total, bias_first, bias_second, VECTOR_RATE, 0.0
    )
    vector_square, vector_new = adam_step(
        vectors, vector_total, vector_first, vector_second, VECTOR_RATE, 0.0
    )
    return (
        output_tokens,
        input_grad,
        attention_total,
        attention_square,
        attention_new,
        inner_total,
        inner_square,
        inner_new,
        outer_total,
        outer_square,
        outer_new,
        bias_total,
        bias_square,
        bias_new,
        vector_total,
        vector_square,
        vector_new,
    )


def solution(mesh):
    split = Mesh(
        np.asarray(mesh.devices).reshape(
            mesh.shape["dp"] // 2, 2, mesh.shape["context"] // 2, 2
        ),
        ALL,
    )
    dp = ("dp_hi", "dp_lo")
    rows3 = P(dp, CONTEXT, None)
    mid3 = P(None, ALL, None)
    row2 = P(ALL, None)
    col2 = P(None, ALL)
    one = P(ALL)
    return jax.shard_map(
        local,
        mesh=split,
        in_specs=(rows3, rows3, P(dp), mid3, row2, row2, one, col2)
        + (mid3, mid3, row2, row2, row2, row2, one, one, col2, col2),
        out_specs=(rows3, rows3)
        + (mid3,) * 3
        + (row2,) * 6
        + (one,) * 3
        + (col2,) * 3,
        check_vma=False,
    )
```

time: 651 us -> 773 us (1.19); the launches traced: 640 us -> 772 us
  waiting for transfers between devices: 166 us -> 561 us
  matrix products: 193 us -> 0 us
  Pallas kernels: 0 us -> 128 us
  other arithmetic: 111 us -> 24.2 us
  local copies, waits for them, and re-layouts: 103 us -> 25.9 us
  starting transfers between devices: 66.2 us -> 17.6 us
  between operations: 2.82 us -> 14.8 us
    reduce_scatter x0 -> x3, waiting for transfers between devices: none -> 310 us  [the longest x1 132 us: local(): lax.psum_scatter(inner_keep + swap_side(inner_send), CHIPS, scatter_dimen...]
    dot_general x24 -> x0, matrix products: 193 us -> none  [the longest x6 54.2 us: matmul(): return jnp.dot(left, right, preferred_element_type=WIDE)]
    all_gather x0 -> x3, waiting for transfers between devices: none -> 186 us  [the longest x1 64.5 us: local(): lax.all_gather(gather_half(inner_weights.astype(LOW), side), CHIPS, axis=...]
    pallas_call x0 -> x5, Pallas kernels: none -> 128 us  [call(): pl.pallas_call(kernel, grid=(grid,), in_specs=[spec for _, spec in inputs...]
    ppermute x61 -> x29, waiting for transfers between devices: 166 us -> 65.1 us  [the longest x12 44.7 us: swap_context(): return lax.ppermute(value, CONTEXT, [(i, i ^ offset) for i in range(parts)])]
    ppermute x61 -> x29, starting transfers between devices: 66.2 us -> 17.1 us  [the longest x12 7.52 us: swap_context(): return lax.ppermute(value, CONTEXT, [(i, i ^ offset) for i in range(parts)])]
    select_n x28 -> x5, other arithmetic: 32.8 us -> 2.34 us  [in_order(): jnp.where(side == 0, jnp.concatenate([mine, theirs], axis=axis), jnp.conc...]
    convert_element_type x23 -> x4, other arithmetic: 35.2 us -> 5.15 us  [the longest x1 2.05 us: local(): cot_rows = to_sequences(cotangent.astype(LOW), parts).reshape(rows, width)]
  transfers between devices with their start and end apart: 61 -> 35, of which waited for: 28 -> 23; matrix products, arithmetic and copies ran while one was open for 14% -> 5% of each run, Pallas kernels for 0% -> 5%
where the time goes in v2:
time: 773 us; the launch traced here: 772 us
  waiting for transfers between devices  561 us (73%)
  Pallas kernels  128 us (17%)
  local copies, waits for them, and re-layouts  25.9 us (3%)
  other arithmetic  24.2 us (3%)
  starting transfers between devices  17.6 us (2%)
  between operations  14.8 us (2%)
    reduce_scatter x1, waiting for transfers between devices, local(): lax.psum_scatter(inner_keep + swap_side(inner_send), CHIPS, scatter_dimen...  132 us
    reduce_scatter x1, waiting for transfers between devices, local(): lax.psum_scatter(outer_keep + swap_side(outer_send), CHIPS, scatter_dimen...  131 us
    pallas_call x5, Pallas kernels, call(): pl.pallas_call(kernel, grid=(grid,), in_specs=[spec for _, spec in inputs...  128 us
    all_gather x1, waiting for transfers between devices, local(): lax.all_gather(gather_half(inner_weights.astype(LOW), side), CHIPS, axis=...  64.5 us
    all_gather x1, waiting for transfers between devices, local(): lax.all_gather(jnp.concatenate([att_pair, small], axis=0), CHIPS, axis=0,...  62.1 us
    all_gather x1, waiting for transfers between devices, local(): lax.all_gather(gather_half(outer_weights.astype(LOW), side), CHIPS, axis=...  59.4 us
    reduce_scatter x1, waiting for transfers between devices, local(): lax.psum_scatter(att_partial, CHIPS, scatter_dimension=0, tiled=True)  47.4 us
    ppermute x12, waiting for transfers between devices, swap_context(): return lax.ppermute(value, CONTEXT, [(i, i ^ offset) for i in range(parts)])  44.7 us
  transfers between devices with their start and end apart: 35, of which 23 were waited for; matrix products, arithmetic and copies ran while one was open for 5% of the time, Pallas kernels for 5%

profile of v2, /device:TPU:0, one launch (start us, length us, event | category | flops | bytes accessed | tf_op | source)
XLA Modules:
  0.0 772.5 jit_solution(2057791328429581869)
XLA Ops:
  15.5 62.1 %all-gather.9.cloned.1.call-done = bf16[3328,384]{1,0:T(8,128)(2,1)} async-done(((bf16[208,384]{1,0:T(8,128)(2,1)}), bf16[3328,384]{1,0:T(8,128)(2,1)}) %all-gather.9.cloned.1.call-update) | async-done | bytes 2555920 | tf_op jit(solution)/shard_map/all_gather | solution.py:589
  77.6 2.1 convert_element_type.43
  82.8 59.4 %all-gather.7.cloned.1.call-done.outer_mine = bf16[3072,384]{1,0:T(8,128)(2,1)} async-done(((bf16[192,384]{1,0:T(8,128)(2,1)}), bf16[3072,384]{1,0:T(8,128)(2,1)}) %all-gather.7.cloned.1.call-update) | async-done | bytes 2359312 | tf_op jit(solution)/shard_map/all_gather | solution.py:597
  142.2 64.5 %all-gather.5.cloned.1.call-done.inner_mine = bf16[768,1536]{1,0:T(8,128)(2,1)} async-done(((bf16[48,1536]{1,0:T(8,128)(2,1)}), bf16[768,1536]{1,0:T(8,128)(2,1)}) %all-gather.5.cloned.1.call-update) | async-done | bytes 2359312 | tf_op jit(solution)/shard_map/all_gather | solution.py:593
  214.2 7.5 collective-permute-done.1
  224.3 4.9 collective-permute-done.7
  229.2 7.6 collective-permute-done.2
  241.2 26.6 %shard_map.305 = (bf16[1024,768]{1,0:T(8,128)(2,1)}, bf16[1024,768]{1,0:T(8,128)(2,1)}, bf16[1024,768]{1,0:T(8,128)(2,1)}, bf16[1024,768]{1,0:T(8,128)(2,1)}, f3...) custom-call(s32[2]{0:T(128)} %dynamic_slice.126.lengths, s32[1]{0:T(128)} %bitcast.sides, bf16[1024,768]{1,0:T(8,128)(2,1)} %bitcast.47, ...), custom_call_target="tpu_custom_call" | custom-call | flops 11274289152 | bytes 15728640 | tf_op jit(solution)/shard_map/pallas_call | solution.py:435
  267.8 33.5 %shard_map.306 = (bf16[1024,768]{1,0:T(8,128)(2,1)}, f32[1024,768]{1,0:T(8,128)}, bf16[1024,3072]{1,0:T(8,128)(2,1)}, bf16[3072,384]{1,0:T(8,128)(2,1)}, bf16[30...) custom-call(s32[1]{0:T(128)} %bitcast.sides, f32[1024,768]{1,0:T(8,128)} %get-tuple-element.41.first_sum, ...), custom_call_target="tpu_custom_call" | custom-call | flops 19516096512 | bytes 23592960 | tf_op jit(solution)/shard_map/pallas_call | solution.py:435
  301.3 23.7 %shard_map.307 = (f32[1024,768]{1,0:T(8,128)}, bf16[1024,768]{1,0:T(8,128)(2,1)}, bf16[768,1920]{1,0:T(8,128)(2,1)}, bf16[768,1920]{1,0:T(8,128)(2,1)}, f32[8,768]{1,0:T(8,128)}) custom-call(s32[1]{0:T(128)} %bitcast.sides, f32[1024,768]{1,0:T(8,128)} %get-tuple-element.41.first_sum, f32[1024,768]{1,0:T(8,128)} %get-tuple-element.43.second_grad, ...), custom_call_target="tpu_custom_call" | custom-call | flops 12079595520 | bytes 20447232 | tf_op jit(solution)/shard_map/pallas_call | solution.py:435
  325.0 35.1 %shard_map.308 = (bf16[1024,768]{1,0:T(8,128)(2,1)}, bf16[1024,768]{1,0:T(8,128)(2,1)}, bf16[1024,768]{1,0:T(8,128)(2,1)}, bf16[16,3,48,384]{3,2,1,0:T(8,128)(2,...) custom-call(s32[2]{0:T(128)} %dynamic_slice.126.lengths, s32[1]{0:T(128)} %bitcast.sides, ...), custom_call_target="tpu_custom_call" | custom-call | flops 19730006016 | bytes 15728640 | tf_op jit(solution)/shard_map/pallas_call | solution.py:435
  360.9 3.5 collective-permute-done.18
  364.4 3.4 add.269
  368.3 4.2 collective-permute-done.22
  372.4 3.9 add.283
  377.1 5.2 collective-permute-done.20
  382.3 2.3 add.272
  388.5 1.5 collective-permute-start.25
  390.0 2.2 collective-permute-done.25
  392.3 1.5 collective-permute-start.26
  393.9 9.6 %shard_map.309 = bf16[1024,768]{1,0:T(8,128)(2,1)} custom-call(s32[1]{0:T(128)} %bitcast.sides, f32[1024,768]{1,0:T(8,128)} %get-tuple-element.46.first_grad, bf16[1024,768]{1,0:T(8,128)(2,1)} %get-tuple-element.52.query, bf16[1024,768]{1,0:T(8,128)(2,1)} %get-tuple-element.53.key, bf16[1024,768]{1,0:T(8,128)(2,1)} %get-tuple-element.54.value, ...), custom_call_target="tpu_custom_call" | custom-call | flops 3623878656 | bytes 9437184 | tf_op jit(solution)/shard_map/pallas_call | solution.py:435
  403.6 2.0 collective-permute-start.27
  408.6 1.5 collective-permute-start.28
  411.4 1.8 collective-permute-done.28
  416.1 3.4 collective-permute-done.16
  420.6 7.6 collective-permute-done.17
  429.2 1.9 convert_element_type.46
  432.3 5.7 collective-permute-done.13
  439.0 7.5 collective-permute-done.14
  446.6 47.4 %reduce-scatter.4.cloned.1.call-done = bf16[1,3,48,384]{3,2,1,0:T(8,128)(2,1)} async-done(((bf16[16,3,48,384]{3,2,1,0:T(8,128)(2,1)}), bf16[1,3,48,384]{3,2,1,0:T(8,128)(2,1)}) %reduce-scatter.4.cloned.1.call-update) | async-done | bytes 110608 | tf_op jit(solution)/shard_map/reduce_scatter | solution.py:768
  494.9 131.3 %reduce-scatter.8.cloned.1.call-done = bf16[192,384]{1,0:T(8,128)(2,1)} async-done(((bf16[3072,384]{1,0:T(8,128)(2,1)}), bf16[192,384]{1,0:T(8,128)(2,1)}) %reduce-scatter.8.cloned.1.call-update) | async-done | bytes 147472 | tf_op jit(solution)/shard_map/reduce_scatter | solution.py:696
  629.5 131.6 %reduce-scatter.6.cloned.1.call-done = bf16[48,1920]{1,0:T(8,128)(2,1)} async-done(((bf16[768,1920]{1,0:T(8,128)(2,1)}), bf16[48,1920]{1,0:T(8,128)(2,1)}) %reduce-scatter.6.cloned.1.call-update) | async-done | bytes 184336 | tf_op jit(solution)/shard_map/reduce_scatter | solution.py:733
  (196 shorter events, 51.8 us)
Async XLA Ops:
  7.2 70.3 %all-gather.9.cloned.1.call-start = ((), (), s32[]{:S(2)}) async-start(), calls=%async_computation.8 | async-start | bytes 2715648 | tf_op jit(solution)/shard_map/all_gather | solution.py:589
  8.3 2.0 collective-permute-start.3
  11.1 131.1 %all-gather.7.cloned.1.call-start = ((), (), s32[]{:S(2)}) async-start(), calls=%async_computation.4 | async-start | bytes 2506752 | tf_op jit(solution)/shard_map/all_gather | solution.py:597
  11.2 1.3 collective-permute-start.10
  13.3 193.4 %all-gather.5.cloned.1.call-start = ((), (), s32[]{:S(2)}) async-start(), calls=%async_computation.3 | async-start | bytes 2506752 | tf_op jit(solution)/shard_map/all_gather | solution.py:593
  15.4 478.5 %reduce-scatter.4.cloned.1.call-start = ((), (), s32[]{:S(2)}) async-start(), calls=%async_computation.5 | async-start | bytes 1880064 | tf_op jit(solution)/shard_map/reduce_scatter | solution.py:768
  77.6 160.9 %collective-permute-start.4 = (bf16[16,208,384]{2,1,0:T(8,128)(2,1)}, bf16[16,208,384]{2,1,0:T(8,128)(2,1)}, u32[]{:S(2)}, u32[]{:S(2)}) collective-permute-start(bf16[16,208,384]{2,1,0:T(8,128)(2,1)} %bitcast.40), channel_id=1, source_target_pairs={{0,1},{1,0},{2,3},{3,2},{4,5},{5,4},{6,7},{7,6},{8,9},{9,8},{10,11... | collective-permute-start | bytes 7667720 | tf_op jit(solution)/shard_map/ppermute | solution.py:462
  80.8 128.2 %collective-permute-start.5 = (bf16[2,128,768]{2,1,0:T(8,128)(2,1)}, bf16[2,128,768]{2,1,0:T(8,128)(2,1)}, u32[]{:S(2)}, u32[]{:S(2)}) collective-permute-start(bf16[2,128,768]{2,1,0:T(8,128)(2,1)} %get-tuple-element.91), channel_id=1, source_target_pairs={{0,1},{1,0},{2,3},{3,2},{4,5},{5,4},{6,7},{7,6},{8,9},{9,8},{10,11... | collective-permute-start | bytes 1179656 | tf_op jit(solution)/shard_map/ppermute | solution.py:514
  81.3 128.2 %collective-permute-start.6 = (bf16[2,128,768]{2,1,0:T(8,128)(2,1)}, bf16[2,128,768]{2,1,0:T(8,128)(2,1)}, u32[]{:S(2)}, u32[]{:S(2)}) collective-permute-start(bf16[2,128,768]{2,1,0:T(8,128)(2,1)} %get-tuple-element.90), channel_id=1, source_target_pairs={{0,2},{1,3},{2,0},{3,1},{4,6},{5,7},{6,4},{7,5},{8,10},{9,11},{10,... | collective-permute-start | bytes 1179656 | tf_op jit(solution)/shard_map/ppermute | solution.py:514
  142.2 125.6 %collective-permute-start.11 = (bf16[3072,384]{1,0:T(8,128)(2,1)}, bf16[3072,384]{1,0:T(8,128)(2,1)}, u32[]{:S(2)}, u32[]{:S(2)}) collective-permute-start(bf16[3072,384]{1,0:T(8,128)(2,1)} %all-gather.7.cloned.1.call-done.outer_mine), channel_id=1, source_target_pairs={{0,1},{1,0},{2,3},{3,2},{4,5},{5,4},{6,7},{7,6},{8,9},{9,8},{10,11... | collective-permute-start | bytes 7077896 | tf_op jit(solution)/shard_map/ppermute | solution.py:462
  206.7 61.1 %collective-permute-start.9 = (bf16[768,1536]{1,0:T(8,128)(2,1)}, bf16[768,1536]{1,0:T(8,128)(2,1)}, u32[]{:S(2)}, u32[]{:S(2)}) collective-permute-start(bf16[768,1536]{1,0:T(8,128)(2,1)} %all-gather.5.cloned.1.call-done.inner_mine), channel_id=1, source_target_pairs={{0,1},{1,0},{2,3},{3,2},{4,5},{5,4},{6,7},{7,6},{8,9},{9,8},{10,11... | collective-permute-start | bytes 7077896 | tf_op jit(solution)/shard_map/ppermute | solution.py:462
  209.0 3.0 collective-permute-start
  209.5 12.2 %collective-permute-start.1 = (bf16[2,128,768]{2,1,0:T(8,128)(2,1)}, bf16[2,128,768]{2,1,0:T(8,128)(2,1)S(1)}, u32[]{:S(2)}, u32[]{:S(2)}) collective-permute-start(bf16[2,128,768]{2,1,0:T(8,128)(2,1)} %get-tuple-element.96), channel_id=1, source_target_pairs={{0,2},{1,3},{2,0},{3,1},{4,6},{5,7},{6,4},{7,5},{8,10},{9,11},{10,... | collective-permute-start | bytes 1179656 | tf_op jit(solution)/shard_map/ppermute | solution.py:514
  212.0 17.2 %collective-permute-start.7 = (bf16[2,128,768]{2,1,0:T(8,128)(2,1)}, bf16[2,128,768]{2,1,0:T(8,128)(2,1)S(1)}, u32[]{:S(2)}, u32[]{:S(2)}) collective-permute-start(bf16[2,128,768]{2,1,0:T(8,128)(2,1)} %get-tuple-element.89), channel_id=1, source_target_pairs={{0,3},{1,2},{2,1},{3,0},{4,7},{5,6},{6,5},{7,4},{8,11},{9,10},{10,... | collective-permute-start | bytes 1179656 | tf_op jit(solution)/shard_map/ppermute | solution.py:514
  221.7 15.1 %collective-permute-start.2 = (bf16[2,128,768]{2,1,0:T(8,128)(2,1)}, bf16[2,128,768]{2,1,0:T(8,128)(2,1)S(1)}, u32[]{:S(2)}, u32[]{:S(2)}) collective-permute-start(bf16[2,128,768]{2,1,0:T(8,128)(2,1)} %get-tuple-element.93), channel_id=1, source_target_pairs={{0,3},{1,2},{2,1},{3,0},{4,7},{5,6},{6,5},{7,4},{8,11},{9,10},{10,... | collective-permute-start | bytes 1179656 | tf_op jit(solution)/shard_map/ppermute | solution.py:514
  360.1 4.3 collective-permute-start.18
  367.8 258.4 %reduce-scatter.8.cloned.1.call-start = ((), (), s32[]{:S(2)}) async-start(), calls=%async_computation.7 | async-start | bytes 2506752 | tf_op jit(solution)/shard_map/reduce_scatter | solution.py:696
  367.8 4.6 collective-permute-start.22
  376.3 384.7 %reduce-scatter.6.cloned.1.call-start = ((), (), s32[]{:S(2)}) async-start(), calls=%async_computation.6 | async-start | bytes 3133440 | tf_op jit(solution)/shard_map/reduce_scatter | solution.py:733
  376.6 5.7 collective-permute-start.20
  388.5 3.8 collective-permute-start.25
  392.3 11.2 %collective-permute-start.26 = (f32[2,2,288]{2,1,0:T(2,128)S(1)}, f32[2,2,288]{2,1,0:T(2,128)S(1)}, u32[]{:S(2)}, u32[]{:S(2)}) collective-permute-start(f32[2,2,288]{2,1,0:T(2,128)S(1)} %bitcast.54), channel_id=1, source_target_pairs={{0,4},{1,5},{2,6},{3,7},{4,0},{5,1},{6,2},{7,3},{8,12},{9,13},{10,... | collective-permute-start | bytes 13832 | tf_op jit(solution)/shard_map/ppermute | solution.py:502
  403.6 5.0 collective-permute-start.27
  406.7 8.4 %collective-permute-start.15 = (bf16[2,128,768]{2,1,0:T(8,128)(2,1)}, bf16[2,128,768]{2,1,0:T(8,128)(2,1)}, u32[]{:S(2)}, u32[]{:S(2)}) collective-permute-start(bf16[2,128,768]{2,1,0:T(8,128)(2,1)} %get-tuple-element.83), channel_id=1, source_target_pairs={{0,1},{1,0},{2,3},{3,2},{4,5},{5,4},{6,7},{7,6},{8,9},{9,8},{10,11... | collective-permute-start | bytes 1179656 | tf_op jit(solution)/shard_map/ppermute | solution.py:514
  406.7 12.8 %collective-permute-start.16 = (bf16[2,128,768]{2,1,0:T(8,128)(2,1)}, bf16[2,128,768]{2,1,0:T(8,128)(2,1)}, u32[]{:S(2)}, u32[]{:S(2)}) collective-permute-start(bf16[2,128,768]{2,1,0:T(8,128)(2,1)} %get-tuple-element.82), channel_id=1, source_target_pairs={{0,2},{1,3},{2,0},{3,1},{4,6},{5,7},{6,4},{7,5},{8,10},{9,11},{10,... | collective-permute-start | bytes 1179656 | tf_op jit(solution)/shard_map/ppermute | solution.py:514
  407.3 20.9 %collective-permute-start.17 = (bf16[2,128,768]{2,1,0:T(8,128)(2,1)}, bf16[2,128,768]{2,1,0:T(8,128)(2,1)}, u32[]{:S(2)}, u32[]{:S(2)}) collective-permute-start(bf16[2,128,768]{2,1,0:T(8,128)(2,1)} %get-tuple-element.81), channel_id=1, source_target_pairs={{0,3},{1,2},{2,1},{3,0},{4,7},{5,6},{6,5},{7,4},{8,11},{9,10},{10,... | collective-permute-start | bytes 1179656 | tf_op jit(solution)/shard_map/ppermute | solution.py:514
  408.6 4.5 collective-permute-start.28
  411.3 19.8 %collective-permute-start.12 = (bf16[2,128,768]{2,1,0:T(8,128)(2,1)}, bf16[2,128,768]{2,1,0:T(8,128)(2,1)}, u32[]{:S(2)}, u32[]{:S(2)}) collective-permute-start(bf16[2,128,768]{2,1,0:T(8,128)(2,1)} %get-tuple-element.87), channel_id=1, source_target_pairs={{0,1},{1,0},{2,3},{3,2},{4,5},{5,4},{6,7},{7,6},{8,9},{9,8},{10,11... | collective-permute-start | bytes 1179656 | tf_op jit(solution)/shard_map/ppermute | solution.py:514
  413.2 24.8 %collective-permute-start.13 = (bf16[2,128,768]{2,1,0:T(8,128)(2,1)}, bf16[2,128,768]{2,1,0:T(8,128)(2,1)}, u32[]{:S(2)}, u32[]{:S(2)}) collective-permute-start(bf16[2,128,768]{2,1,0:T(8,128)(2,1)} %get-tuple-element.86), channel_id=1, source_target_pairs={{0,2},{1,3},{2,0},{3,1},{4,6},{5,7},{6,4},{7,5},{8,10},{9,11},{10,... | collective-permute-start | bytes 1179656 | tf_op jit(solution)/shard_map/ppermute | solution.py:514
  415.1 31.4 %collective-permute-start.14 = (bf16[2,128,768]{2,1,0:T(8,128)(2,1)}, bf16[2,128,768]{2,1,0:T(8,128)(2,1)S(1)}, u32[]{:S(2)}, u32[]{:S(2)}) collective-permute-start(bf16[2,128,768]{2,1,0:T(8,128)(2,1)} %get-tuple-element.85), channel_id=1, source_target_pairs={{0,3},{1,2},{2,1},{3,0},{4,7},{5,6},{6,5},{7,4},{8,11},{9,10},{10,... | collective-permute-start | bytes 1179656 | tf_op jit(solution)/shard_map/ppermute | solution.py:514
  494.8 132.4 %collective-permute-start.19 = (bf16[3,24,384]{2,1,0:T(8,128)(2,1)S(1)}, bf16[3,24,384]{2,1,0:T(8,128)(2,1)}, u32[]{:S(2)}, u32[]{:S(2)}) collective-permute-start(bf16[3,24,384]{2,1,0:T(8,128)(2,1)S(1)} %get-tuple-element.106), channel_id=1, source_target_pairs={{0,1},{1,0},{2,3},{3,2},{4,5},{5,4},{6,7},{7,6},{8,9},{9,8},{10,11... | collective-permute-start | bytes 165896 | tf_op jit(solution)/shard_map/ppermute | solution.py:462
  761.9 1.6 collective-permute-start.21
  (33 other events, 2171.3 us)
Sparse Core Ops, SparseCore 0:
  11.4 66.0 all-gather.8
  80.9 61.1 all-gather.6
  145.5 61.0 all-gather.4
  367.9 125.9 reduce-scatter.3
  498.7 127.4 reduce-scatter.7
  631.8 129.1 reduce-scatter.5

commit v3 on v2

v3 whole, which is shorter than its diff:
```python
import functools

import jax
import jax.numpy as jnp
import numpy as np
from jax import lax
from jax.experimental import pallas as pl
from jax.experimental.pallas import tpu as pltpu
from jax.sharding import Mesh, PartitionSpec as P

HEADS = 12
HEAD = 64
PAIR = 2 * HEAD
PAIRS = HEADS // 2
STEP = 10

NORM_EPS = 1e-12
BETA_ONE = 0.9
BETA_TWO = 0.999
ADAM_EPS = 1e-06
MATRIX_LEARN_RATE = 0.05
VECTOR_RATE = 0.5
WEIGHT_DECAY = 0.01
MASK_FILL = -1e30
SCORE_SCALE = HEAD ** (-0.5)
ROOT_HALF = 0.5**0.5
DENSITY = 0.3989422804014327

CHIPS = ("dp_hi", "dp_lo", "ctx_hi")
SIDE = "ctx_lo"
ALL = CHIPS + (SIDE,)
CONTEXT = ("ctx_hi", "ctx_lo")
LOW = jnp.bfloat16
WIDE = jnp.float32
VMEM_BYTES = 60 * 1024 * 1024


def adam_step(weight, gradient, moment_one, moment_two, step_rate, decay_rate):
    first_new = BETA_ONE * moment_one + (1.0 - BETA_ONE) * gradient
    second_new = BETA_TWO * moment_two + (1.0 - BETA_TWO) * gradient * gradient
    first_hat = first_new / (1.0 - BETA_ONE**STEP)
    second_hat = second_new / (1.0 - BETA_TWO**STEP)
    updated = weight - step_rate * (
        first_hat / (jnp.sqrt(second_hat) + ADAM_EPS) + decay_rate * weight
    )
    return (second_new, updated)


def matmul(left, right):
    return jnp.dot(left, right, preferred_element_type=WIDE)


def contract_rows(left, right):
    return lax.dot_general(left, right, (((0,), (0,)), ((), ())), preferred_element_type=WIDE)


def times_transpose(left, right):
    return lax.dot_general(left, right, (((1,), (1,)), ((), ())), preferred_element_type=WIDE)


def flip(value):
    return value.astype(WIDE).T


def norm_stats(value):
    centered = value - jnp.mean(value, axis=-1, keepdims=True)
    variance = jnp.mean(centered * centered, axis=-1, keepdims=True)
    scale = lax.rsqrt(variance + NORM_EPS)
    return centered * scale, scale


def norm_back(grad, gain, unit, scale):
    scaled = grad * gain
    return scale * (
        scaled
        - jnp.mean(scaled, axis=-1, keepdims=True)
        - unit * jnp.mean(scaled * unit, axis=-1, keepdims=True)
    )


def load_pieces(coords, picks, pieces, target, sems, first=0):
    rows = target.shape[4]
    side, y_here, x_here = coords[0], coords[1], coords[2]
    squares = target.shape[2] * target.shape[3]
    per_side = len(pieces) // 2
    half = pieces[0].shape[2]
    copies = []
    for place, pick in enumerate(picks):
        for number, source in enumerate(pieces):
            which, order = divmod(number, per_side)
            start = pl.multiple_of((side if which == 0 else 1 - side) * half, half)
            if squares == 1:
                planes, y_at, x_at = pl.ds(0, 1), 0, 0
            else:
                y_at = 1 - y_here if order >= 2 else y_here
                x_at = 1 - x_here if order in (1, 3, 4) else x_here
                low = pieces[3].shape[0]
                planes = pl.ds(low if order == 4 else 0, source.shape[0])
            copies.append(
                pltpu.make_async_copy(
                    source.at[:, pl.ds(pick * rows, rows), :],
                    target.at[place, planes, y_at, x_at, :, pl.ds(start, half)],
                    sems.at[first + len(copies)],
                )
            )
    return copies


def load_now(copies):
    for copy in copies:
        copy.start()
    for copy in copies:
        copy.wait()


def flat(target, place=0):
    _, planes, high, wide, rows, width = target.shape
    return target.at[place].reshape(planes * high * wide * rows, width)


def store_pieces(coords, keep_out, send_out, read, place=None):
    side, y_here, x_here = coords[0], coords[1], coords[2]
    squares, planes = keep_out.shape[:2]
    rows = keep_out.shape[-2]
    half = keep_out.shape[-1]
    for out, own_side in ((keep_out, side), (send_out, 1 - side)):
        columns = pl.ds(pl.multiple_of(own_side * half, half), half)
        for square in range(squares):
            for plane in range(planes):
                if squares == 1:
                    block = plane
                else:
                    y_at = 1 - y_here if square >= 2 else y_here
                    x_at = 1 - x_here if square % 2 else x_here
                    block = (plane * 2 + y_at) * 2 + x_at
                part = read(pl.ds(pl.multiple_of(block * rows, rows), rows), columns).astype(LOW)
                if place is None:
                    out[square, plane] = part
                else:
                    out[square, plane, place] = part


def head_masks():
    lane = lax.broadcasted_iota(jnp.int32, (1, PAIR), 1)
    return [lane < HEAD, lane >= HEAD]


def only(value, mask):
    return jnp.where(mask, value, 0.0).astype(LOW)


def attend_kernel(sequence, pieces, earlier, *refs):
    lengths, coords, tokens, vec = refs[:4]
    sources = refs[4 : 4 + pieces]
    query_out, key_out, value_out, mixed_out, sum_out, norm_out = refs[
        4 + pieces + earlier : 10 + pieces + earlier
    ]
    weights, value_flip, mixed_flip, sems = refs[10 + pieces + earlier :]
    copies = load_pieces(coords, range(4), sources, weights, sems)
    for copy in copies:
        copy.start()

    def need(place):
        for copy in copies[place * pieces : (place + 1) * pieces]:
            copy.wait()

    length = lengths[sequence]
    rows = tokens[...]
    need(0)
    query_out[...] = (matmul(rows, flat(weights, 0)[...]) + vec[0:1, :]).astype(LOW)
    need(1)
    key_out[...] = matmul(rows, flat(weights, 1)[...]).astype(LOW)
    need(2)
    value_low = (matmul(rows, flat(weights, 2)[...]) + vec[1:2, :]).astype(LOW)
    value_out[...] = value_low
    value_flip[...] = flip(value_low).astype(LOW)
    size = tokens.shape[0]
    key_valid = lax.broadcasted_iota(jnp.int32, (size, size), 0) < length
    masks = head_masks()

    def one_pair(pair, carry):
        lanes = pl.ds(pl.multiple_of(pair * PAIR, PAIR), PAIR)
        keys = key_out[:, lanes]
        queries = query_out[:, lanes].astype(WIDE) * SCORE_SCALE
        mixed, norms = [], []
        for head in range(2):
            scores = times_transpose(keys, only(queries, masks[head]))
            scores = jnp.where(key_valid, scores, MASK_FILL)
            peak = jnp.max(scores, axis=0, keepdims=True)
            exponent = jnp.exp(scores - peak)
            total = jnp.sum(exponent, axis=0, keepdims=True)
            prob = (exponent * (1.0 / total)).astype(LOW)
            start = pl.multiple_of(pair * PAIR + head * HEAD, HEAD)
            mixed.append(matmul(value_flip[pl.ds(start, HEAD), :], prob))
            norms.append(peak + jnp.log(total))
        mixed_flip[lanes, :] = jnp.concatenate(mixed, axis=0)
        norm_out[0, pair] = jnp.concatenate(norms, axis=0)
        return carry

    lax.fori_loop(0, PAIRS, one_pair, 0)
    need(3)
    mixed_low = mixed_flip[...].T.astype(LOW)
    mixed_out[...] = mixed_low
    sum_out[...] = rows.astype(WIDE) + matmul(mixed_low, flat(weights, 3)[...]) + vec[2:3, :]


def ffn_kernel(inner_pieces, outer_pieces, *refs):
    coords, first_sum, cotangent, vec, bias = refs[:5]
    inner_from = refs[5 : 5 + inner_pieces]
    outer_from = refs[5 + inner_pieces : 5 + inner_pieces + outer_pieces]
    result_out, second_out, hidden_out, keep_out, send_out, vec_grad, bias_grad = refs[
        5 + inner_pieces + outer_pieces : 12 + inner_pieces + outer_pieces
    ]
    inner_at, outer_at, total, activated, slope, sems = refs[12 + inner_pieces + outer_pieces :]
    step = pl.program_id(0)

    @pl.when(step == 0)
    def _():
        copies = load_pieces(coords, (0,), inner_from, inner_at, sems) + load_pieces(
            coords, (0,), outer_from, outer_at, sems, inner_pieces
        )
        for copy in copies:
            copy.start()
        vec_grad[...] = jnp.zeros_like(vec_grad)
        bias_grad[...] = jnp.zeros_like(bias_grad)
        total[...] = jnp.zeros_like(total)
        for copy in copies:
            copy.wait()

    inner, outer = flat(inner_at), flat(outer_at)
    unit, _ = norm_stats(first_sum[...])
    normed = unit * vec[4:5, :] + vec[5:6, :]
    normed_low = normed.astype(LOW)
    width, hidden = inner.shape
    second = normed + vec[3:4, :]
    for start in range(0, hidden, width):
        part = slice(start, start + width)
        pre = matmul(normed_low, inner[:, part]) + bias[:, part]
        cdf = 0.5 * (1.0 + lax.erf(pre * ROOT_HALF))
        active = (pre * cdf).astype(LOW)
        activated[:, part] = active
        slope[:, part] = cdf + pre * (DENSITY * jnp.exp(-0.5 * pre * pre))
        second = second + matmul(active, outer[part, :])
    unit_two, scale_two = norm_stats(second)
    result_out[...] = (unit_two * vec[6:7, :] + vec[7:8, :]).astype(LOW)
    grad = cotangent[...].astype(WIDE)
    second_grad = norm_back(grad, vec[6:7, :], unit_two, scale_two)
    second_out[...] = second_grad
    grad_low = second_grad.astype(LOW)
    vec_grad[3:4, :] += jnp.sum(grad_low.astype(WIDE), axis=0, keepdims=True)
    vec_grad[6:7, :] += jnp.sum(grad * unit_two, axis=0, keepdims=True)
    vec_grad[7:8, :] += jnp.sum(grad, axis=0, keepdims=True)
    for start in range(0, hidden, width):
        part = slice(start, start + width)
        back = times_transpose(grad_low, outer[part, :])
        hidden_low = (back * slope[:, part]).astype(LOW)
        hidden_out[:, part] = hidden_low
        bias_grad[:, part] += jnp.sum(hidden_low.astype(WIDE), axis=0, keepdims=True)
        total[part, :] += contract_rows(activated[:, part], grad_low)

    @pl.when(step == pl.num_programs(0) - 1)
    def _():
        store_pieces(coords, keep_out, send_out, lambda r, c: total[r, c])


def inner_grad_kernel(coords, first_sum, hidden_low, vec, keep_out, send_out, total):
    step = pl.program_id(0)

    @pl.when(step == 0)
    def _():
        total[...] = jnp.zeros_like(total)

    unit, _ = norm_stats(first_sum[...])
    normed_flip = flip(unit * vec[4:5, :] + vec[5:6, :]).astype(LOW)
    width, hidden = total.shape
    for start in range(0, hidden, width):
        part = slice(start, start + width)
        total[:, part] += matmul(normed_flip, hidden_low[:, part])

    @pl.when(step == pl.num_programs(0) - 1)
    def _():
        store_pieces(coords, keep_out, send_out, lambda r, c: total[r, c])


def back_kernel(inner_pieces, att_pieces, *refs):
    coords, first_sum, second_grad, hidden_low, mixed, vec = refs[:6]
    inner_from = refs[6 : 6 + inner_pieces]
    att_from = refs[6 + inner_pieces : 6 + inner_pieces + att_pieces]
    first_out, mixed_grad_out, keep_out, send_out, vec_grad = refs[
        6 + inner_pieces + att_pieces : 11 + inner_pieces + att_pieces
    ]
    inner_at, project_at, total, sems = refs[11 + inner_pieces + att_pieces :]
    step = pl.program_id(0)

    @pl.when(step == 0)
    def _():
        copies = load_pieces(coords, (0,), inner_from, inner_at, sems) + load_pieces(
            coords, (3,), att_from, project_at, sems, inner_pieces
        )
        for copy in copies:
            copy.start()
        vec_grad[...] = jnp.zeros_like(vec_grad)
        total[...] = jnp.zeros_like(total)
        for copy in copies:
            copy.wait()

    unit, scale = norm_stats(first_sum[...])
    grad = second_grad[...] + times_transpose(hidden_low[...], flat(inner_at)[...])
    first_grad = norm_back(grad, vec[4:5, :], unit, scale)
    first_out[...] = first_grad
    branch = first_grad.astype(LOW)
    vec_grad[2:3, :] += jnp.sum(branch.astype(WIDE), axis=0, keepdims=True)
    vec_grad[4:5, :] += jnp.sum(grad * unit, axis=0, keepdims=True)
    vec_grad[5:6, :] += jnp.sum(grad, axis=0, keepdims=True)
    mixed_grad_out[...] = times_transpose(branch, flat(project_at)[...]).astype(LOW)
    total[...] += contract_rows(mixed[...], branch)

    @pl.when(step == pl.num_programs(0) - 1)
    def _():
        store_pieces(coords, keep_out, send_out, lambda r, c: total[r, c])


def attend_back_kernel(sequence, last, *refs):
    lengths, coords, tokens, query, key, value, mixed_grad, normalizer = refs[:8]
    count = 3 * sequence if last else 0
    earlier = refs[8 : 8 + count]
    query_out, key_out, value_out = refs[8 + count : 11 + count]
    scratch = refs[11 + count :]
    if last:
        keep_out, send_out, vec_grad = scratch[:3]
        scratch = scratch[3:]
        total = scratch[2]
    key_flip, query_flip = scratch[:2]
    length = lengths[sequence]
    size = query.shape[0]
    key_flip[...] = flip(key[...]).astype(LOW)
    key_valid = lax.broadcasted_iota(jnp.int32, (size, size), 0) < length
    masks = head_masks()

    def one_pair(pair, carry):
        lanes = pl.ds(pl.multiple_of(pair * PAIR, PAIR), PAIR)
        keys = key[:, lanes]
        values = value[:, lanes]
        queries = query[:, lanes].astype(WIDE) * SCORE_SCALE
        grads = mixed_grad[:, lanes].astype(WIDE)
        norms = normalizer[0, pair]
        query_parts, key_part, value_part = [], 0.0, 0.0
        for head in range(2):
            own_query = only(queries, masks[head])
            own_grad = only(grads, masks[head])
            scores = times_transpose(keys, own_query)
            prob = jnp.where(key_valid, jnp.exp(scores - norms[head : head + 1, :]), 0.0)
            prob_grad = times_transpose(values, own_grad)
            row_term = jnp.sum(prob_grad * prob, axis=0, keepdims=True)
            score_low = (prob * (prob_grad - row_term)).astype(LOW)
            value_part = value_part + matmul(prob.astype(LOW), own_grad)
            key_part = key_part + matmul(score_low, own_query)
            start = pl.multiple_of(pair * PAIR + head * HEAD, HEAD)
            query_parts.append(matmul(key_flip[pl.ds(start, HEAD), :], score_low))
        query_flip[lanes, :] = jnp.concatenate(query_parts, axis=0) * SCORE_SCALE
        key_out[:, lanes] = key_part.astype(LOW)
        value_out[:, lanes] = value_part.astype(LOW)
        return carry

    lax.fori_loop(0, PAIRS, one_pair, 0)
    query_out[...] = query_flip[...].T.astype(LOW)
    if not last:
        return
    vec_grad[...] = jnp.zeros_like(vec_grad)
    token_flip = flip(tokens[...]).astype(LOW)
    for place, own in enumerate((query_out, key_out, value_out)):
        grads = [earlier[3 * i + place] for i in range(sequence)] + [own]
        sums = 0.0
        for i, grad in enumerate(grads):
            part = matmul(token_flip[:, i * size : (i + 1) * size], grad[...])
            total[...] = part if i == 0 else total[...] + part
            if place != 1:
                sums = sums + jnp.sum(grad[...].astype(WIDE), axis=0, keepdims=True)
        if place != 1:
            vec_grad[place // 2 : place // 2 + 1, :] = sums
        store_pieces(coords, keep_out, send_out, lambda r, c: total[r, c], place)


def input_kernel(pieces, *refs):
    coords, first_grad, query, key, value = refs[:5]
    sources = refs[5 : 5 + pieces]
    grad_out, weights, sems = refs[5 + pieces :]
    load_now(load_pieces(coords, range(3), sources, weights, sems))
    grad = first_grad[...]
    for place, grads in enumerate((query, key, value)):
        grad = grad + times_transpose(grads[...], flat(weights, place)[...])
    grad_out[...] = grad.astype(grad_out.dtype)


def call(kernel, grid, inputs, outputs, scratch, flops, moved, aliases=None):
    return pl.pallas_call(
        kernel,
        grid=(grid,),
        in_specs=[spec for _, spec in inputs],
        out_specs=[spec for _, _, spec in outputs],
        out_shape=[jax.ShapeDtypeStruct(shape, kind) for shape, kind, _ in outputs],
        scratch_shapes=scratch,
        input_output_aliases=aliases or {},
        compiler_params=pltpu.CompilerParams(
            dimension_semantics=("arbitrary",), vmem_limit_bytes=VMEM_BYTES
        ),
        cost_estimate=pl.CostEstimate(flops=flops, bytes_accessed=moved, transcendentals=0),
    )(*[array for array, _ in inputs])


SCALARS = pl.BlockSpec(memory_space=pltpu.SMEM)
WHERE_IT_IS = pl.BlockSpec(memory_space=pl.ANY)


def tiles(rows, width):
    return pl.BlockSpec((rows, width), lambda i: (i, 0))


def block(number, *shape):
    return pl.BlockSpec(shape, lambda i: (number,) + (0,) * (len(shape) - 1))


def whole(*shape):
    return pl.BlockSpec(shape, lambda i: (0,) * len(shape))


def swap(value, axis, offset=1):
    size = lax.axis_size(axis)
    return lax.ppermute(value, axis, [(i, i ^ offset) for i in range(size)])


def swap_side(value):
    return swap(value, SIDE)


def swap_x(value):
    return swap(value, "ctx_hi")


def swap_y(value):
    return swap(value, "dp_lo")


def together(*arrays):
    return lax.optimization_barrier(arrays)


def in_order(mine, theirs, here, axis):
    return jnp.where(
        here == 0,
        jnp.concatenate([mine, theirs], axis=axis),
        jnp.concatenate([theirs, mine], axis=axis),
    )


def pair_shards(shard, side):
    half = shard.shape[-1] // 2
    axis = shard.ndim - 1
    mine = lax.dynamic_slice_in_dim(shard, side * half, half, axis)
    theirs = lax.dynamic_slice_in_dim(shard, (1 - side) * half, half, axis)
    return in_order(mine, swap_side(theirs), side, shard.ndim - 2)


def gather_planes(value):
    count = lax.axis_size("dp_hi")
    here = lax.axis_index("dp_hi")
    full = jnp.zeros((count,) + value.shape, value.dtype)
    for offset in range(count):
        part = swap(value, "dp_hi", offset) if offset else value
        full = lax.dynamic_update_slice_in_dim(full, part[None], here ^ offset, 0)
    return full


def gather_diagonal(from_x, from_y, low):
    parts = [swap_y(from_x[:low])]
    if low < from_x.shape[0]:
        parts.append(swap_x(from_y[low:]))
    return parts


def wide_sum(*arrays):
    return functools.reduce(lambda a, b: a + b, [a.astype(WIDE) for a in arrays])


class Sum:
    def __init__(self, keep, send, low):
        self.keep, self.low, self.planes = keep, low, keep.shape[1]
        self.recv = swap_side(send)

    def part(self, square, planes):
        return wide_sum(self.keep[square, planes], self.recv[square, planes])

    def first(self):
        lower, upper = slice(0, self.low), slice(self.low, self.planes)
        self.lower, self.upper = lower, upper
        self.split = self.low < self.planes
        out = [self.part(3, lower), self.part(2, lower)]
        if self.split:
            out += [self.part(3, upper), self.part(1, upper)]
        self.ready = [value.astype(LOW) for value in out]
        return self.ready

    def second(self, ready):
        self.diagonal = [swap_y(ready[0])]
        self.from_y = [swap_y(ready[1])]
        self.from_x = []
        if self.split:
            self.diagonal.append(swap_x(ready[2]))
            self.from_x.append(swap_x(ready[3]))
        out = [(self.part(1, self.lower) + self.diagonal[0].astype(WIDE)).astype(LOW)]
        if self.split:
            out.append((self.part(2, self.upper) + self.diagonal[1].astype(WIDE)).astype(LOW))
        return out

    def third(self, ready):
        self.from_x.insert(0, swap_x(ready[0]))
        if self.split:
            self.from_y.append(swap_y(ready[1]))
        runs = [self.lower] + ([self.upper] if self.split else [])
        out = [
            wide_sum(self.part(0, run), from_x, from_y).astype(LOW)
            for run, from_x, from_y in zip(runs, self.from_x, self.from_y)
        ]
        return out[0] if len(out) == 1 else jnp.concatenate(out, axis=0)

    def last(self, ready):
        here = lax.axis_index("dp_hi")
        total = lax.dynamic_index_in_dim(ready, here, 0, keepdims=False).astype(WIDE)
        for offset in range(1, self.planes):
            sent = lax.dynamic_index_in_dim(ready, here ^ offset, 0, keepdims=False)
            total = total + swap(sent, "dp_hi", offset).astype(WIDE)
        return total


def own_rows(total, side):
    rows = total.shape[-2] // 2
    axis = total.ndim - 2
    total = total.astype(LOW)
    mine = lax.dynamic_slice_in_dim(total, side * rows, rows, axis)
    theirs = lax.dynamic_slice_in_dim(total, (1 - side) * rows, rows, axis)
    return in_order(mine, swap_side(theirs), side, total.ndim - 1).astype(WIDE)


def bit_of(bit):
    return (lax.axis_index(ALL) >> bit) & 1


def halve(partial, bit, axis, count):
    mine = bit_of(bit)
    sent = lax.dynamic_index_in_dim(partial, 1 - mine, axis, keepdims=False)
    kept = lax.dynamic_index_in_dim(partial, mine, axis, keepdims=False)
    return kept + lax.ppermute(sent, ALL, [(i, i ^ (1 << bit)) for i in range(count)])


def reduce_small(partial, count):
    bits = count.bit_length() - 1
    partial = partial.reshape((2,) * bits + partial.shape[1:])
    for bit in range(bits):
        partial = halve(partial, bit, bits - 1 - bit, count)
    return partial


def to_sequences(value, parts):
    seqs, here, width = value.shape
    own = seqs // parts
    me = lax.axis_index(CONTEXT)
    full = jnp.zeros((own, parts * here, width), value.dtype)
    for offset in range(parts):
        peer = me ^ offset
        part = lax.dynamic_slice_in_dim(value, peer * own, own, 0)
        if offset:
            part = swap(part, CONTEXT, offset)
        full = lax.dynamic_update_slice_in_dim(full, part, peer * here, 1)
    return full


def to_positions(values, parts):
    own = len(values)
    length, width = values[0].shape
    here = length // parts
    me = lax.axis_index(CONTEXT)
    full = jnp.zeros((own * parts, here, width), values[0].dtype)
    for number, value in enumerate(values):
        for offset in range(parts):
            peer = me ^ offset
            part = lax.dynamic_slice_in_dim(value, peer * here, here, 0)
            if offset:
                part = swap(part, CONTEXT, offset)
            full = lax.dynamic_update_slice(full, part[None], (peer * own + number, 0, 0))
    return full


def local(
    tokens,
    cotangent,
    lengths,
    attention_weights,
    inner_weights,
    outer_weights,
    inner_bias,
    vectors,
    attention_first,
    attention_second,
    inner_first,
    inner_second,
    outer_moment_first,
    outer_second,
    bias_first,
    bias_second,
    vector_first,
    vector_second,
):
    parts = lax.axis_size(CONTEXT)
    planes = lax.axis_size("dp_hi")
    chips = lax.axis_size(CHIPS)
    count = 2 * chips
    side = lax.axis_index(SIDE)
    coords = jnp.stack([side, lax.axis_index("dp_lo"), lax.axis_index("ctx_hi")]).astype(
        jnp.int32
    )
    seq_count, local_len, width = tokens.shape
    hidden = inner_weights.shape[1]
    full_len = local_len * parts
    own_seqs = seq_count // parts
    rows = own_seqs * full_len
    att_rows, vec_cols, bias_cols = (
        attention_weights.shape[1],
        vectors.shape[1],
        inner_bias.shape[0],
    )
    half = width // 2
    tall = 16
    in_pieces = (2 * att_rows) % tall == 0
    if in_pieces:
        dims, squares = (planes, 2, 2), 4
        att_block, inner_block, outer_block = (
            2 * att_rows,
            2 * inner_weights.shape[0],
            2 * outer_weights.shape[0],
        )
    else:
        dims, squares = (1, 1, 1), 1
        att_block, inner_block, outer_block = width, width, hidden

    small = jnp.concatenate([vectors.reshape(-1), inner_bias]).astype(LOW)
    small_size = small.shape[0]
    small = jnp.pad(small.reshape(1, -1), ((0, tall - 1), (0, half - small_size)))
    small_row = 8 * att_rows
    token_rows = to_sequences(tokens, parts).reshape(rows, width)
    att_pair = pair_shards(attention_weights.astype(LOW), side).reshape(small_row, half)
    att_pair = jnp.concatenate([att_pair, small], axis=0)
    inner_pair = pair_shards(inner_weights.astype(LOW), side)
    outer_pair = pair_shards(outer_weights.astype(LOW), side)
    if in_pieces:
        att = gather_planes(att_pair)
        inner = gather_planes(inner_pair)
        outer = gather_planes(outer_pair)
        att_x, att_y = swap_x(att), swap_y(att)
        att_x, att_y, token_rows = together(att_x, att_y, token_rows)
        att_mine = [att, att_x, att_y] + gather_diagonal(att_x, att_y, planes // 2)
        att_all = att_mine + [swap_side(piece) for piece in att_mine]
        token_rows, inner, outer = together(token_rows, inner, outer)
        inner_x, inner_y = swap_x(inner), swap_y(inner)
        outer_x, outer_y = swap_x(outer), swap_y(outer)

        def small_of(pieces):
            own, from_x, from_y = [
                piece[:, None, None, small_row, :small_size] for piece in pieces[:3]
            ]
            diagonal = jnp.concatenate(
                [piece[:, None, None, small_row, :small_size] for piece in pieces[3:]], axis=0
            )
            x_here, y_here = coords[2], coords[1]
            return in_order(
                in_order(own, from_x, x_here, 2), in_order(from_y, diagonal, x_here, 2), y_here, 1
            ).reshape(chips, 1, small_size)

        small_all = in_order(
            small_of(att_mine), small_of(att_all[len(att_mine) :]), side, 1
        )
    else:
        att = lax.all_gather(att_pair, CHIPS, axis=0, tiled=False)
        inner = lax.all_gather(inner_pair, CHIPS, axis=0, tiled=True)[None]
        outer = lax.all_gather(outer_pair, CHIPS, axis=0, tiled=True)[None]
        small_mine = att[:, None, small_row, :small_size]
        small_all = in_order(small_mine, swap_side(small_mine), side, 1)
        att = att[:, :small_row].reshape(chips, 4, 2 * att_rows, half)
        att = att.transpose(1, 0, 2, 3).reshape(1, 4 * width, half)
        att_all, inner_all, outer_all = [
            [value, swap_side(value)] for value in (att, inner, outer)
        ]
    small_all = small_all.reshape(count, small_size).astype(WIDE)
    vec = (
        small_all[:, : 8 * vec_cols].reshape(count, 8, vec_cols).transpose(1, 0, 2).reshape(8, -1)
    )
    bias = small_all[:, 8 * vec_cols :].reshape(1, -1)
    own_lengths = lax.dynamic_slice_in_dim(lengths, lax.axis_index(CONTEXT) * own_seqs, own_seqs)

    def in_place(pieces):
        return [(piece, WHERE_IT_IS) for piece in pieces]

    norm_shape = (own_seqs, PAIRS, 2, full_len)
    low_rows = (rows, width)
    vec_spec = whole(8, width)
    square = 2 * rows * width * width
    attend_flops = 8 * rows * full_len * width

    held = []
    for number in range(own_seqs):
        own_rows_spec = block(number, full_len, width)
        inputs = [
            (own_lengths, SCALARS),
            (coords, SCALARS),
            (token_rows, own_rows_spec),
            (vec, vec_spec),
        ] + in_place(att_all)
        held = call(
            functools.partial(attend_kernel, number, len(att_all), len(held)),
            1,
            inputs + in_place(held),
            [(low_rows, LOW, own_rows_spec)] * 4
            + [
                (low_rows, WIDE, own_rows_spec),
                (norm_shape, WIDE, block(number, 1, PAIRS, 2, full_len)),
            ],
            [
                pltpu.VMEM((4,) + dims + (att_block, width), LOW),
                pltpu.VMEM((width, full_len), LOW),
                pltpu.VMEM((width, full_len), WIDE),
                pltpu.SemaphoreType.DMA((4 * len(att_all),)),
            ],
            (4 * square + 2 * attend_flops) // own_seqs,
            20 * rows * width // own_seqs,
            {len(inputs) + i: i for i in range(len(held))},
        )
        if in_pieces and number == 0:
            *held, inner_x, inner_y, outer_x, outer_y = together(
                *held, inner_x, inner_y, outer_x, outer_y
            )
            inner_all = [inner, inner_x, inner_y] + gather_diagonal(inner_x, inner_y, planes)
            outer_all = [outer, outer_x, outer_y] + gather_diagonal(outer_x, outer_y, planes)
            inner_all = inner_all + [swap_side(piece) for piece in inner_all]
            outer_all = outer_all + [swap_side(piece) for piece in outer_all]
    query, key, value, mixed, first_sum, normalizer = held
    cot_rows = to_sequences(cotangent.astype(LOW), parts).reshape(rows, width)

    def grad_pieces(rows_here, columns, matrices=None):
        lead = (squares, dims[0]) + ((matrices,) if matrices else ())
        shape = lead + (rows_here, columns)
        return [(shape, LOW, whole(*shape))] * 2

    tile = 256
    row_tile = tiles(tile, width)
    hidden_tile = tiles(tile, hidden)
    result, second_grad, hidden_low, outer_keep, outer_send, vec_ffn, bias_grad = call(
        functools.partial(ffn_kernel, len(inner_all), len(outer_all)),
        rows // tile,
        [
            (coords, SCALARS),
            (first_sum, row_tile),
            (cot_rows, row_tile),
            (vec, vec_spec),
            (bias, whole(1, hidden)),
        ]
        + in_place(inner_all)
        + in_place(outer_all),
        [
            (low_rows, LOW, row_tile),
            (low_rows, WIDE, row_tile),
            ((rows, hidden), LOW, hidden_tile),
        ]
        + grad_pieces(outer_block, half)
        + [((8, width), WIDE, vec_spec), ((1, hidden), WIDE, whole(1, hidden))],
        [
            pltpu.VMEM((1,) + dims + (inner_block, hidden), LOW),
            pltpu.VMEM((1,) + dims + (outer_block, width), LOW),
            pltpu.VMEM((hidden, width), WIDE),
            pltpu.VMEM((tile, hidden), LOW),
            pltpu.VMEM((tile, hidden), WIDE),
            pltpu.SemaphoreType.DMA((len(inner_all) + len(outer_all),)),
        ],
        16 * square + 60 * rows * hidden,
        30 * rows * width,
    )
    output_tokens = to_positions(list(result.reshape(own_seqs, full_len, width)), parts)

    inner_keep, inner_send = call(
        inner_grad_kernel,
        rows // tile,
        [
            (coords, SCALARS),
            (first_sum, row_tile),
            (hidden_low, hidden_tile),
            (vec, vec_spec),
        ],
        grad_pieces(inner_block, hidden // 2),
        [pltpu.VMEM((width, hidden), WIDE)],
        4 * square,
        18 * rows * width,
    )
    if in_pieces:
        outer_sum = Sum(outer_keep, outer_send, planes)
        outer_ready = outer_sum.first()
        *outer_ready, second_grad, inner_send = together(*outer_ready, second_grad, inner_send)

    first_grad, mixed_grad, project_keep, project_send, vec_mid = call(
        functools.partial(back_kernel, len(inner_all), len(att_all)),
        rows // tile,
        [
            (coords, SCALARS),
            (first_sum, row_tile),
            (second_grad, row_tile),
            (hidden_low, hidden_tile),
            (mixed, row_tile),
            (vec, vec_spec),
        ]
        + in_place(inner_all)
        + in_place(att_all),
        [(low_rows, WIDE, row_tile), (low_rows, LOW, row_tile)]
        + grad_pieces(att_block, half)
        + [((8, width), WIDE, vec_spec)],
        [
            pltpu.VMEM((1,) + dims + (inner_block, hidden), LOW),
            pltpu.VMEM((1,) + dims + (att_block, width), LOW),
            pltpu.VMEM((width, width), WIDE),
            pltpu.SemaphoreType.DMA((len(inner_all) + len(att_all),)),
        ],
        6 * square,
        24 * rows * width,
    )
    if in_pieces:
        outer_ready = outer_sum.second(outer_ready)
        inner_sum = Sum(inner_keep, inner_send, planes)
        inner_ready = inner_sum.first()
        mixed_grad, *ready = together(mixed_grad, *outer_ready, *inner_ready)
        outer_ready, inner_ready = ready[: len(outer_ready)], ready[len(outer_ready) :]

    grads = []
    for number in range(own_seqs):
        last = number == own_seqs - 1
        own_rows_spec = block(number, full_len, width)
        seq_shape = (full_len, width)
        earlier = [value for three in grads for value in three] if last else []
        outputs = [(seq_shape, LOW, whole(*seq_shape))] * 3
        scratch = [pltpu.VMEM((width, full_len), LOW), pltpu.VMEM((width, full_len), WIDE)]
        if last:
            outputs = (
                outputs + grad_pieces(att_block, half, 3) + [((8, width), WIDE, vec_spec)]
            )
            scratch = scratch + [pltpu.VMEM((width, width), WIDE)]
        three = call(
            functools.partial(attend_back_kernel, number, last),
            1,
            [
                (own_lengths, SCALARS),
                (coords, SCALARS),
                (token_rows, whole(rows, width)),
                (query, own_rows_spec),
                (key, own_rows_spec),
                (value, own_rows_spec),
                (mixed_grad, own_rows_spec),
                (normalizer, block(number, 1, PAIRS, 2, full_len)),
            ]
            + [(value_, whole(*seq_shape)) for value_ in earlier],
            outputs,
            scratch,
            5 * attend_flops // own_seqs + (3 * square if last else 0),
            20 * rows * width // own_seqs,
        )
        grads.append(list(three[:3]))
        if in_pieces and number == 0:
            outer_ready = outer_sum.third(outer_ready)
            inner_ready = inner_sum.second(inner_ready)
            project_sum = Sum(project_keep, project_send, planes)
            project_ready = project_sum.first()
            mixed_grad, grads[0][0], outer_ready, *ready = together(
                mixed_grad, grads[0][0], outer_ready, *inner_ready, *project_ready
            )
            inner_ready, project_ready = ready[: len(inner_ready)], ready[len(inner_ready) :]
    att_keep, att_send, vec_att = three[3:]

    if in_pieces:
        att_sum = Sum(att_keep, att_send, planes // 2)
        att_total = att_sum.last(att_sum.third(att_sum.second(att_sum.first())))
        outer_total = outer_sum.last(outer_ready)
        inner_total = inner_sum.last(inner_sum.third(inner_ready))
        project_total = project_sum.last(project_sum.third(project_sum.second(project_ready)))
    else:

        def scatter(keep, send):
            partial = (keep + swap_side(send)).reshape((-1,) + keep.shape[-2:])
            matrices, length, columns = partial.shape
            partial = partial.reshape(matrices, chips, length // chips, columns)
            return lax.psum_scatter(
                partial.transpose(1, 0, 2, 3), CHIPS, scatter_dimension=0, tiled=False
            )

        att_total = scatter(att_keep, att_send)
        outer_total = scatter(outer_keep, outer_send)[0]
        inner_total = scatter(inner_keep, inner_send)[0]
        project_total = scatter(project_keep, project_send)[0]
    attention_total = jnp.concatenate(
        [own_rows(att_total, side), own_rows(project_total, side)[None]], axis=0
    )
    inner_total = own_rows(inner_total, side)
    outer_total = own_rows(outer_total, side)

    vector_grad = vec_ffn + vec_mid + vec_att
    small_grad = jnp.concatenate(
        [
            vector_grad.reshape(8, count, vec_cols).transpose(1, 0, 2).reshape(count, -1),
            bias_grad.reshape(count, bias_cols),
        ],
        axis=1,
    )
    small_total = reduce_small(small_grad, count)
    vector_total = small_total[: 8 * vec_cols].reshape(8, vec_cols)
    bias_total = small_total[8 * vec_cols :]

    input_grads = []
    for number in range(own_seqs):
        seq_shape = (full_len, width)
        (grad,) = call(
            functools.partial(input_kernel, len(att_all)),
            1,
            [(coords, SCALARS), (first_grad, block(number, full_len, width))]
            + [(value_, whole(*seq_shape)) for value_ in grads[number]]
            + in_place(att_all),
            [(seq_shape, LOW, whole(*seq_shape))],
            [
                pltpu.VMEM((3,) + dims + (att_block, width), LOW),
                pltpu.SemaphoreType.DMA((3 * len(att_all),)),
            ],
            3 * square // own_seqs,
            12 * rows * width // own_seqs,
        )
        input_grads.append(grad)
    input_grad = to_positions(input_grads, parts).astype(WIDE)

    attention_square, attention_new = adam_step(
        attention_weights,
        attention_total,
        attention_first,
        attention_second,
        MATRIX_LEARN_RATE,
        WEIGHT_DECAY,
    )
    inner_square, inner_new = adam_step(
        inner_weights, inner_total, inner_first, inner_second, MATRIX_LEARN_RATE, WEIGHT_DECAY
    )
    outer_square, outer_new = adam_step(
        outer_weights,
        outer_total,
        outer_moment_first,
        outer_second,
        MATRIX_LEARN_RATE,
        WEIGHT_DECAY,
    )
    bias_square, bias_new = adam_step(
        inner_bias, bias_total, bias_first, bias_second, VECTOR_RATE, 0.0
    )
    vector_square, vector_new = adam_step(
        vectors, vector_total, vector_first, vector_second, VECTOR_RATE, 0.0
    )
    return (
        output_tokens,
        input_grad,
        attention_total,
        attention_square,
        attention_new,
        inner_total,
        inner_square,
        inner_new,
        outer_total,
        outer_square,
        outer_new,
        bias_total,
        bias_square,
        bias_new,
        vector_total,
        vector_square,
        vector_new,
    )


def solution(mesh):
    split = Mesh(
        np.asarray(mesh.devices).reshape(
            mesh.shape["dp"] // 2, 2, mesh.shape["context"] // 2, 2
        ),
        ALL,
    )
    dp = ("dp_hi", "dp_lo")
    rows3 = P(dp, CONTEXT, None)
    mid3 = P(None, ALL, None)
    row2 = P(ALL, None)
    col2 = P(None, ALL)
    one = P(ALL)
    return jax.shard_map(
        local,
        mesh=split,
        in_specs=(rows3, rows3, P(dp), mid3, row2, row2, one, col2)
        + (mid3, mid3, row2, row2, row2, row2, one, one, col2, col2),
        out_specs=(rows3, rows3)
        + (mid3,) * 3
        + (row2,) * 6
        + (one,) * 3
        + (col2,) * 3,
        check_vma=False,
    )
```

time: 773 us -> 445 us (0.58)
  waiting for transfers between devices: 561 us -> 120 us
  starting transfers between devices: 17.6 us -> 83 us
  Pallas kernels: 128 us -> 151 us
  local copies, waits for them, and re-layouts: 25.9 us -> 44.4 us
  other arithmetic: 24.2 us -> 38.1 us
  between operations: 14.8 us -> 2.34 us
    reduce_scatter x3 -> x0, waiting for transfers between devices: 310 us -> none  [the longest x1 132 us: local(): lax.psum_scatter(inner_keep + swap_side(inner_send), CHIPS, scatter_dimen...]
    all_gather x3 -> x0, waiting for transfers between devices: 186 us -> none  [the longest x1 64.5 us: local(): lax.all_gather(gather_half(inner_weights.astype(LOW), side), CHIPS, axis=...]
    ppermute x24 -> x88, starting transfers between devices: 10.2 us -> 78.2 us  [swap(): return lax.ppermute(value, axis, [(i, i ^ offset) for i in range(size)])]
    ppermute x24 -> x88, waiting for transfers between devices: 60.2 us -> 113 us  [swap(): return lax.ppermute(value, axis, [(i, i ^ offset) for i in range(size)])]
    pallas_call x5 -> x9, Pallas kernels: 128 us -> 151 us  [call(): pl.pallas_call(kernel, grid=(grid,), in_specs=[spec for _, spec in inputs...]
    convert_element_type x4 -> x21, other arithmetic: 2.1 us -> 23.1 us  [the longest x4 7.1 us: first(): self.ready = [value.astype(LOW) for value in out]]
    add x3 -> x0, other arithmetic: 9.53 us -> none  [the longest x1 3.85 us: local(): outer_keep + swap_side(outer_send)]
  transfers between devices with their start and end apart: 35 -> 93, of which waited for: 23 -> 32; matrix products, arithmetic and copies ran while one was open for 5% -> 17% of each run, Pallas kernels for 5% -> 27%
where the time goes in v3:
time: 445 us; the launch traced here: 438 us
  Pallas kernels  151 us (34%)
  waiting for transfers between devices  120 us (27%)
  starting transfers between devices  83 us (19%)
  local copies, waits for them, and re-layouts  44.4 us (10%)
  other arithmetic  38.1 us (9%)
    pallas_call x9, Pallas kernels, call(): pl.pallas_call(kernel, grid=(grid,), in_specs=[spec for _, spec in inputs...  151 us
    ppermute x88, waiting for transfers between devices, swap(): return lax.ppermute(value, axis, [(i, i ^ offset) for i in range(size)])  113 us
    ppermute x88, starting transfers between devices, swap(): return lax.ppermute(value, axis, [(i, i ^ offset) for i in range(size)])  78.2 us
  transfers between devices with their start and end apart: 93, of which 32 were waited for; matrix products, arithmetic and copies ran while one was open for 17% of the time, Pallas kernels for 27%

profile of v3, /device:TPU:0, one launch (start us, length us, event | category | flops | bytes accessed | tf_op | source)
XLA Modules:
  0.0 437.8 jit_solution(16630054756649437483)
XLA Ops:
  26.5 3.2 collective-permute-done.11
  32.3 3.1 collective-permute-start.3
  35.5 6.9 %collective-permute-done.2 = bf16[208,384]{1,0:T(8,128)(2,1)S(1)} collective-permute-done((bf16[208,384]{1,0:T(8,128)(2,1)S(1)}, bf16[208,384]{1,0:T(8,128)(2,1)S(1)}, u32[]{:S(2)}, u32[]{:S(2)}) %collective-permute-start.2) | collective-permute-done | bytes 159776 | tf_op jit(solution)/shard_map/ppermute | solution.py:429
  45.5 4.5 %collective-permute-done.12 = bf16[48,1536]{1,0:T(8,128)(2,1)S(1)} collective-permute-done((bf16[48,1536]{1,0:T(8,128)(2,1)S(1)}, bf16[48,1536]{1,0:T(8,128)(2,1)S(1)}, u32[]{:S(2)}, u32[]{:S(2)}) %collective-permute-start.12) | collective-permute-done | bytes 147488 | tf_op jit(solution)/shard_map/ppermute | solution.py:429
  52.1 2.7 collective-permute-start.14
  60.5 4.6 %collective-permute-done.5.refs_6_.refs_16_.refs_7_ = bf16[4,208,384]{2,1,0:T(8,128)(2,1)S(1)} collective-permute-done((bf16[4,208,384]{2,1,0:T(8,128)(2,1)S(1)}, bf16[4,208,384]{2,1,0:T(8,128)(2,1)S(1)}, u32[]{:S(2)}, u32[]{:S(2)}) %collective-permute-start.5) | collective-permute-done | bytes 639008 | tf_op jit(solution)/shard_map/ppermute | solution.py:429
  65.8 3.1 collective-permute-done.15
  71.8 7.7 %collective-permute-done.18.refs_8_.refs_18_.refs_9_ = bf16[2,208,384]{2,1,0:T(8,128)(2,1)S(1)} collective-permute-done((bf16[2,208,384]{2,1,0:T(8,128)(2,1)S(1)}, bf16[2,208,384]{2,1,0:T(8,128)(2,1)S(1)}, u32[]{:S(2)}, u32[]{:S(2)}) %collective-permute-start.18) | collective-permute-done | bytes 319520 | tf_op jit(solution)/shard_map/ppermute | solution.py:429
  94.9 15.9 %shard_map.305 = (bf16[1024,768]{1,0:T(8,128)(2,1)}, bf16[1024,768]{1,0:T(8,128)(2,1)}, bf16[1024,768]{1,0:T(8,128)(2,1)}, bf16[1024,768]{1,0:T(8,128)(2,1)}, f3...) custom-call(s32[2]{0:T(128)} %dynamic_slice.204.refs_0_, s32[3]{0:T(128)} %pad_add_fusion.refs_1_.refs_0_.coords, ...), custom_call_target="tpu_custom_call" | custom-call | flops 5637144576 | bytes 7864320 | tf_op jit(solution)/shard_map/pallas_call | solution.py:396
  114.3 3.8 collective-permute-done.30
  122.1 6.5 %collective-permute-done.31.refs_8_.refs_9_ = bf16[4,48,1536]{2,1,0:T(8,128)(2,1)S(1)} collective-permute-done((bf16[4,48,1536]{2,1,0:T(8,128)(2,1)}, bf16[4,48,1536]{2,1,0:T(8,128)(2,1)S(1)}, u32[]{:S(2)}, u32[]{:S(2)}) %collective-permute-start.31) | collective-permute-done | bytes 589856 | tf_op jit(solution)/shard_map/ppermute | solution.py:429
  128.6 12.3 %collective-permute-done.36.refs_16_ = bf16[4,192,384]{2,1,0:T(8,128)(2,1)} collective-permute-done((bf16[4,192,384]{2,1,0:T(8,128)(2,1)}, bf16[4,192,384]{2,1,0:T(8,128)(2,1)}, u32[]{:S(2)}, u32[]{:S(2)}) %collective-permute-start.36) | collective-permute-done | bytes 589856 | tf_op jit(solution)/shard_map/ppermute | solution.py:429
  143.7 15.7 %shard_map.306 = (bf16[1024,768]{1,0:T(8,128)(2,1)}, bf16[1024,768]{1,0:T(8,128)(2,1)}, bf16[1024,768]{1,0:T(8,128)(2,1)}, bf16[1024,768]{1,0:T(8,128)(2,1)}, f3...) custom-call(s32[2]{0:T(128)} %dynamic_slice.204.refs_0_, ...), custom_call_target="tpu_custom_call", output_to_operand_aliasing={{0}: (14, {}), {1}: (15, {}), {2}: (16, {}), {3}: (17, {}),... | custom-call | flops 5637144576 | bytes 7864320 | tf_op jit(solution)/shard_map/pallas_call | solution.py:396
  160.5 33.8 %shard_map.307 = (bf16[1024,768]{1,0:T(8,128)(2,1)}, f32[1024,768]{1,0:T(8,128)}, bf16[1024,3072]{1,0:T(8,128)(2,1)}, bf16[4,4,192,384]{3,2,1,0:T(8,128)(2,1)}, ...) custom-call(s32[3]{0:T(128)} %pad_add_fusion.refs_1_.refs_0_.coords, ...), custom_call_target="tpu_custom_call" | custom-call | flops 19516096512 | bytes 23592960 | tf_op jit(solution)/shard_map/pallas_call | solution.py:396
  201.2 11.8 %shard_map.308 = (bf16[4,4,48,1536]{3,2,1,0:T(8,128)(2,1)}, bf16[4,4,48,1536]{3,2,1,0:T(8,128)(2,1)}) custom-call(s32[3]{0:T(128)} %pad_add_fusion.refs_1_.refs_0_.coords, f32[1024,768]{1,0:T(8,128)} %get-tuple-element.100.refs_1_.first_sum, bf16[1024,3072]{1,0:T(8,128)(2,1)} %get-tuple-element.109.hidden_low.refs_3_, f32[8,768]{1,0:T(8,128)} %reshape.667.refs_3_.vec.refs_5_), custom_call_target="tpu_custom_call" | custom-call | flops 4831838208 | bytes 14155776 | tf_op jit(solution)/shard_map/pallas_call | solution.py:396
  222.2 20.1 %shard_map.309 = (f32[1024,768]{1,0:T(8,128)}, bf16[1024,768]{1,0:T(8,128)(2,1)}, bf16[4,4,48,384]{3,2,1,0:T(8,128)(2,1)}, bf16[4,4,48,384]{3,2,1,0:T(8,128)(2,1)}, f32[8,768]{1,0:T(8,128)}) custom-call(s32[3]{0:T(128)} %pad_add_fusion.refs_1_.refs_0_.coords, f32[1024,768]{1,0:T(8,128)} %get-tuple-element.100.refs_1_.first_sum, ...), custom_call_target="tpu_custom_call" | custom-call | flops 7247757312 | bytes 18874368 | tf_op jit(solution)/shard_map/pallas_call | solution.py:396
  250.2 10.2 %collective-permute-done.48 = bf16[4,192,384]{2,1,0:T(8,128)(2,1)S(1)} collective-permute-done((bf16[4,192,384]{2,1,0:T(8,128)(2,1)}, bf16[4,192,384]{2,1,0:T(8,128)(2,1)S(1)}, u32[]{:S(2)}, u32[]{:S(2)}) %collective-permute-start.48) | collective-permute-done | bytes 589856 | tf_op jit(solution)/shard_map/ppermute | solution.py:429
  267.0 16.1 %shard_map.310 = (bf16[512,768]{1,0:T(8,128)(2,1)}, bf16[512,768]{1,0:T(8,128)(2,1)}, bf16[512,768]{1,0:T(8,128)(2,1)}) custom-call(s32[2]{0:T(128)} %dynamic_slice.204.refs_0_, s32[3]{0:T(128)} %pad_add_fusion.refs_1_.refs_0_.coords, bf16[1024,768]{1,0:T(8,128)(2,1)} %bitcast.229, bf16[1024,768]{1,0:T(8,128)(2,1)} %get-tuple-element.119.refs_3_, ...), custom_call_target="tpu_custom_call" | custom-call | flops 8053063680 | bytes 7864320 | tf_op jit(solution)/shard_map/pallas_call | solution.py:396
  283.1 2.7 collective-permute-done.52
  289.8 22.4 %shard_map.312 = (bf16[512,768]{1,0:T(8,128)(2,1)}, bf16[512,768]{1,0:T(8,128)(2,1)}, bf16[512,768]{1,0:T(8,128)(2,1)}, bf16[4,4,3,48,384]{4,3,2,1,0:T(8,128)(2,...) custom-call(s32[2]{0:T(128)} %dynamic_slice.204.refs_0_, s32[3]{0:T(128)} %pad_add_fusion.refs_1_.refs_0_.coords, ...), custom_call_target="tpu_custom_call" | custom-call | flops 11676942336 | bytes 7864320 | tf_op jit(solution)/shard_map/pallas_call | solution.py:396
  318.7 7.4 %shard_map.311 = bf16[512,768]{1,0:T(8,128)(2,1)} custom-call(s32[3]{0:T(128)} %pad_add_fusion.refs_1_.refs_0_.coords, f32[1024,768]{1,0:T(8,128)} %get-tuple-element.113.refs_1_, bf16[512,768]{1,0:T(8,128)(2,1)} %get-tuple-element.129.refs_2_.refs_8_, bf16[512,768]{1,0:T(8,128)(2,1)} %get-tuple-element.130.refs_3_.refs_9_, ...), custom_call_target="tpu_custom_call" | custom-call | flops 1811939328 | bytes 4718592 | tf_op jit(solution)/shard_map/pallas_call | solution.py:396
  327.0 7.4 %shard_map.313 = bf16[512,768]{1,0:T(8,128)(2,1)} custom-call(s32[3]{0:T(128)} %pad_add_fusion.refs_1_.refs_0_.coords, f32[1024,768]{1,0:T(8,128)} %get-tuple-element.113.refs_1_, bf16[512,768]{1,0:T(8,128)(2,1)} %get-tuple-element.133.refs_2_, bf16[512,768]{1,0:T(8,128)(2,1)} %get-tuple-element.134.refs_3_, bf16[512,768]{1,0:T(8,128)(2,1)} %get-tuple-element.135.refs_4_, ...), custom_call_target="tpu_custom_call" | custom-call | flops 1811939328 | bytes 4718592 | tf_op jit(solution)/shard_map/pallas_call | solution.py:396
  343.3 3.2 collective-permute-done.92
  351.8 3.6 collective-permute-done.71
  357.8 4.6 %collective-permute-done.55 = bf16[128,768]{1,0:T(8,128)(2,1)S(1)} collective-permute-done((bf16[128,768]{1,0:T(8,128)(2,1)}, bf16[128,768]{1,0:T(8,128)(2,1)S(1)}, u32[]{:S(2)}, u32[]{:S(2)}) %collective-permute-start.55) | collective-permute-done | bytes 196640 | tf_op jit(solution)/shard_map/ppermute | solution.py:429
  362.4 2.8 collective-permute-done.56
  367.3 5.7 %collective-permute-done.58 = bf16[128,768]{1,0:T(8,128)(2,1)S(1)} collective-permute-done((bf16[128,768]{1,0:T(8,128)(2,1)S(1)}, bf16[128,768]{1,0:T(8,128)(2,1)S(1)}, u32[]{:S(2)}, u32[]{:S(2)}) %collective-permute-start.58) | collective-permute-done | bytes 196640 | tf_op jit(solution)/shard_map/ppermute | solution.py:429
  373.7 6.3 %collective-permute-done.72 = bf16[4,48,384]{2,1,0:T(8,128)(2,1)S(1)} collective-permute-done((bf16[4,48,384]{2,1,0:T(8,128)(2,1)S(1)}, bf16[4,48,384]{2,1,0:T(8,128)(2,1)S(1)}, u32[]{:S(2)}, u32[]{:S(2)}) %collective-permute-start.72) | collective-permute-done | bytes 147488 | tf_op jit(solution)/shard_map/ppermute | solution.py:429
  393.5 10.4 %collective-permute-done.78 = bf16[4,48,1536]{2,1,0:T(8,128)(2,1)S(1)} collective-permute-done((bf16[4,48,1536]{2,1,0:T(8,128)(2,1)S(1)}, bf16[4,48,1536]{2,1,0:T(8,128)(2,1)S(1)}, u32[]{:S(2)}, u32[]{:S(2)}) %collective-permute-start.78) | collective-permute-done | bytes 589856 | tf_op jit(solution)/shard_map/ppermute | solution.py:429
  412.9 2.7 collective-permute-start.82
  421.7 3.0 collective-permute-done.62
  432.0 3.1 collective-permute-done.69
  (426 shorter events, 168.3 us)
Async XLA Ops:
  3.1 49.0 %collective-permute-start.6 = (bf16[2,128,768]{2,1,0:T(8,128)(2,1)}, bf16[2,128,768]{2,1,0:T(8,128)(2,1)}, u32[]{:S(2)}, u32[]{:S(2)}) collective-permute-start(bf16[2,128,768]{2,1,0:T(8,128)(2,1)} %get-tuple-element.180), channel_id=1, source_target_pairs={{0,1},{1,0},{2,3},{3,2},{4,5},{5,4},{6,7},{7,6},{8,9},{9,8},{10,11... | collective-permute-start | bytes 1179656 | tf_op jit(solution)/shard_map/ppermute | solution.py:429
  3.6 52.2 %collective-permute-start.7 = (bf16[2,128,768]{2,1,0:T(8,128)(2,1)}, bf16[2,128,768]{2,1,0:T(8,128)(2,1)}, u32[]{:S(2)}, u32[]{:S(2)}) collective-permute-start(bf16[2,128,768]{2,1,0:T(8,128)(2,1)} %get-tuple-element.182), channel_id=1, source_target_pairs={{0,2},{1,3},{2,0},{3,1},{4,6},{5,7},{6,4},{7,5},{8,10},{9,11},{10,... | collective-permute-start | bytes 1179656 | tf_op jit(solution)/shard_map/ppermute | solution.py:429
  6.1 50.8 %collective-permute-start.8 = (bf16[2,128,768]{2,1,0:T(8,128)(2,1)}, bf16[2,128,768]{2,1,0:T(8,128)(2,1)}, u32[]{:S(2)}, u32[]{:S(2)}) collective-permute-start(bf16[2,128,768]{2,1,0:T(8,128)(2,1)} %get-tuple-element.179), channel_id=1, source_target_pairs={{0,3},{1,2},{2,1},{3,0},{4,7},{5,6},{6,5},{7,4},{8,11},{9,10},{10,... | collective-permute-start | bytes 1179656 | tf_op jit(solution)/shard_map/ppermute | solution.py:429
  71.2 22.8 %collective-permute-start.24 = (bf16[4,48,1536]{2,1,0:T(8,128)(2,1)}, bf16[4,48,1536]{2,1,0:T(8,128)(2,1)}, u32[]{:S(2)}, u32[]{:S(2)}) collective-permute-start(bf16[4,48,1536]{2,1,0:T(8,128)(2,1)} %bitcast_dynamic-update-slice_fusion.23.refs_5_.refs_6_), channel_id=1, source_target_pairs={{0,2},{2,0},{1,3},{3,1},{4,6},{6,4},{5,7},{7,5},{8,10},{10,8},{9,1... | collective-permute-start | bytes 1769480 | tf_op jit(solution)/shard_map/ppermute | solution.py:429
  81.4 30.8 %collective-permute-start.28 = (bf16[2,128,768]{2,1,0:T(8,128)(2,1)}, bf16[2,128,768]{2,1,0:T(8,128)(2,1)}, u32[]{:S(2)}, u32[]{:S(2)}) collective-permute-start(bf16[2,128,768]{2,1,0:T(8,128)(2,1)} %get-tuple-element.177), channel_id=1, source_target_pairs={{0,1},{1,0},{2,3},{3,2},{4,5},{5,4},{6,7},{7,6},{8,9},{9,8},{10,11... | collective-permute-start | bytes 1179656 | tf_op jit(solution)/shard_map/ppermute | solution.py:429
  82.5 28.4 %collective-permute-start.26 = (bf16[4,192,384]{2,1,0:T(8,128)(2,1)}, bf16[4,192,384]{2,1,0:T(8,128)(2,1)}, u32[]{:S(2)}, u32[]{:S(2)}) collective-permute-start(bf16[4,192,384]{2,1,0:T(8,128)(2,1)} %copy-done.23), channel_id=1, source_target_pairs={{0,2},{2,0},{1,3},{3,1},{4,6},{6,4},{5,7},{7,5},{8,10},{10,8},{9,1... | collective-permute-start | bytes 1769480 | tf_op jit(solution)/shard_map/ppermute | solution.py:429
  84.7 27.4 %collective-permute-start.27 = (bf16[4,192,384]{2,1,0:T(8,128)(2,1)}, bf16[4,192,384]{2,1,0:T(8,128)(2,1)}, u32[]{:S(2)}, u32[]{:S(2)}) collective-permute-start(bf16[4,192,384]{2,1,0:T(8,128)(2,1)} %copy-done.23), channel_id=1, source_target_pairs={{0,4},{4,0},{1,5},{5,1},{2,6},{6,2},{3,7},{7,3},{8,12},{12,8},{9,1... | collective-permute-start | bytes 1769480 | tf_op jit(solution)/shard_map/ppermute | solution.py:429
  93.9 19.2 %collective-permute-start.29 = (bf16[2,128,768]{2,1,0:T(8,128)(2,1)}, bf16[2,128,768]{2,1,0:T(8,128)(2,1)S(1)}, u32[]{:S(2)}, u32[]{:S(2)}) collective-permute-start(bf16[2,128,768]{2,1,0:T(8,128)(2,1)} %get-tuple-element.176), channel_id=1, source_target_pairs={{0,2},{1,3},{2,0},{3,1},{4,6},{5,7},{6,4},{7,5},{8,10},{9,11},{10,... | collective-permute-start | bytes 1179656 | tf_op jit(solution)/shard_map/ppermute | solution.py:429
  94.5 23.6 %collective-permute-start.30 = (bf16[2,128,768]{2,1,0:T(8,128)(2,1)}, bf16[2,128,768]{2,1,0:T(8,128)(2,1)S(1)}, u32[]{:S(2)}, u32[]{:S(2)}) collective-permute-start(bf16[2,128,768]{2,1,0:T(8,128)(2,1)} %get-tuple-element.175), channel_id=1, source_target_pairs={{0,3},{1,2},{2,1},{3,0},{4,7},{5,6},{6,5},{7,4},{8,11},{9,10},{10,... | collective-permute-start | bytes 1179656 | tf_op jit(solution)/shard_map/ppermute | solution.py:429
  113.1 27.7 %collective-permute-start.36 = (bf16[4,192,384]{2,1,0:T(8,128)(2,1)}, bf16[4,192,384]{2,1,0:T(8,128)(2,1)}, u32[]{:S(2)}, u32[]{:S(2)}) collective-permute-start(bf16[4,192,384]{2,1,0:T(8,128)(2,1)} %collective-permute-done.26.refs_14_), channel_id=1, source_target_pairs={{0,4},{4,0},{1,5},{5,1},{2,6},{6,2},{3,7},{7,3},{8,12},{12,8},{9,1... | collective-permute-start | bytes 1769480 | tf_op jit(solution)/shard_map/ppermute | solution.py:429
  118.1 22.8 %collective-permute-start.33 = (bf16[4,48,1536]{2,1,0:T(8,128)(2,1)}, bf16[4,48,1536]{2,1,0:T(8,128)(2,1)S(1)}, u32[]{:S(2)}, u32[]{:S(2)}) collective-permute-start(bf16[4,48,1536]{2,1,0:T(8,128)(2,1)} %collective-permute-done.24.refs_6_.refs_7_), channel_id=1, source_target_pairs={{0,1},{1,0},{2,3},{3,2},{4,5},{5,4},{6,7},{7,6},{8,9},{9,8},{10,11... | collective-permute-start | bytes 1769480 | tf_op jit(solution)/shard_map/ppermute | solution.py:429
  121.6 37.8 %collective-permute-start.38 = (bf16[4,192,384]{2,1,0:T(8,128)(2,1)}, bf16[4,192,384]{2,1,0:T(8,128)(2,1)}, u32[]{:S(2)}, u32[]{:S(2)}) collective-permute-start(bf16[4,192,384]{2,1,0:T(8,128)(2,1)} %collective-permute-done.26.refs_14_), channel_id=1, source_target_pairs={{0,1},{1,0},{2,3},{3,2},{4,5},{5,4},{6,7},{7,6},{8,9},{9,8},{10,11... | collective-permute-start | bytes 1769480 | tf_op jit(solution)/shard_map/ppermute | solution.py:429
  121.6 37.8 %collective-permute-start.34 = (bf16[4,48,1536]{2,1,0:T(8,128)(2,1)}, bf16[4,48,1536]{2,1,0:T(8,128)(2,1)S(1)}, u32[]{:S(2)}, u32[]{:S(2)}) collective-permute-start(bf16[4,48,1536]{2,1,0:T(8,128)(2,1)} %collective-permute-done.25.refs_7_.refs_8_), channel_id=1, source_target_pairs={{0,1},{1,0},{2,3},{3,2},{4,5},{5,4},{6,7},{7,6},{8,9},{9,8},{10,11... | collective-permute-start | bytes 1769480 | tf_op jit(solution)/shard_map/ppermute | solution.py:429
  128.6 30.9 %collective-permute-start.39 = (bf16[4,192,384]{2,1,0:T(8,128)(2,1)}, bf16[4,192,384]{2,1,0:T(8,128)(2,1)}, u32[]{:S(2)}, u32[]{:S(2)}) collective-permute-start(bf16[4,192,384]{2,1,0:T(8,128)(2,1)} %collective-permute-done.27.refs_15_), channel_id=1, source_target_pairs={{0,1},{1,0},{2,3},{3,2},{4,5},{5,4},{6,7},{7,6},{8,9},{9,8},{10,11... | collective-permute-start | bytes 1769480 | tf_op jit(solution)/shard_map/ppermute | solution.py:429
  140.9 18.6 %collective-permute-start.35 = (bf16[4,48,1536]{2,1,0:T(8,128)(2,1)S(1)}, bf16[4,48,1536]{2,1,0:T(8,128)(2,1)S(1)}, u32[]{:S(2)}, u32[]{:S(2)}) collective-permute-start(bf16[4,48,1536]{2,1,0:T(8,128)(2,1)S(1)} %collective-permute-done.31.refs_8_.refs_9_), channel_id=1, source_target_pairs={{0,1},{1,0},{2,3},{3,2},{4,5},{5,4},{6,7},{7,6},{8,9},{9,8},{10,11... | collective-permute-start | bytes 1769480 | tf_op jit(solution)/shard_map/ppermute | solution.py:429
  140.9 18.6 %collective-permute-start.40 = (bf16[4,192,384]{2,1,0:T(8,128)(2,1)}, bf16[4,192,384]{2,1,0:T(8,128)(2,1)}, u32[]{:S(2)}, u32[]{:S(2)}) collective-permute-start(bf16[4,192,384]{2,1,0:T(8,128)(2,1)} %collective-permute-done.36.refs_16_), channel_id=1, source_target_pairs={{0,1},{1,0},{2,3},{3,2},{4,5},{5,4},{6,7},{7,6},{8,9},{9,8},{10,11... | collective-permute-start | bytes 1769480 | tf_op jit(solution)/shard_map/ppermute | solution.py:429
  194.3 21.9 %collective-permute-start.47 = (bf16[4,4,192,384]{3,2,1,0:T(8,128)(2,1)}, bf16[4,4,192,384]{3,2,1,0:T(8,128)(2,1)S(1)}, u32[]{:S(2)}, u32[]{:S(2)}) collective-permute-start(bf16[4,4,192,384]{3,2,1,0:T(8,128)(2,1)} %get-tuple-element.107), channel_id=1, source_target_pairs={{0,1},{1,0},{2,3},{3,2},{4,5},{5,4},{6,7},{7,6},{8,9},{9,8},{10,11... | collective-permute-start | bytes 7077896 | tf_op jit(solution)/shard_map/ppermute | solution.py:429
  199.7 18.6 %collective-permute-start.42 = (bf16[128,768]{1,0:T(8,128)(2,1)}, bf16[128,768]{1,0:T(8,128)(2,1)}, u32[]{:S(2)}, u32[]{:S(2)}) collective-permute-start(bf16[128,768]{1,0:T(8,128)(2,1)} %get-tuple-element.195), channel_id=1, source_target_pairs={{0,2},{1,3},{2,0},{3,1},{4,6},{5,7},{6,4},{7,5},{8,10},{9,11},{10,... | collective-permute-start | bytes 589832 | tf_op jit(solution)/shard_map/ppermute | solution.py:429
  200.3 19.8 %collective-permute-start.43 = (bf16[128,768]{1,0:T(8,128)(2,1)}, bf16[128,768]{1,0:T(8,128)(2,1)}, u32[]{:S(2)}, u32[]{:S(2)}) collective-permute-start(bf16[128,768]{1,0:T(8,128)(2,1)} %get-tuple-element.194), channel_id=1, source_target_pairs={{0,3},{1,2},{2,1},{3,0},{4,7},{5,6},{6,5},{7,4},{8,11},{9,10},{10,... | collective-permute-start | bytes 589832 | tf_op jit(solution)/shard_map/ppermute | solution.py:429
  213.8 28.6 %collective-permute-start.44 = (bf16[128,768]{1,0:T(8,128)(2,1)}, bf16[128,768]{1,0:T(8,128)(2,1)}, u32[]{:S(2)}, u32[]{:S(2)}) collective-permute-start(bf16[128,768]{1,0:T(8,128)(2,1)} %get-tuple-element.193), channel_id=1, source_target_pairs={{0,1},{1,0},{2,3},{3,2},{4,5},{5,4},{6,7},{7,6},{8,9},{9,8},{10,11... | collective-permute-start | bytes 589832 | tf_op jit(solution)/shard_map/ppermute | solution.py:429
  214.6 30.0 %collective-permute-start.45 = (bf16[128,768]{1,0:T(8,128)(2,1)}, bf16[128,768]{1,0:T(8,128)(2,1)S(1)}, u32[]{:S(2)}, u32[]{:S(2)}) collective-permute-start(bf16[128,768]{1,0:T(8,128)(2,1)} %get-tuple-element.192), channel_id=1, source_target_pairs={{0,2},{1,3},{2,0},{3,1},{4,6},{5,7},{6,4},{7,5},{8,10},{9,11},{10,... | collective-permute-start | bytes 589832 | tf_op jit(solution)/shard_map/ppermute | solution.py:429
  216.2 29.1 %collective-permute-start.46 = (bf16[128,768]{1,0:T(8,128)(2,1)S(1)}, bf16[128,768]{1,0:T(8,128)(2,1)S(1)}, u32[]{:S(2)}, u32[]{:S(2)}) collective-permute-start(bf16[128,768]{1,0:T(8,128)(2,1)S(1)} %get-tuple-element.191), channel_id=1, source_target_pairs={{0,3},{1,2},{2,1},{3,0},{4,7},{5,6},{6,5},{7,4},{8,11},{9,10},{10,... | collective-permute-start | bytes 589832 | tf_op jit(solution)/shard_map/ppermute | solution.py:429
  218.4 43.5 %collective-permute-start.49 = (bf16[4,4,48,1536]{3,2,1,0:T(8,128)(2,1)}, bf16[4,4,48,1536]{3,2,1,0:T(8,128)(2,1)}, u32[]{:S(2)}, u32[]{:S(2)}) collective-permute-start(bf16[4,4,48,1536]{3,2,1,0:T(8,128)(2,1)} %get-tuple-element.117), channel_id=1, source_target_pairs={{0,1},{1,0},{2,3},{3,2},{4,5},{5,4},{6,7},{7,6},{8,9},{9,8},{10,11... | collective-permute-start | bytes 7077896 | tf_op jit(solution)/shard_map/ppermute | solution.py:429
  245.9 42.1 %collective-permute-start.51 = (bf16[4,192,384]{2,1,0:T(8,128)(2,1)}, bf16[4,192,384]{2,1,0:T(8,128)(2,1)S(1)}, u32[]{:S(2)}, u32[]{:S(2)}) collective-permute-start(bf16[4,192,384]{2,1,0:T(8,128)(2,1)} %get-tuple-element.125), channel_id=1, source_target_pairs={{0,4},{4,0},{1,5},{5,1},{2,6},{6,2},{3,7},{7,3},{8,12},{12,8},{9,1... | collective-permute-start | bytes 1769480 | tf_op jit(solution)/shard_map/ppermute | solution.py:429
  264.2 21.5 %collective-permute-start.52 = (bf16[4,48,1536]{2,1,0:T(8,128)(2,1)S(1)}, bf16[4,48,1536]{2,1,0:T(8,128)(2,1)}, u32[]{:S(2)}, u32[]{:S(2)}) collective-permute-start(bf16[4,48,1536]{2,1,0:T(8,128)(2,1)S(1)} %get-tuple-element.126), channel_id=1, source_target_pairs={{0,4},{4,0},{1,5},{5,1},{2,6},{6,2},{3,7},{7,3},{8,12},{12,8},{9,1... | collective-permute-start | bytes 1769480 | tf_op jit(solution)/shard_map/ppermute | solution.py:429
  264.7 23.3 %collective-permute-start.50 = (bf16[4,192,384]{2,1,0:T(8,128)(2,1)S(1)}, bf16[4,192,384]{2,1,0:T(8,128)(2,1)}, u32[]{:S(2)}, u32[]{:S(2)}) collective-permute-start(bf16[4,192,384]{2,1,0:T(8,128)(2,1)S(1)} %fusion.5), channel_id=1, source_target_pairs={{0,2},{2,0},{1,3},{3,1},{4,6},{6,4},{5,7},{7,5},{8,10},{10,8},{9,1... | collective-permute-start | bytes 1769480 | tf_op jit(solution)/shard_map/ppermute | solution.py:429
  265.5 128.0 %collective-permute-start.79 = (bf16[4,48,1536]{2,1,0:T(8,128)(2,1)}, bf16[4,48,1536]{2,1,0:T(8,128)(2,1)}, u32[]{:S(2)}, u32[]{:S(2)}) collective-permute-start(bf16[4,48,1536]{2,1,0:T(8,128)(2,1)} %get-tuple-element.141), channel_id=1, source_target_pairs={{0,4},{4,0},{1,5},{5,1},{2,6},{6,2},{3,7},{7,3},{8,12},{12,8},{9,1... | collective-permute-start | bytes 1769480 | tf_op jit(solution)/shard_map/ppermute | solution.py:429
  314.3 34.2 %collective-permute-start.84 = (bf16[192,384]{1,0:T(8,128)(2,1)}, bf16[192,384]{1,0:T(8,128)(2,1)}, u32[]{:S(2)}, u32[]{:S(2)}) collective-permute-start(bf16[192,384]{1,0:T(8,128)(2,1)} %get-tuple-element.197), channel_id=1, source_target_pairs={{0,8},{8,0},{16,24},{24,16},{1,9},{9,1},{17,25},{25,17},{2,10},{10... | collective-permute-start | bytes 442376 | tf_op jit(solution)/shard_map/ppermute | solution.py:429
  316.3 33.7 %collective-permute-start.85 = (bf16[192,384]{1,0:T(8,128)(2,1)}, bf16[192,384]{1,0:T(8,128)(2,1)}, u32[]{:S(2)}, u32[]{:S(2)}) collective-permute-start(bf16[192,384]{1,0:T(8,128)(2,1)} %get-tuple-element.199), channel_id=1, source_target_pairs={{0,16},{8,24},{16,0},{24,8},{1,17},{9,25},{17,1},{25,9},{2,18},{10... | collective-permute-start | bytes 442376 | tf_op jit(solution)/shard_map/ppermute | solution.py:429
  316.7 33.9 %collective-permute-start.86 = (bf16[192,384]{1,0:T(8,128)(2,1)}, bf16[192,384]{1,0:T(8,128)(2,1)}, u32[]{:S(2)}, u32[]{:S(2)}) collective-permute-start(bf16[192,384]{1,0:T(8,128)(2,1)} %get-tuple-element.198), channel_id=1, source_target_pairs={{0,24},{8,16},{16,8},{24,0},{1,25},{9,17},{17,9},{25,1},{2,26},{10... | collective-permute-start | bytes 442376 | tf_op jit(solution)/shard_map/ppermute | solution.py:429
  346.5 44.5 %collective-permute-start.60 = (bf16[4,4,3,48,384]{4,3,2,1,0:T(8,128)(2,1)}, bf16[4,4,3,48,384]{4,3,2,1,0:T(8,128)(2,1)}, u32[]{:S(2)}, u32[]{:S(2)}) collective-permute-start(bf16[4,4,3,48,384]{4,3,2,1,0:T(8,128)(2,1)} %get-tuple-element.137), channel_id=1, source_target_pairs={{0,1},{1,0},{2,3},{3,2},{4,5},{5,4},{6,7},{7,6},{8,9},{9,8},{10,11... | collective-permute-start | bytes 5308424 | tf_op jit(solution)/shard_map/ppermute | solution.py:429
  350.0 23.6 %collective-permute-start.73 = (bf16[4,48,384]{2,1,0:T(8,128)(2,1)}, bf16[4,48,384]{2,1,0:T(8,128)(2,1)S(1)}, u32[]{:S(2)}, u32[]{:S(2)}) collective-permute-start(bf16[4,48,384]{2,1,0:T(8,128)(2,1)} %get-tuple-element.139), channel_id=1, source_target_pairs={{0,4},{4,0},{1,5},{5,1},{2,6},{6,2},{3,7},{7,3},{8,12},{12,8},{9,1... | collective-permute-start | bytes 442376 | tf_op jit(solution)/shard_map/ppermute | solution.py:429
  (112 other events, 1148.0 us)

commit v4 on v3

--- a/solution.py
+++ b/solution.py
@@ -78,31 +78,28 @@
     )
 
 
-def load_pieces(coords, picks, pieces, target, sems, first=0):
+def load_pieces(coords, picks, pieces, layout, target, sems, first=0):
     rows = target.shape[4]
     side, y_here, x_here = coords[0], coords[1], coords[2]
-    squares = target.shape[2] * target.shape[3]
-    per_side = len(pieces) // 2
-    half = pieces[0].shape[2]
+    single = target.shape[2] == 1
+    half = pieces[0].shape[-1]
     copies = []
     for place, pick in enumerate(picks):
         for number, source in enumerate(pieces):
-            which, order = divmod(number, per_side)
+            which, order = divmod(number, len(layout))
+            y_other, x_other, plane, planes = layout[order]
             start = pl.multiple_of((side if which == 0 else 1 - side) * half, half)
-            if squares == 1:
-                planes, y_at, x_at = pl.ds(0, 1), 0, 0
+            y_at = 0 if single else (1 - y_here if y_other else y_here)
+            run = pl.ds(plane, planes)
+            part, columns = pl.ds(pick * rows, rows), pl.ds(start, half)
+            if x_other is None:
+                source = source.at[:, :, part, :]
+                goal = target.at[place, run, y_at, :, :, columns]
             else:
-                y_at = 1 - y_here if order >= 2 else y_here
-                x_at = 1 - x_here if order in (1, 3, 4) else x_here
-                low = pieces[3].shape[0]
-                planes = pl.ds(low if order == 4 else 0, source.shape[0])
-            copies.append(
-                pltpu.make_async_copy(
-                    source.at[:, pl.ds(pick * rows, rows), :],
-                    target.at[place, planes, y_at, x_at, :, pl.ds(start, half)],
-                    sems.at[first + len(copies)],
-                )
-            )
+                x_at = 0 if single else (1 - x_here if x_other else x_here)
+                source = source.at[:, part, :]
+                goal = target.at[place, run, y_at, x_at, :, columns]
+            copies.append(pltpu.make_async_copy(source, goal, sems.at[first + len(copies)]))
     return copies
 
 
@@ -149,14 +146,15 @@
     return jnp.where(mask, value, 0.0).astype(LOW)
 
 
-def attend_kernel(sequence, pieces, earlier, *refs):
+def attend_kernel(sequence, layout, earlier, *refs):
+    pieces = 2 * len(layout)
     lengths, coords, tokens, vec = refs[:4]
     sources = refs[4 : 4 + pieces]
     query_out, key_out, value_out, mixed_out, sum_out, norm_out = refs[
         4 + pieces + earlier : 10 + pieces + earlier
     ]
     weights, value_flip, mixed_flip, sems = refs[10 + pieces + earlier :]
-    copies = load_pieces(coords, range(4), sources, weights, sems)
+    copies = load_pieces(coords, range(4), sources, layout, weights, sems)
     for copy in copies:
         copy.start()
 
@@ -204,7 +202,8 @@
     sum_out[...] = rows.astype(WIDE) + matmul(mixed_low, flat(weights, 3)[...]) + vec[2:3, :]
 
 
-def ffn_kernel(inner_pieces, outer_pieces, *refs):
+def ffn_kernel(inner_layout, outer_layout, *refs):
+    inner_pieces, outer_pieces = 2 * len(inner_layout), 2 * len(outer_layout)
     coords, first_sum, cotangent, vec, bias = refs[:5]
     inner_from = refs[5 : 5 + inner_pieces]
     outer_from = refs[5 + inner_pieces : 5 + inner_pieces + outer_pieces]
@@ -216,9 +215,9 @@
 
     @pl.when(step == 0)
     def _():
-        copies = load_pieces(coords, (0,), inner_from, inner_at, sems) + load_pieces(
-            coords, (0,), outer_from, outer_at, sems, inner_pieces
-        )
+        copies = load_pieces(
+            coords, (0,), inner_from, inner_layout, inner_at, sems
+        ) + load_pieces(coords, (0,), outer_from, outer_layout, outer_at, sems, inner_pieces)
         for copy in copies:
             copy.start()
         vec_grad[...] = jnp.zeros_like(vec_grad)
@@ -282,7 +281,8 @@
         store_pieces(coords, keep_out, send_out, lambda r, c: total[r, c])
 
 
-def back_kernel(inner_pieces, att_pieces, *refs):
+def back_kernel(inner_layout, att_layout, *refs):
+    inner_pieces, att_pieces = 2 * len(inner_layout), 2 * len(att_layout)
     coords, first_sum, second_grad, hidden_low, mixed, vec = refs[:6]
     inner_from = refs[6 : 6 + inner_pieces]
     att_from = refs[6 + inner_pieces : 6 + inner_pieces + att_pieces]
@@ -294,9 +294,9 @@
 
     @pl.when(step == 0)
     def _():
-        copies = load_pieces(coords, (0,), inner_from, inner_at, sems) + load_pieces(
-            coords, (3,), att_from, project_at, sems, inner_pieces
-        )
+        copies = load_pieces(
+            coords, (0,), inner_from, inner_layout, inner_at, sems
+        ) + load_pieces(coords, (3,), att_from, att_layout, project_at, sems, inner_pieces)
         for copy in copies:
             copy.start()
         vec_grad[...] = jnp.zeros_like(vec_grad)
@@ -381,11 +381,12 @@
         store_pieces(coords, keep_out, send_out, lambda r, c: total[r, c], place)
 
 
-def input_kernel(pieces, *refs):
+def input_kernel(layout, *refs):
+    pieces = 2 * len(layout)
     coords, first_grad, query, key, value = refs[:5]
     sources = refs[5 : 5 + pieces]
     grad_out, weights, sems = refs[5 + pieces :]
-    load_now(load_pieces(coords, range(3), sources, weights, sems))
+    load_now(load_pieces(coords, range(3), sources, layout, weights, sems))
     grad = first_grad[...]
     for place, grads in enumerate((query, key, value)):
         grad = grad + times_transpose(grads[...], flat(weights, place)[...])
@@ -441,8 +442,8 @@
     return swap(value, "dp_lo")
 
 
-def together(*arrays):
-    return lax.optimization_barrier(arrays)
+def phase(*values):
+    return lax.optimization_barrier(values)
 
 
 def in_order(mine, theirs, here, axis):
@@ -461,75 +462,77 @@
     return in_order(mine, swap_side(theirs), side, shard.ndim - 2)
 
 
-def gather_planes(value):
-    count = lax.axis_size("dp_hi")
+def swap_planes(value):
+    return [swap(value, "dp_hi", offset) for offset in range(1, lax.axis_size("dp_hi"))]
+
+
+def place_planes(value, others):
     here = lax.axis_index("dp_hi")
-    full = jnp.zeros((count,) + value.shape, value.dtype)
-    for offset in range(count):
-        part = swap(value, "dp_hi", offset) if offset else value
+    full = jnp.zeros((len(others) + 1,) + value.shape, value.dtype)
+    for offset, part in enumerate([value] + others):
         full = lax.dynamic_update_slice_in_dim(full, part[None], here ^ offset, 0)
     return full
 
 
-def gather_diagonal(from_x, from_y, low):
-    parts = [swap_y(from_x[:low])]
-    if low < from_x.shape[0]:
-        parts.append(swap_x(from_y[low:]))
-    return parts
-
-
 def wide_sum(*arrays):
     return functools.reduce(lambda a, b: a + b, [a.astype(WIDE) for a in arrays])
 
 
 class Sum:
-    def __init__(self, keep, send, low):
-        self.keep, self.low, self.planes = keep, low, keep.shape[1]
-        self.recv = swap_side(send)
+    def __init__(self, keep, send):
+        self.keep, self.planes = keep, keep.shape[1]
+        self.lower = slice(0, self.planes // 2)
+        self.upper = slice(self.planes // 2, self.planes)
+        self.send = send
+
+    def core(self):
+        return [swap_side(self.send)]
 
     def part(self, square, planes):
-        return wide_sum(self.keep[square, planes], self.recv[square, planes])
-
-    def first(self):
-        lower, upper = slice(0, self.low), slice(self.low, self.planes)
-        self.lower, self.upper = lower, upper
-        self.split = self.low < self.planes
-        out = [self.part(3, lower), self.part(2, lower)]
-        if self.split:
-            out += [self.part(3, upper), self.part(1, upper)]
-        self.ready = [value.astype(LOW) for value in out]
-        return self.ready
-
-    def second(self, ready):
-        self.diagonal = [swap_y(ready[0])]
-        self.from_y = [swap_y(ready[1])]
-        self.from_x = []
-        if self.split:
-            self.diagonal.append(swap_x(ready[2]))
-            self.from_x.append(swap_x(ready[3]))
-        out = [(self.part(1, self.lower) + self.diagonal[0].astype(WIDE)).astype(LOW)]
-        if self.split:
-            out.append((self.part(2, self.upper) + self.diagonal[1].astype(WIDE)).astype(LOW))
-        return out
-
-    def third(self, ready):
-        self.from_x.insert(0, swap_x(ready[0]))
-        if self.split:
-            self.from_y.append(swap_y(ready[1]))
-        runs = [self.lower] + ([self.upper] if self.split else [])
-        out = [
-            wide_sum(self.part(0, run), from_x, from_y).astype(LOW)
-            for run, from_x, from_y in zip(runs, self.from_x, self.from_y)
+        return wide_sum(self.keep[square, planes], self.other[square, planes])
+
+    def diagonal(self, got):
+        (self.other,) = got
+        lower, upper = self.lower, self.upper
+        return [
+            swap_y(self.part(3, lower).astype(LOW)),
+            swap_x(self.part(3, upper).astype(LOW)),
+            swap_x(self.part(1, upper).astype(LOW)),
+            swap_y(self.part(2, lower).astype(LOW)),
         ]
-        return out[0] if len(out) == 1 else jnp.concatenate(out, axis=0)
-
-    def last(self, ready):
+
+    def near(self, got):
+        by_y, by_x, self.x_upper, self.y_lower = got
+        return [
+            swap_x(wide_sum(self.part(1, self.lower), by_y).astype(LOW)),
+            swap_y(wide_sum(self.part(2, self.upper), by_x).astype(LOW)),
+        ]
+
+    def along(self, got):
+        x_lower, y_upper = got
+        whole_sum = jnp.concatenate(
+            [
+                wide_sum(self.part(0, self.lower), x_lower, self.y_lower).astype(LOW),
+                wide_sum(self.part(0, self.upper), self.x_upper, y_upper).astype(LOW),
+            ],
+            axis=0,
+        )
         here = lax.axis_index("dp_hi")
-        total = lax.dynamic_index_in_dim(ready, here, 0, keepdims=False).astype(WIDE)
-        for offset in range(1, self.planes):
-            sent = lax.dynamic_index_in_dim(ready, here ^ offset, 0, keepdims=False)
-            total = total + swap(sent, "dp_hi", offset).astype(WIDE)
-        return total
+        pick = functools.partial(lax.dynamic_index_in_dim, whole_sum, axis=0, keepdims=False)
+        self.own = pick(here)
+        return [
+            swap(pick(here ^ offset), "dp_hi", offset) for offset in range(1, self.planes)
+        ]
+
+    def pair(self, got, side):
+        total = wide_sum(self.own, *got).astype(LOW)
+        rows = total.shape[-2] // 2
+        axis = total.ndim - 2
+        self.rows = lax.dynamic_slice_in_dim(total, side * rows, rows, axis)
+        return [swap_side(lax.dynamic_slice_in_dim(total, (1 - side) * rows, rows, axis))]
+
+    def done(self, got, side):
+        return in_order(self.rows, got[0], side, self.rows.ndim - 1).astype(WIDE)
 
 
 def own_rows(total, side):
@@ -541,52 +544,53 @@
     return in_order(mine, swap_side(theirs), side, total.ndim - 1).astype(WIDE)
 
 
-def bit_of(bit):
-    return (lax.axis_index(ALL) >> bit) & 1
-
-
-def halve(partial, bit, axis, count):
-    mine = bit_of(bit)
-    sent = lax.dynamic_index_in_dim(partial, 1 - mine, axis, keepdims=False)
-    kept = lax.dynamic_index_in_dim(partial, mine, axis, keepdims=False)
-    return kept + lax.ppermute(sent, ALL, [(i, i ^ (1 << bit)) for i in range(count)])
-
-
-def reduce_small(partial, count):
-    bits = count.bit_length() - 1
-    partial = partial.reshape((2,) * bits + partial.shape[1:])
-    for bit in range(bits):
-        partial = halve(partial, bit, bits - 1 - bit, count)
-    return partial
-
-
-def to_sequences(value, parts):
-    seqs, here, width = value.shape
-    own = seqs // parts
+def swap_square(value):
+    diagonal = [((y, x), (1 - y, 1 - x)) for y in range(2) for x in range(2)]
+    index = lambda place: place[0] * 2 + place[1]
+    return [
+        swap_x(value),
+        swap_y(value),
+        lax.ppermute(value, ("dp_lo", "ctx_hi"), [(index(a), index(b)) for a, b in diagonal]),
+    ]
+
+
+def swap_sequences(value, parts):
+    own = value.shape[0] // parts
     me = lax.axis_index(CONTEXT)
-    full = jnp.zeros((own, parts * here, width), value.dtype)
-    for offset in range(parts):
-        peer = me ^ offset
-        part = lax.dynamic_slice_in_dim(value, peer * own, own, 0)
-        if offset:
-            part = swap(part, CONTEXT, offset)
-        full = lax.dynamic_update_slice_in_dim(full, part, peer * here, 1)
+    blocks = [
+        lax.dynamic_slice_in_dim(value, (me ^ offset) * own, own, 0) for offset in range(parts)
+    ]
+    return blocks[:1] + [swap(blocks[i], CONTEXT, i) for i in range(1, parts)]
+
+
+def place_sequences(blocks):
+    own, here, width = blocks[0].shape
+    me = lax.axis_index(CONTEXT)
+    full = jnp.zeros((own, len(blocks) * here, width), blocks[0].dtype)
+    for offset, part in enumerate(blocks):
+        full = lax.dynamic_update_slice_in_dim(full, part, (me ^ offset) * here, 1)
     return full
 
 
-def to_positions(values, parts):
-    own = len(values)
-    length, width = values[0].shape
-    here = length // parts
+def swap_positions(value, parts):
+    here = value.shape[0] // parts
     me = lax.axis_index(CONTEXT)
-    full = jnp.zeros((own * parts, here, width), values[0].dtype)
-    for number, value in enumerate(values):
-        for offset in range(parts):
-            peer = me ^ offset
-            part = lax.dynamic_slice_in_dim(value, peer * here, here, 0)
-            if offset:
-                part = swap(part, CONTEXT, offset)
-            full = lax.dynamic_update_slice(full, part[None], (peer * own + number, 0, 0))
+    blocks = [
+        lax.dynamic_slice_in_dim(value, (me ^ offset) * here, here, 0) for offset in range(parts)
+    ]
+    return blocks[:1] + [swap(blocks[i], CONTEXT, i) for i in range(1, parts)]
+
+
+def place_positions(sequences):
+    own, parts = len(sequences), len(sequences[0])
+    here, width = sequences[0][0].shape
+    me = lax.axis_index(CONTEXT)
+    full = jnp.zeros((own * parts, here, width), sequences[0][0].dtype)
+    for number, blocks in enumerate(sequences):
+        for offset, part in enumerate(blocks):
+            full = lax.dynamic_update_slice(
+                full, part[None], ((me ^ offset) * own + number, 0, 0)
+            )
     return full
 
 
@@ -642,58 +646,77 @@
         dims, squares = (1, 1, 1), 1
         att_block, inner_block, outer_block = width, width, hidden
 
-    small = jnp.concatenate([vectors.reshape(-1), inner_bias]).astype(LOW)
-    small_size = small.shape[0]
-    small = jnp.pad(small.reshape(1, -1), ((0, tall - 1), (0, half - small_size)))
-    small_row = 8 * att_rows
-    token_rows = to_sequences(tokens, parts).reshape(rows, width)
-    att_pair = pair_shards(attention_weights.astype(LOW), side).reshape(small_row, half)
-    att_pair = jnp.concatenate([att_pair, small], axis=0)
+    me = lax.axis_index(ALL)
+    per_row = width // bias_cols
+    small = jnp.zeros((tall, width), LOW)
+    small = lax.dynamic_update_slice(small, vectors.astype(LOW), (0, me * vec_cols))
+    small = lax.dynamic_update_slice(
+        small, inner_bias.astype(LOW)[None], (8 + me // per_row, me % per_row * bias_cols)
+    )
+    token_blocks = swap_sequences(tokens, parts)
+    att_pair = pair_shards(attention_weights.astype(LOW), side).reshape(8 * att_rows, half)
     inner_pair = pair_shards(inner_weights.astype(LOW), side)
     outer_pair = pair_shards(outer_weights.astype(LOW), side)
+    cot_low = cotangent.astype(LOW)
     if in_pieces:
-        att = gather_planes(att_pair)
-        inner = gather_planes(inner_pair)
-        outer = gather_planes(outer_pair)
+        middle = planes // 2
+        small_part = swap_side(small)
+        att_pair, inner_pair, outer_pair, small_part = phase(
+            att_pair, inner_pair, outer_pair, small_part
+        )
+        small = small + small_part
+        att_parts, inner_parts = swap_planes(att_pair), swap_planes(inner_pair)
+        outer_x = swap_x(outer_pair)
+        small_parts = swap_planes(small)
+        att_parts, inner_parts, outer_x, small_parts, token_blocks = phase(
+            att_parts, inner_parts, outer_x, small_parts, token_blocks
+        )
+        small = wide_sum(small, *small_parts).astype(LOW)
+        att, inner = place_planes(att_pair, att_parts), place_planes(inner_pair, inner_parts)
+        outer_row = in_order(outer_pair[None], outer_x[None], coords[2], 0)
         att_x, att_y = swap_x(att), swap_y(att)
-        att_x, att_y, token_rows = together(att_x, att_y, token_rows)
-        att_mine = [att, att_x, att_y] + gather_diagonal(att_x, att_y, planes // 2)
-        att_all = att_mine + [swap_side(piece) for piece in att_mine]
-        token_rows, inner, outer = together(token_rows, inner, outer)
         inner_x, inner_y = swap_x(inner), swap_y(inner)
-        outer_x, outer_y = swap_x(outer), swap_y(outer)
-
-        def small_of(pieces):
-            own, from_x, from_y = [
-                piece[:, None, None, small_row, :small_size] for piece in pieces[:3]
-            ]
-            diagonal = jnp.concatenate(
-                [piece[:, None, None, small_row, :small_size] for piece in pieces[3:]], axis=0
-            )
-            x_here, y_here = coords[2], coords[1]
-            return in_order(
-                in_order(own, from_x, x_here, 2), in_order(from_y, diagonal, x_here, 2), y_here, 1
-            ).reshape(chips, 1, small_size)
-
-        small_all = in_order(
-            small_of(att_mine), small_of(att_all[len(att_mine) :]), side, 1
-        )
+        outer_parts = swap_planes(outer_row)
+        small_parts = swap_square(small)
+        token_rows = place_sequences(token_blocks)
+        att_x, att_y, inner_x, inner_y, outer_parts, small_parts, token_rows = phase(
+            att_x, att_y, inner_x, inner_y, outer_parts, small_parts, token_rows
+        )
+        small = wide_sum(small, *small_parts)
+        outer = place_planes(outer_row, outer_parts)
+        att_mine = [att, att_x, att_y, swap_y(att_x[:middle]), swap_x(att_y[middle:])]
+        att_other = [swap_side(piece) for piece in att_mine[:3]]
+        att_mine, att_other, small, outer = phase(att_mine, att_other, small, outer)
+        att_all = att_mine + att_other + [swap_side(piece) for piece in att_mine[3:]]
+        att_layout = [
+            (0, 0, 0, planes),
+            (0, 1, 0, planes),
+            (1, 0, 0, planes),
+            (1, 1, 0, middle),
+            (1, 1, middle, planes - middle),
+        ]
+        inner_layout = [(y, x, 0, planes) for y in range(2) for x in range(2)]
+        outer_layout = [
+            (0, None, 0, planes),
+            (1, None, 0, middle),
+            (1, None, middle, planes - middle),
+        ]
     else:
+        small = lax.psum(small, ALL).astype(WIDE)
         att = lax.all_gather(att_pair, CHIPS, axis=0, tiled=False)
         inner = lax.all_gather(inner_pair, CHIPS, axis=0, tiled=True)[None]
         outer = lax.all_gather(outer_pair, CHIPS, axis=0, tiled=True)[None]
-        small_mine = att[:, None, small_row, :small_size]
-        small_all = in_order(small_mine, swap_side(small_mine), side, 1)
-        att = att[:, :small_row].reshape(chips, 4, 2 * att_rows, half)
+        att = att.reshape(chips, 4, 2 * att_rows, half)
         att = att.transpose(1, 0, 2, 3).reshape(1, 4 * width, half)
         att_all, inner_all, outer_all = [
             [value, swap_side(value)] for value in (att, inner, outer)
         ]
-    small_all = small_all.reshape(count, small_size).astype(WIDE)
-    vec = (
-        small_all[:, : 8 * vec_cols].reshape(count, 8, vec_cols).transpose(1, 0, 2).reshape(8, -1)
-    )
-    bias = small_all[:, 8 * vec_cols :].reshape(1, -1)
+        att_layout = inner_layout = outer_layout = [(0, 0, 0, 1)]
+        token_rows = place_sequences(token_blocks)
+        cot_blocks = swap_sequences(cot_low, parts)
+    token_rows = token_rows.reshape(rows, width)
+    vec = small[:8]
+    bias = small[8 : 8 + hidden // width].reshape(1, hidden)
     own_lengths = lax.dynamic_slice_in_dim(lengths, lax.axis_index(CONTEXT) * own_seqs, own_seqs)
 
     def in_place(pieces):
@@ -715,7 +738,7 @@
             (vec, vec_spec),
         ] + in_place(att_all)
         held = call(
-            functools.partial(attend_kernel, number, len(att_all), len(held)),
+            functools.partial(attend_kernel, number, att_layout, len(held)),
             1,
             inputs + in_place(held),
             [(low_rows, LOW, own_rows_spec)] * 4
@@ -733,16 +756,35 @@
             20 * rows * width // own_seqs,
             {len(inputs) + i: i for i in range(len(held))},
         )
-        if in_pieces and number == 0:
-            *held, inner_x, inner_y, outer_x, outer_y = together(
-                *held, inner_x, inner_y, outer_x, outer_y
+        if not in_pieces:
+            continue
+        if number == 0:
+            inner_far = swap_x(inner_y)
+            outer_low = swap_y(outer[:middle])
+            inner_other = [swap_side(piece) for piece in (inner, inner_x, inner_y)]
+            outer_other = swap_side(outer)
+            held, inner_far, outer_low, inner_other, outer_other = phase(
+                held, inner_far, outer_low, inner_other, outer_other
             )
-            inner_all = [inner, inner_x, inner_y] + gather_diagonal(inner_x, inner_y, planes)
-            outer_all = [outer, outer_x, outer_y] + gather_diagonal(outer_x, outer_y, planes)
-            inner_all = inner_all + [swap_side(piece) for piece in inner_all]
-            outer_all = outer_all + [swap_side(piece) for piece in outer_all]
+        if number == min(1, own_seqs - 1):
+            outer_high = swap_y(outer[middle:])
+            cot_blocks = swap_sequences(cot_low, parts)
+            inner_all = [inner, inner_x, inner_y, inner_far] + inner_other
+            inner_all = inner_all + [swap_side(inner_far)]
+            outer_low_other = swap_side(outer_low)
+            held, outer_high, cot_blocks, inner_all, outer_low_other = phase(
+                held, outer_high, cot_blocks, inner_all, outer_low_other
+            )
+            outer_all = [
+                outer,
+                outer_low,
+                outer_high,
+                outer_other,
+                outer_low_other,
+                swap_side(outer_high),
+            ]
     query, key, value, mixed, first_sum, normalizer = held
-    cot_rows = to_sequences(cotangent.astype(LOW), parts).reshape(rows, width)
+    cot_rows = place_sequences(cot_blocks).reshape(rows, width)
 
     def grad_pieces(rows_here, columns, matrices=None):
         lead = (squares, dims[0]) + ((matrices,) if matrices else ())
@@ -752,39 +794,41 @@
     tile = 256
     row_tile = tiles(tile, width)
     hidden_tile = tiles(tile, hidden)
-    result, second_grad, hidden_low, outer_keep, outer_send, vec_ffn, bias_grad = call(
-        functools.partial(ffn_kernel, len(inner_all), len(outer_all)),
-        rows // tile,
-        [
-            (coords, SCALARS),
-            (first_sum, row_tile),
-            (cot_rows, row_tile),
-            (vec, vec_spec),
-            (bias, whole(1, hidden)),
-        ]
-        + in_place(inner_all)
-        + in_place(outer_all),
-        [
-            (low_rows, LOW, row_tile),
-            (low_rows, WIDE, row_tile),
-            ((rows, hidden), LOW, hidden_tile),
-        ]
-        + grad_pieces(outer_block, half)
-        + [((8, width), WIDE, vec_spec), ((1, hidden), WIDE, whole(1, hidden))],
-        [
-            pltpu.VMEM((1,) + dims + (inner_block, hidden), LOW),
-            pltpu.VMEM((1,) + dims + (outer_block, width), LOW),
-            pltpu.VMEM((hidden, width), WIDE),
-            pltpu.VMEM((tile, hidden), LOW),
-            pltpu.VMEM((tile, hidden), WIDE),
-            pltpu.SemaphoreType.DMA((len(inner_all) + len(outer_all),)),
-        ],
-        16 * square + 60 * rows * hidden,
-        30 * rows * width,
-    )
-    output_tokens = to_positions(list(result.reshape(own_seqs, full_len, width)), parts)
-
-    inner_keep, inner_send = call(
+    result, second_grad, hidden_low, outer_keep, outer_send, vec_ffn, bias_grad = phase(
+        *call(
+            functools.partial(ffn_kernel, inner_layout, outer_layout),
+            rows // tile,
+            [
+                (coords, SCALARS),
+                (first_sum, row_tile),
+                (cot_rows, row_tile),
+                (vec, vec_spec),
+                (bias, whole(1, hidden)),
+            ]
+            + in_place(inner_all)
+            + in_place(outer_all),
+            [
+                (low_rows, LOW, row_tile),
+                (low_rows, WIDE, row_tile),
+                ((rows, hidden), LOW, hidden_tile),
+            ]
+            + grad_pieces(outer_block, half)
+            + [((8, width), WIDE, vec_spec), ((1, hidden), WIDE, whole(1, hidden))],
+            [
+                pltpu.VMEM((1,) + dims + (inner_block, hidden), LOW),
+                pltpu.VMEM((1,) + dims + (outer_block, width), LOW),
+                pltpu.VMEM((hidden, width), WIDE),
+                pltpu.VMEM((tile, hidden), LOW),
+                pltpu.VMEM((tile, hidden), WIDE),
+                pltpu.SemaphoreType.DMA((len(inner_all) + len(outer_all),)),
+            ],
+            16 * square + 60 * rows * hidden,
+            30 * rows * width,
+        )
+    )
+    results = result.reshape(own_seqs, full_len, width)
+
+    inner_grads = call(
         inner_grad_kernel,
         rows // tile,
         [
@@ -798,13 +842,17 @@
         4 * square,
         18 * rows * width,
     )
+    result_blocks = [swap_positions(results[0], parts)]
     if in_pieces:
-        outer_sum = Sum(outer_keep, outer_send, planes)
-        outer_ready = outer_sum.first()
-        *outer_ready, second_grad, inner_send = together(*outer_ready, second_grad, inner_send)
+        outer_sum = Sum(outer_keep, outer_send)
+        inner_grads, outer_got, result_blocks, second_grad = phase(
+            inner_grads, outer_sum.core(), result_blocks, second_grad
+        )
+        inner_sum = Sum(*inner_grads)
+        outer_got, inner_got = outer_sum.diagonal(outer_got), inner_sum.core()
 
     first_grad, mixed_grad, project_keep, project_send, vec_mid = call(
-        functools.partial(back_kernel, len(inner_all), len(att_all)),
+        functools.partial(back_kernel, inner_layout, att_layout),
         rows // tile,
         [
             (coords, SCALARS),
@@ -829,18 +877,27 @@
         24 * rows * width,
     )
     if in_pieces:
-        outer_ready = outer_sum.second(outer_ready)
-        inner_sum = Sum(inner_keep, inner_send, planes)
-        inner_ready = inner_sum.first()
-        mixed_grad, *ready = together(mixed_grad, *outer_ready, *inner_ready)
-        outer_ready, inner_ready = ready[: len(outer_ready)], ready[len(outer_ready) :]
+        (
+            first_grad,
+            mixed_grad,
+            project_keep,
+            project_send,
+            vec_mid,
+            outer_got,
+            inner_got,
+        ) = phase(
+            first_grad, mixed_grad, project_keep, project_send, vec_mid, outer_got, inner_got
+        )
+        project_sum = Sum(project_keep, project_send)
+        outer_got, inner_got = outer_sum.near(outer_got), inner_sum.diagonal(inner_got)
+        project_got = project_sum.core()
 
     grads = []
     for number in range(own_seqs):
         last = number == own_seqs - 1
         own_rows_spec = block(number, full_len, width)
         seq_shape = (full_len, width)
-        earlier = [value for three in grads for value in three] if last else []
+        earlier = [value_ for three in grads for value_ in three] if last else []
         outputs = [(seq_shape, LOW, whole(*seq_shape))] * 3
         scratch = [pltpu.VMEM((width, full_len), LOW), pltpu.VMEM((width, full_len), WIDE)]
         if last:
@@ -848,7 +905,7 @@
                 outputs + grad_pieces(att_block, half, 3) + [((8, width), WIDE, vec_spec)]
             )
             scratch = scratch + [pltpu.VMEM((width, width), WIDE)]
-        three = call(
+        found = call(
             functools.partial(attend_back_kernel, number, last),
             1,
             [
@@ -867,61 +924,39 @@
             5 * attend_flops // own_seqs + (3 * square if last else 0),
             20 * rows * width // own_seqs,
         )
-        grads.append(list(three[:3]))
-        if in_pieces and number == 0:
-            outer_ready = outer_sum.third(outer_ready)
-            inner_ready = inner_sum.second(inner_ready)
-            project_sum = Sum(project_keep, project_send, planes)
-            project_ready = project_sum.first()
-            mixed_grad, grads[0][0], outer_ready, *ready = together(
-                mixed_grad, grads[0][0], outer_ready, *inner_ready, *project_ready
+        if number:
+            result_blocks.append(swap_positions(results[number], parts))
+        if in_pieces:
+            found, outer_got, inner_got, project_got, mixed_grad, result_blocks = phase(
+                found, outer_got, inner_got, project_got, mixed_grad, result_blocks
             )
-            inner_ready, project_ready = ready[: len(inner_ready)], ready[len(inner_ready) :]
-    att_keep, att_send, vec_att = three[3:]
-
-    if in_pieces:
-        att_sum = Sum(att_keep, att_send, planes // 2)
-        att_total = att_sum.last(att_sum.third(att_sum.second(att_sum.first())))
-        outer_total = outer_sum.last(outer_ready)
-        inner_total = inner_sum.last(inner_sum.third(inner_ready))
-        project_total = project_sum.last(project_sum.third(project_sum.second(project_ready)))
-    else:
-
-        def scatter(keep, send):
-            partial = (keep + swap_side(send)).reshape((-1,) + keep.shape[-2:])
-            matrices, length, columns = partial.shape
-            partial = partial.reshape(matrices, chips, length // chips, columns)
-            return lax.psum_scatter(
-                partial.transpose(1, 0, 2, 3), CHIPS, scatter_dimension=0, tiled=False
-            )
-
-        att_total = scatter(att_keep, att_send)
-        outer_total = scatter(outer_keep, outer_send)[0]
-        inner_total = scatter(inner_keep, inner_send)[0]
-        project_total = scatter(project_keep, project_send)[0]
-    attention_total = jnp.concatenate(
-        [own_rows(att_total, side), own_rows(project_total, side)[None]], axis=0
-    )
-    inner_total = own_rows(inner_total, side)
-    outer_total = own_rows(outer_total, side)
-
-    vector_grad = vec_ffn + vec_mid + vec_att
+            if number == 0:
+                outer_got, inner_got = outer_sum.along(outer_got), inner_sum.near(inner_got)
+                project_got = project_sum.diagonal(project_got)
+        grads.append(list(found[:3]))
+    att_keep, att_send, vec_att = found[3:]
+    output_tokens = place_positions(result_blocks)
+
     small_grad = jnp.concatenate(
         [
-            vector_grad.reshape(8, count, vec_cols).transpose(1, 0, 2).reshape(count, -1),
-            bias_grad.reshape(count, bias_cols),
+            vec_ffn + vec_mid + vec_att,
+            bias_grad.reshape(-1, width),
+            jnp.zeros((tall - 8 - hidden // width, width), WIDE),
         ],
-        axis=1,
-    )
-    small_total = reduce_small(small_grad, count)
-    vector_total = small_total[: 8 * vec_cols].reshape(8, vec_cols)
-    bias_total = small_total[8 * vec_cols :]
-
-    input_grads = []
+        axis=0,
+    )
+    if in_pieces:
+        att_sum = Sum(att_keep, att_send)
+        att_got = att_sum.core()
+        outer_got, inner_got = outer_sum.pair(outer_got, side), inner_sum.along(inner_got)
+        project_got = project_sum.near(project_got)
+        small_got = [swap_side(small_grad)]
+
+    input_blocks = []
     for number in range(own_seqs):
         seq_shape = (full_len, width)
         (grad,) = call(
-            functools.partial(input_kernel, len(att_all)),
+            functools.partial(input_kernel, att_layout),
             1,
             [(coords, SCALARS), (first_grad, block(number, full_len, width))]
             + [(value_, whole(*seq_shape)) for value_ in grads[number]]
@@ -934,8 +969,51 @@
             3 * square // own_seqs,
             12 * rows * width // own_seqs,
         )
-        input_grads.append(grad)
-    input_grad = to_positions(input_grads, parts).astype(WIDE)
+        if in_pieces and number == 0:
+            grad, first_grad, att_got, outer_got, inner_got, project_got, small_got = phase(
+                grad, first_grad, att_got, outer_got, inner_got, project_got, small_got
+            )
+            outer_total = outer_sum.done(outer_got, side)
+            small_grad = wide_sum(small_grad, *small_got)
+            att_got, inner_got = att_sum.diagonal(att_got), inner_sum.pair(inner_got, side)
+            project_got, small_got = project_sum.along(project_got), swap_planes(small_grad)
+        input_blocks.append(swap_positions(grad, parts))
+    if in_pieces:
+        input_blocks[:-1], att_got, inner_got, project_got, small_got, input_blocks[-1][0] = (
+            phase(
+                input_blocks[:-1], att_got, inner_got, project_got, small_got, input_blocks[-1][0]
+            )
+        )
+        inner_total = inner_sum.done(inner_got, side)
+        small_grad = wide_sum(small_grad, *small_got)
+        att_got, small_got = att_sum.near(att_got), swap_square(small_grad)
+        project_got = project_sum.pair(project_got, side)
+        att_got, small_got, project_got = phase(att_got, small_got, project_got)
+        small_total = wide_sum(small_grad, *small_got)
+        project_total = project_sum.done(project_got, side)
+        att_total = att_sum.done(att_sum.pair(att_sum.along(att_got), side), side)
+    else:
+
+        def scatter(keep, send):
+            partial = (keep + swap_side(send)).reshape((-1,) + keep.shape[-2:])
+            matrices, length, columns = partial.shape
+            partial = partial.reshape(matrices, chips, length // chips, columns)
+            partial = lax.psum_scatter(
+                partial.transpose(1, 0, 2, 3), CHIPS, scatter_dimension=0, tiled=False
+            )
+            return own_rows(partial, side)
+
+        att_total = scatter(att_keep, att_send)
+        outer_total = scatter(outer_keep, outer_send)[0]
+        inner_total = scatter(*inner_grads)[0]
+        project_total = scatter(project_keep, project_send)[0]
+        small_total = lax.psum(small_grad, ALL)
+    attention_total = jnp.concatenate([att_total, project_total[None]], axis=0)
+    vector_total = lax.dynamic_slice(small_total, (0, me * vec_cols), (8, vec_cols))
+    bias_total = lax.dynamic_slice(
+        small_total, (8 + me // per_row, me % per_row * bias_cols), (1, bias_cols)
+    ).reshape(bias_cols)
+    input_grad = place_positions(input_blocks).astype(WIDE)
 
     attention_square, attention_new = adam_step(
         attention_weights,

time: 445 us -> 411 us (0.924)
  waiting for transfers between devices: 120 us -> 87.4 us
  starting transfers between devices: 83 us -> 105 us
  local copies, waits for them, and re-layouts: 44.4 us -> 23.6 us
  other arithmetic: 38.1 us -> 33.5 us
    ppermute x88 -> x108, waiting for transfers between devices: 113 us -> 87.4 us  [swap(): return lax.ppermute(value, axis, [(i, i ^ offset) for i in range(size)])]
    ppermute x88 -> x108, starting transfers between devices: 78.2 us -> 104 us  [swap(): return lax.ppermute(value, axis, [(i, i ^ offset) for i in range(size)])]
    dynamic_update_slice x31 -> x37, local copies, waits for them, and re-layouts: 14.6 us -> 7.82 us  [the longest x16 6.79 us: place_positions(): lax.dynamic_update_slice(full, part[None], ((me ^ offset) * own + number,...]
    ppermute x5 -> x2, waiting for transfers between devices: 6.24 us -> 0.01 us  [swap_square(): lax.ppermute(value, ('dp_lo', 'ctx_hi'), [(index(a), index(b)) for a, b i...]
  transfers between devices with their start and end apart: 93 -> 110, of which waited for: 32 -> 29; matrix products, arithmetic and copies ran while one was open for 17% -> 12% of each run, Pallas kernels for 27% -> 29%
where the time goes in v4:
time: 411 us; the launch traced here: 403 us
  Pallas kernels  151 us (37%)
  starting transfers between devices  105 us (26%)
  waiting for transfers between devices  87.4 us (21%)
  other arithmetic  33.5 us (8%)
  local copies, waits for them, and re-layouts  23.6 us (6%)
    pallas_call x9, Pallas kernels, call(): pl.pallas_call(kernel, grid=(grid,), in_specs=[spec for _, spec in inputs...  151 us
    ppermute x108, starting transfers between devices, swap(): return lax.ppermute(value, axis, [(i, i ^ offset) for i in range(size)])  104 us
    ppermute x108, waiting for transfers between devices, swap(): return lax.ppermute(value, axis, [(i, i ^ offset) for i in range(size)])  87.4 us
  transfers between devices with their start and end apart: 110, of which 29 were waited for; matrix products, arithmetic and copies ran while one was open for 12% of the time, Pallas kernels for 29%

profile of v4, /device:TPU:0, one launch (start us, length us, event | category | flops | bytes accessed | tf_op | source)
XLA Modules:
  0.0 403.3 jit_solution(6791617737129444812)
XLA Ops:
  7.7 2.7 collective-permute-start.11
  10.3 2.6 collective-permute-start.12
  13.8 3.5 collective-permute-start.5
  24.6 5.4 %collective-permute-done.6 = bf16[192,384]{1,0:T(8,128)(2,1)S(1)} collective-permute-done((bf16[192,384]{1,0:T(8,128)(2,1)S(1)}, bf16[192,384]{1,0:T(8,128)(2,1)S(1)}, u32[]{:S(2)}, u32[]{:S(2)}) %collective-permute-start.6) | collective-permute-done | bytes 147488 | tf_op jit(solution)/shard_map/ppermute | solution.py:430
  30.0 3.6 collective-permute-done.7
  35.8 7.9 %collective-permute-done.8 = bf16[48,1536]{1,0:T(8,128)(2,1)S(1)} collective-permute-done((bf16[48,1536]{1,0:T(8,128)(2,1)S(1)}, bf16[48,1536]{1,0:T(8,128)(2,1)S(1)}, u32[]{:S(2)}, u32[]{:S(2)}) %collective-permute-start.8) | collective-permute-done | bytes 147488 | tf_op jit(solution)/shard_map/ppermute | solution.py:430
  47.3 3.8 collective-permute-start.21
  54.9 7.8 %collective-permute-done.21 = bf16[2,192,384]{2,1,0:T(8,128)(2,1)S(1)} collective-permute-done((bf16[2,192,384]{2,1,0:T(8,128)(2,1)S(1)}, bf16[2,192,384]{2,1,0:T(8,128)(2,1)S(1)}, u32[]{:S(2)}, u32[]{:S(2)}) %collective-permute-start.21) | collective-permute-done | bytes 294944 | tf_op jit(solution)/shard_map/ppermute | solution.py:430
  68.0 7.2 %collective-permute-done.23 = bf16[2,192,384]{2,1,0:T(8,128)(2,1)S(1)} collective-permute-done((bf16[2,192,384]{2,1,0:T(8,128)(2,1)S(1)}, bf16[2,192,384]{2,1,0:T(8,128)(2,1)S(1)}, u32[]{:S(2)}, u32[]{:S(2)}) %collective-permute-start.23) | collective-permute-done | bytes 294944 | tf_op jit(solution)/shard_map/ppermute | solution.py:430
  75.2 3.1 collective-permute-done.17.refs_5_.refs_15_.refs_6_
  82.4 5.9 %collective-permute-done.27.refs_7_.refs_17_.refs_8_ = bf16[2,192,384]{2,1,0:T(8,128)(2,1)S(1)} collective-permute-done((bf16[2,192,384]{2,1,0:T(8,128)(2,1)S(1)}, bf16[2,192,384]{2,1,0:T(8,128)(2,1)S(1)}, u32[]{:S(2)}, u32[]{:S(2)}) %collective-permute-start.27) | collective-permute-done | bytes 294944 | tf_op jit(solution)/shard_map/ppermute | solution.py:430
  93.8 9.4 %collective-permute-done.34.refs_8_.refs_9_ = bf16[4,48,1536]{2,1,0:T(8,128)(2,1)S(1)} collective-permute-done((bf16[4,48,1536]{2,1,0:T(8,128)(2,1)}, bf16[4,48,1536]{2,1,0:T(8,128)(2,1)S(1)}, u32[]{:S(2)}, u32[]{:S(2)}) %collective-permute-start.34) | collective-permute-done | bytes 589856 | tf_op jit(solution)/shard_map/ppermute | solution.py:430
  107.2 16.0 %shard_map.305 = (bf16[1024,768]{1,0:T(8,128)(2,1)}, bf16[1024,768]{1,0:T(8,128)(2,1)}, bf16[1024,768]{1,0:T(8,128)(2,1)}, bf16[1024,768]{1,0:T(8,128)(2,1)}, f3...) custom-call(s32[2]{0:T(128)} %dynamic_slice.175.refs_0_, s32[3]{0:T(128)} %pad_add_fusion.refs_1_.refs_0_.coords, ...), custom_call_target="tpu_custom_call" | custom-call | flops 5637144576 | bytes 7864320 | tf_op jit(solution)/shard_map/pallas_call | solution.py:397
  125.4 15.7 %shard_map.306 = (bf16[1024,768]{1,0:T(8,128)(2,1)}, bf16[1024,768]{1,0:T(8,128)(2,1)}, bf16[1024,768]{1,0:T(8,128)(2,1)}, bf16[1024,768]{1,0:T(8,128)(2,1)}, f3...) custom-call(s32[2]{0:T(128)} %dynamic_slice.175.refs_0_, ...), custom_call_target="tpu_custom_call", output_to_operand_aliasing={{0}: (14, {}), {1}: (15, {}), {2}: (16, {}), {3}: (17, {}),... | custom-call | flops 5637144576 | bytes 7864320 | tf_op jit(solution)/shard_map/pallas_call | solution.py:397
  146.2 34.1 %shard_map.307 = (bf16[1024,768]{1,0:T(8,128)(2,1)}, f32[1024,768]{1,0:T(8,128)}, bf16[1024,3072]{1,0:T(8,128)(2,1)}, bf16[4,4,192,384]{3,2,1,0:T(8,128)(2,1)}, ...) custom-call(s32[3]{0:T(128)} %pad_add_fusion.refs_1_.refs_0_.coords, ...), custom_call_target="tpu_custom_call" | custom-call | flops 19516096512 | bytes 23592960 | tf_op jit(solution)/shard_map/pallas_call | solution.py:397
  183.9 11.9 %shard_map.308 = (bf16[4,4,48,1536]{3,2,1,0:T(8,128)(2,1)}, bf16[4,4,48,1536]{3,2,1,0:T(8,128)(2,1)}) custom-call(s32[3]{0:T(128)} %pad_add_fusion.refs_1_.refs_0_.coords, f32[1024,768]{1,0:T(8,128)} %get-tuple-element.276.refs_1_.first_sum, bf16[1024,3072]{1,0:T(8,128)(2,1)} %get-tuple-element.292.hidden_low.refs_3_, f32[8,768]{1,0:T(8,128)} %slice.220.refs_3_.vec.refs_5_), custom_call_target="tpu_custom_call" | custom-call | flops 4831838208 | bytes 14155776 | tf_op jit(solution)/shard_map/pallas_call | solution.py:397
  196.8 2.4 fusion.24
  203.2 20.0 %shard_map.309 = (f32[1024,768]{1,0:T(8,128)}, bf16[1024,768]{1,0:T(8,128)(2,1)}, bf16[4,4,48,384]{3,2,1,0:T(8,128)(2,1)}, bf16[4,4,48,384]{3,2,1,0:T(8,128)(2,1)}, f32[8,768]{1,0:T(8,128)}) custom-call(s32[3]{0:T(128)} %pad_add_fusion.refs_1_.refs_0_.coords, f32[1024,768]{1,0:T(8,128)} %get-tuple-element.276.refs_1_.first_sum, ...), custom_call_target="tpu_custom_call" | custom-call | flops 7247757312 | bytes 18874368 | tf_op jit(solution)/shard_map/pallas_call | solution.py:397
  223.3 2.5 fusion.28
  232.0 2.4 fusion.10
  235.5 2.3 collective-permute-start.57
  237.8 16.1 %shard_map.310 = (bf16[512,768]{1,0:T(8,128)(2,1)}, bf16[512,768]{1,0:T(8,128)(2,1)}, bf16[512,768]{1,0:T(8,128)(2,1)}) custom-call(s32[2]{0:T(128)} %dynamic_slice.175.refs_0_, s32[3]{0:T(128)} %pad_add_fusion.refs_1_.refs_0_.coords, bf16[1024,768]{1,0:T(8,128)(2,1)} %bitcast.234, bf16[1024,768]{1,0:T(8,128)(2,1)} %get-tuple-element.273.refs_3_, ...), custom_call_target="tpu_custom_call" | custom-call | flops 8053063680 | bytes 7864320 | tf_op jit(solution)/shard_map/pallas_call | solution.py:397
  261.2 22.2 %shard_map.311 = (bf16[512,768]{1,0:T(8,128)(2,1)}, bf16[512,768]{1,0:T(8,128)(2,1)}, bf16[512,768]{1,0:T(8,128)(2,1)}, bf16[4,4,3,48,384]{4,3,2,1,0:T(8,128)(2,...) custom-call(s32[2]{0:T(128)} %dynamic_slice.175.refs_0_, s32[3]{0:T(128)} %pad_add_fusion.refs_1_.refs_0_.coords, ...), custom_call_target="tpu_custom_call" | custom-call | flops 11676942336 | bytes 7864320 | tf_op jit(solution)/shard_map/pallas_call | solution.py:397
  297.4 7.4 %shard_map.312 = bf16[512,768]{1,0:T(8,128)(2,1)} custom-call(s32[3]{0:T(128)} %pad_add_fusion.refs_1_.refs_0_.coords, f32[1024,768]{1,0:T(8,128)} %get-tuple-element.378.refs_1_, bf16[512,768]{1,0:T(8,128)(2,1)} %get-tuple-element.323.refs_8_.refs_2_, bf16[512,768]{1,0:T(8,128)(2,1)} %get-tuple-element.324.refs_9_.refs_3_, ...), custom_call_target="tpu_custom_call" | custom-call | flops 1811939328 | bytes 4718592 | tf_op jit(solution)/shard_map/pallas_call | solution.py:397
  311.0 2.7 collective-permute-start.77
  323.7 9.3 %collective-permute-done.78 = bf16[48,1536]{1,0:T(8,128)(2,1)S(1)} collective-permute-done((bf16[48,1536]{1,0:T(8,128)(2,1)S(1)}, bf16[48,1536]{1,0:T(8,128)(2,1)S(1)}, u32[]{:S(2)}, u32[]{:S(2)}) %collective-permute-start.78) | collective-permute-done | bytes 147488 | tf_op jit(solution)/shard_map/ppermute | solution.py:430
  333.1 3.7 collective-permute-start.94
  355.9 7.6 %shard_map.313 = bf16[512,768]{1,0:T(8,128)(2,1)} custom-call(s32[3]{0:T(128)} %pad_add_fusion.refs_1_.refs_0_.coords, f32[1024,768]{1,0:T(8,128)} %get-tuple-element.378.refs_1_, bf16[512,768]{1,0:T(8,128)(2,1)} %get-tuple-element.379.refs_2_, bf16[512,768]{1,0:T(8,128)(2,1)} %get-tuple-element.380.refs_3_, bf16[512,768]{1,0:T(8,128)(2,1)} %get-tuple-element.381.refs_4_, ...), custom_call_target="tpu_custom_call" | custom-call | flops 1811939328 | bytes 4718592 | tf_op jit(solution)/shard_map/pallas_call | solution.py:397
  364.9 3.2 collective-permute-done.85
  383.6 3.6 collective-permute-done.100
  389.0 2.6 collective-permute-start.107
  395.4 5.1 %collective-permute-done.107 = bf16[3,48,384]{2,1,0:T(8,128)(2,1)S(1)} collective-permute-done((bf16[3,48,384]{2,1,0:T(8,128)(2,1)S(1)}, bf16[3,48,384]{2,1,0:T(8,128)(2,1)S(1)}, u32[]{:S(2)}, u32[]{:S(2)}) %collective-permute-start.107) | collective-permute-done | bytes 110624 | tf_op jit(solution)/shard_map/ppermute | solution.py:430
  (458 shorter events, 147.2 us)
Async XLA Ops:
  19.9 23.7 %collective-permute-start.14 = (bf16[2,128,768]{2,1,0:T(8,128)(2,1)}, bf16[2,128,768]{2,1,0:T(8,128)(2,1)S(1)}, u32[]{:S(2)}, u32[]{:S(2)}) collective-permute-start(bf16[2,128,768]{2,1,0:T(8,128)(2,1)} %get-tuple-element.451), channel_id=1, source_target_pairs={{0,1},{1,0},{2,3},{3,2},{4,5},{5,4},{6,7},{7,6},{8,9},{9,8},{10,11... | collective-permute-start | bytes 1179656 | tf_op jit(solution)/shard_map/ppermute | solution.py:430
  19.9 23.7 %collective-permute-start.15 = (bf16[2,128,768]{2,1,0:T(8,128)(2,1)}, bf16[2,128,768]{2,1,0:T(8,128)(2,1)S(1)}, u32[]{:S(2)}, u32[]{:S(2)}) collective-permute-start(bf16[2,128,768]{2,1,0:T(8,128)(2,1)} %get-tuple-element.453), channel_id=1, source_target_pairs={{0,2},{1,3},{2,0},{3,1},{4,6},{5,7},{6,4},{7,5},{8,10},{9,11},{10,... | collective-permute-start | bytes 1179656 | tf_op jit(solution)/shard_map/ppermute | solution.py:430
  22.5 21.2 %collective-permute-start.16 = (bf16[2,128,768]{2,1,0:T(8,128)(2,1)S(1)}, bf16[2,128,768]{2,1,0:T(8,128)(2,1)S(1)}, u32[]{:S(2)}, u32[]{:S(2)}) collective-permute-start(bf16[2,128,768]{2,1,0:T(8,128)(2,1)S(1)} %get-tuple-element.450), channel_id=1, source_target_pairs={{0,3},{1,2},{2,1},{3,0},{4,7},{5,6},{6,5},{7,4},{8,11},{9,10},{10,... | collective-permute-start | bytes 1179656 | tf_op jit(solution)/shard_map/ppermute | solution.py:430
  51.5 23.7 %collective-permute-start.19 = (bf16[4,48,1536]{2,1,0:T(8,128)(2,1)S(1)}, bf16[4,48,1536]{2,1,0:T(8,128)(2,1)}, u32[]{:S(2)}, u32[]{:S(2)}) collective-permute-start(bf16[4,48,1536]{2,1,0:T(8,128)(2,1)S(1)} %bitcast_dynamic-update-slice_fusion.19.refs_5_.refs_6_), channel_id=1, source_target_pairs={{0,2},{2,0},{1,3},{3,1},{4,6},{6,4},{5,7},{7,5},{8,10},{10,8},{9,1... | collective-permute-start | bytes 1769480 | tf_op jit(solution)/shard_map/ppermute | solution.py:430
  52.0 23.2 %collective-permute-start.20 = (bf16[4,48,1536]{2,1,0:T(8,128)(2,1)S(1)}, bf16[4,48,1536]{2,1,0:T(8,128)(2,1)}, u32[]{:S(2)}, u32[]{:S(2)}) collective-permute-start(bf16[4,48,1536]{2,1,0:T(8,128)(2,1)S(1)} %bitcast_dynamic-update-slice_fusion.19.refs_5_.refs_6_), channel_id=1, source_target_pairs={{0,4},{4,0},{1,5},{5,1},{2,6},{6,2},{3,7},{7,3},{8,12},{12,8},{9,1... | collective-permute-start | bytes 1769480 | tf_op jit(solution)/shard_map/ppermute | solution.py:430
  53.4 24.9 %collective-permute-start.17 = (bf16[4,192,384]{2,1,0:T(8,128)(2,1)S(1)}, bf16[4,192,384]{2,1,0:T(8,128)(2,1)S(1)}, u32[]{:S(2)}, u32[]{:S(2)}) collective-permute-start(bf16[4,192,384]{2,1,0:T(8,128)(2,1)S(1)} %bitcast_dynamic-update-slice_fusion.23.refs_4_.refs_14_.refs_5_), channel_id=1, source_target_pairs={{0,2},{2,0},{1,3},{3,1},{4,6},{6,4},{5,7},{7,5},{8,10},{10,8},{9,1... | collective-permute-start | bytes 1769480 | tf_op jit(solution)/shard_map/ppermute | solution.py:430
  89.9 33.6 %collective-permute-start.39 = (bf16[4,2,192,384]{3,2,1,0:T(8,128)(2,1)S(1)}, bf16[4,2,192,384]{3,2,1,0:T(8,128)(2,1)}, u32[]{:S(2)}, u32[]{:S(2)}) collective-permute-start(bf16[4,2,192,384]{3,2,1,0:T(8,128)(2,1)S(1)} %bitcast_dynamic-update-slice_fusion.refs_13_), channel_id=1, source_target_pairs={{0,1},{1,0},{2,3},{3,2},{4,5},{5,4},{6,7},{7,6},{8,9},{9,8},{10,11... | collective-permute-start | bytes 3538952 | tf_op jit(solution)/shard_map/ppermute | solution.py:430
  93.8 29.6 %collective-permute-start.38 = (bf16[4,48,1536]{2,1,0:T(8,128)(2,1)}, bf16[4,48,1536]{2,1,0:T(8,128)(2,1)}, u32[]{:S(2)}, u32[]{:S(2)}) collective-permute-start(bf16[4,48,1536]{2,1,0:T(8,128)(2,1)} %collective-permute-done.20.refs_7_.refs_8_), channel_id=1, source_target_pairs={{0,1},{1,0},{2,3},{3,2},{4,5},{5,4},{6,7},{7,6},{8,9},{9,8},{10,11... | collective-permute-start | bytes 1769480 | tf_op jit(solution)/shard_map/ppermute | solution.py:430
  103.2 20.0 %collective-permute-start.37 = (bf16[4,48,1536]{2,1,0:T(8,128)(2,1)}, bf16[4,48,1536]{2,1,0:T(8,128)(2,1)}, u32[]{:S(2)}, u32[]{:S(2)}) collective-permute-start(bf16[4,48,1536]{2,1,0:T(8,128)(2,1)} %collective-permute-done.19.refs_6_.refs_7_), channel_id=1, source_target_pairs={{0,1},{1,0},{2,3},{3,2},{4,5},{5,4},{6,7},{7,6},{8,9},{9,8},{10,11... | collective-permute-start | bytes 1769480 | tf_op jit(solution)/shard_map/ppermute | solution.py:430
  103.3 20.1 %collective-permute-start.35 = (bf16[2,2,192,384]{3,2,1,0:T(8,128)(2,1)}, bf16[2,2,192,384]{3,2,1,0:T(8,128)(2,1)}, u32[]{:S(2)}, u32[]{:S(2)}) collective-permute-start(bf16[2,2,192,384]{3,2,1,0:T(8,128)(2,1)} %get-tuple-element.463), channel_id=1, source_target_pairs={{0,4},{4,0},{1,5},{5,1},{2,6},{6,2},{3,7},{7,3},{8,12},{12,8},{9,1... | collective-permute-start | bytes 1769480 | tf_op jit(solution)/shard_map/ppermute | solution.py:430
  106.5 18.7 %collective-permute-start.41 = (bf16[2,128,768]{2,1,0:T(8,128)(2,1)}, bf16[2,128,768]{2,1,0:T(8,128)(2,1)S(1)}, u32[]{:S(2)}, u32[]{:S(2)}) collective-permute-start(bf16[2,128,768]{2,1,0:T(8,128)(2,1)} %get-tuple-element.448), channel_id=1, source_target_pairs={{0,1},{1,0},{2,3},{3,2},{4,5},{5,4},{6,7},{7,6},{8,9},{9,8},{10,11... | collective-permute-start | bytes 1179656 | tf_op jit(solution)/shard_map/ppermute | solution.py:430
  123.2 19.4 %collective-permute-start.40 = (bf16[2,2,192,384]{3,2,1,0:T(8,128)(2,1)S(1)}, bf16[2,2,192,384]{3,2,1,0:T(8,128)(2,1)}, u32[]{:S(2)}, u32[]{:S(2)}) collective-permute-start(bf16[2,2,192,384]{3,2,1,0:T(8,128)(2,1)S(1)} %get-tuple-element.462), channel_id=1, source_target_pairs={{0,4},{4,0},{1,5},{5,1},{2,6},{6,2},{3,7},{7,3},{8,12},{12,8},{9,1... | collective-permute-start | bytes 1769480 | tf_op jit(solution)/shard_map/ppermute | solution.py:430
  123.4 19.2 %collective-permute-start.44 = (bf16[4,48,1536]{2,1,0:T(8,128)(2,1)}, bf16[4,48,1536]{2,1,0:T(8,128)(2,1)S(1)}, u32[]{:S(2)}, u32[]{:S(2)}) collective-permute-start(bf16[4,48,1536]{2,1,0:T(8,128)(2,1)} %copy-done.68), channel_id=1, source_target_pairs={{0,1},{1,0},{2,3},{3,2},{4,5},{5,4},{6,7},{7,6},{8,9},{9,8},{10,11... | collective-permute-start | bytes 1769480 | tf_op jit(solution)/shard_map/ppermute | solution.py:430
  123.6 19.1 %collective-permute-start.45 = (bf16[2,2,192,384]{3,2,1,0:T(8,128)(2,1)}, bf16[2,2,192,384]{3,2,1,0:T(8,128)(2,1)}, u32[]{:S(2)}, u32[]{:S(2)}) collective-permute-start(bf16[2,2,192,384]{3,2,1,0:T(8,128)(2,1)} %collective-permute-done.35.refs_14_), channel_id=1, source_target_pairs={{0,1},{1,0},{2,3},{3,2},{4,5},{5,4},{6,7},{7,6},{8,9},{9,8},{10,11... | collective-permute-start | bytes 1769480 | tf_op jit(solution)/shard_map/ppermute | solution.py:430
  195.9 27.4 %collective-permute-start.55 = (bf16[4,4,48,1536]{3,2,1,0:T(8,128)(2,1)}, bf16[4,4,48,1536]{3,2,1,0:T(8,128)(2,1)}, u32[]{:S(2)}, u32[]{:S(2)}) collective-permute-start(bf16[4,4,48,1536]{3,2,1,0:T(8,128)(2,1)} %get-tuple-element.307), channel_id=1, source_target_pairs={{0,1},{1,0},{2,3},{3,2},{4,5},{5,4},{6,7},{7,6},{8,9},{9,8},{10,11... | collective-permute-start | bytes 7077896 | tf_op jit(solution)/shard_map/ppermute | solution.py:430
  199.2 24.0 %collective-permute-start.51 = (bf16[2,192,384]{2,1,0:T(8,128)(2,1)}, bf16[2,192,384]{2,1,0:T(8,128)(2,1)}, u32[]{:S(2)}, u32[]{:S(2)}) collective-permute-start(bf16[2,192,384]{2,1,0:T(8,128)(2,1)} %get-tuple-element.435), channel_id=1, source_target_pairs={{0,4},{4,0},{1,5},{5,1},{2,6},{6,2},{3,7},{7,3},{8,12},{12,8},{9,1... | collective-permute-start | bytes 884744 | tf_op jit(solution)/shard_map/ppermute | solution.py:430
  201.1 22.1 %collective-permute-start.52 = (bf16[2,192,384]{2,1,0:T(8,128)(2,1)}, bf16[2,192,384]{2,1,0:T(8,128)(2,1)}, u32[]{:S(2)}, u32[]{:S(2)}) collective-permute-start(bf16[2,192,384]{2,1,0:T(8,128)(2,1)} %get-tuple-element.434), channel_id=1, source_target_pairs={{0,2},{2,0},{1,3},{3,1},{4,6},{6,4},{5,7},{7,5},{8,10},{10,8},{9,1... | collective-permute-start | bytes 884744 | tf_op jit(solution)/shard_map/ppermute | solution.py:430
  201.7 21.5 %collective-permute-start.53 = (bf16[2,192,384]{2,1,0:T(8,128)(2,1)}, bf16[2,192,384]{2,1,0:T(8,128)(2,1)S(1)}, u32[]{:S(2)}, u32[]{:S(2)}) collective-permute-start(bf16[2,192,384]{2,1,0:T(8,128)(2,1)} %get-tuple-element.433), channel_id=1, source_target_pairs={{0,2},{2,0},{1,3},{3,1},{4,6},{6,4},{5,7},{7,5},{8,10},{10,8},{9,1... | collective-permute-start | bytes 884744 | tf_op jit(solution)/shard_map/ppermute | solution.py:430
  203.1 20.1 %collective-permute-start.54 = (bf16[2,192,384]{2,1,0:T(8,128)(2,1)}, bf16[2,192,384]{2,1,0:T(8,128)(2,1)}, u32[]{:S(2)}, u32[]{:S(2)}) collective-permute-start(bf16[2,192,384]{2,1,0:T(8,128)(2,1)} %get-tuple-element.432), channel_id=1, source_target_pairs={{0,4},{4,0},{1,5},{5,1},{2,6},{6,2},{3,7},{7,3},{8,12},{12,8},{9,1... | collective-permute-start | bytes 884744 | tf_op jit(solution)/shard_map/ppermute | solution.py:430
  230.2 23.6 %collective-permute-start.60 = (bf16[2,48,1536]{2,1,0:T(8,128)(2,1)}, bf16[2,48,1536]{2,1,0:T(8,128)(2,1)S(1)}, u32[]{:S(2)}, u32[]{:S(2)}) collective-permute-start(bf16[2,48,1536]{2,1,0:T(8,128)(2,1)} %get-tuple-element.427), channel_id=1, source_target_pairs={{0,2},{2,0},{1,3},{3,1},{4,6},{6,4},{5,7},{7,5},{8,10},{10,8},{9,1... | collective-permute-start | bytes 884744 | tf_op jit(solution)/shard_map/ppermute | solution.py:430
  231.7 22.8 %collective-permute-start.61 = (bf16[2,48,1536]{2,1,0:T(8,128)(2,1)}, bf16[2,48,1536]{2,1,0:T(8,128)(2,1)}, u32[]{:S(2)}, u32[]{:S(2)}) collective-permute-start(bf16[2,48,1536]{2,1,0:T(8,128)(2,1)} %get-tuple-element.426), channel_id=1, source_target_pairs={{0,4},{4,0},{1,5},{5,1},{2,6},{6,2},{3,7},{7,3},{8,12},{12,8},{9,1... | collective-permute-start | bytes 884744 | tf_op jit(solution)/shard_map/ppermute | solution.py:430
  234.5 20.6 %collective-permute-start.56 = (bf16[2,192,384]{2,1,0:T(8,128)(2,1)}, bf16[2,192,384]{2,1,0:T(8,128)(2,1)}, u32[]{:S(2)}, u32[]{:S(2)}) collective-permute-start(bf16[2,192,384]{2,1,0:T(8,128)(2,1)} %get-tuple-element.431), channel_id=1, source_target_pairs={{0,2},{2,0},{1,3},{3,1},{4,6},{6,4},{5,7},{7,5},{8,10},{10,8},{9,1... | collective-permute-start | bytes 884744 | tf_op jit(solution)/shard_map/ppermute | solution.py:430
  235.5 20.4 %collective-permute-start.57 = (bf16[2,192,384]{2,1,0:T(8,128)(2,1)}, bf16[2,192,384]{2,1,0:T(8,128)(2,1)}, u32[]{:S(2)}, u32[]{:S(2)}) collective-permute-start(bf16[2,192,384]{2,1,0:T(8,128)(2,1)} %get-tuple-element.430), channel_id=1, source_target_pairs={{0,4},{4,0},{1,5},{5,1},{2,6},{6,2},{3,7},{7,3},{8,12},{12,8},{9,1... | collective-permute-start | bytes 884744 | tf_op jit(solution)/shard_map/ppermute | solution.py:430
  253.9 29.5 %collective-permute-start.72 = (bf16[128,768]{1,0:T(8,128)(2,1)}, bf16[128,768]{1,0:T(8,128)(2,1)}, u32[]{:S(2)}, u32[]{:S(2)}) collective-permute-start(bf16[128,768]{1,0:T(8,128)(2,1)} %get-tuple-element.474), channel_id=1, source_target_pairs={{0,1},{1,0},{2,3},{3,2},{4,5},{5,4},{6,7},{7,6},{8,9},{9,8},{10,11... | collective-permute-start | bytes 589832 | tf_op jit(solution)/shard_map/ppermute | solution.py:430
  254.5 32.2 %collective-permute-start.73 = (bf16[128,768]{1,0:T(8,128)(2,1)S(1)}, bf16[128,768]{1,0:T(8,128)(2,1)}, u32[]{:S(2)}, u32[]{:S(2)}) collective-permute-start(bf16[128,768]{1,0:T(8,128)(2,1)S(1)} %copy-done.39), channel_id=1, source_target_pairs={{0,2},{1,3},{2,0},{3,1},{4,6},{5,7},{6,4},{7,5},{8,10},{9,11},{10,... | collective-permute-start | bytes 589832 | tf_op jit(solution)/shard_map/ppermute | solution.py:430
  255.1 33.0 %collective-permute-start.74 = (bf16[128,768]{1,0:T(8,128)(2,1)S(1)}, bf16[128,768]{1,0:T(8,128)(2,1)}, u32[]{:S(2)}, u32[]{:S(2)}) collective-permute-start(bf16[128,768]{1,0:T(8,128)(2,1)S(1)} %copy-done.38), channel_id=1, source_target_pairs={{0,3},{1,2},{2,1},{3,0},{4,7},{5,6},{6,5},{7,4},{8,11},{9,10},{10,... | collective-permute-start | bytes 589832 | tf_op jit(solution)/shard_map/ppermute | solution.py:430
  257.7 31.1 %collective-permute-start.68 = (bf16[2,48,384]{2,1,0:T(8,128)(2,1)}, bf16[2,48,384]{2,1,0:T(8,128)(2,1)}, u32[]{:S(2)}, u32[]{:S(2)}) collective-permute-start(bf16[2,48,384]{2,1,0:T(8,128)(2,1)} %get-tuple-element.461), channel_id=1, source_target_pairs={{0,4},{4,0},{1,5},{5,1},{2,6},{6,2},{3,7},{7,3},{8,12},{12,8},{9,1... | collective-permute-start | bytes 221192 | tf_op jit(solution)/shard_map/ppermute | solution.py:430
  260.3 46.2 %collective-permute-start.66 = (bf16[2,48,1536]{2,1,0:T(8,128)(2,1)}, bf16[2,48,1536]{2,1,0:T(8,128)(2,1)}, u32[]{:S(2)}, u32[]{:S(2)}) collective-permute-start(bf16[2,48,1536]{2,1,0:T(8,128)(2,1)} %get-tuple-element.423), channel_id=1, source_target_pairs={{0,2},{2,0},{1,3},{3,1},{4,6},{6,4},{5,7},{7,5},{8,10},{10,8},{9,1... | collective-permute-start | bytes 884744 | tf_op jit(solution)/shard_map/ppermute | solution.py:430
  283.4 23.1 %collective-permute-start.67 = (bf16[2,48,1536]{2,1,0:T(8,128)(2,1)}, bf16[2,48,1536]{2,1,0:T(8,128)(2,1)}, u32[]{:S(2)}, u32[]{:S(2)}) collective-permute-start(bf16[2,48,1536]{2,1,0:T(8,128)(2,1)} %get-tuple-element.422), channel_id=1, source_target_pairs={{0,4},{4,0},{1,5},{5,1},{2,6},{6,2},{3,7},{7,3},{8,12},{12,8},{9,1... | collective-permute-start | bytes 884744 | tf_op jit(solution)/shard_map/ppermute | solution.py:430
  313.7 19.3 %collective-permute-start.75 = (bf16[4,4,3,48,384]{4,3,2,1,0:T(8,128)(2,1)S(1)}, bf16[4,4,3,48,384]{4,3,2,1,0:T(8,128)(2,1)S(1)}, u32[]{:S(2)}, u32[]{:S(2)}) collective-permute-start(bf16[4,4,3,48,384]{4,3,2,1,0:T(8,128)(2,1)S(1)} %copy-done.66), channel_id=1, source_target_pairs={{0,1},{1,0},{2,3},{3,2},{4,5},{5,4},{6,7},{7,6},{8,9},{9,8},{10,11... | collective-permute-start | bytes 5308424 | tf_op jit(solution)/shard_map/ppermute | solution.py:430
  348.8 19.5 %collective-permute-start.86 = (bf16[2,3,48,384]{3,2,1,0:T(8,128)(2,1)S(1)}, bf16[2,3,48,384]{3,2,1,0:T(8,128)(2,1)S(1)}, u32[]{:S(2)}, u32[]{:S(2)}) collective-permute-start(bf16[2,3,48,384]{3,2,1,0:T(8,128)(2,1)S(1)} %get-tuple-element.443), channel_id=1, source_target_pairs={{0,4},{4,0},{1,5},{5,1},{2,6},{6,2},{3,7},{7,3},{8,12},{12,8},{9,1... | collective-permute-start | bytes 663560 | tf_op jit(solution)/shard_map/ppermute | solution.py:430
  351.0 18.5 %collective-permute-start.87 = (bf16[2,3,48,384]{3,2,1,0:T(8,128)(2,1)S(1)}, bf16[2,3,48,384]{3,2,1,0:T(8,128)(2,1)S(1)}, u32[]{:S(2)}, u32[]{:S(2)}) collective-permute-start(bf16[2,3,48,384]{3,2,1,0:T(8,128)(2,1)S(1)} %get-tuple-element.442), channel_id=1, source_target_pairs={{0,2},{2,0},{1,3},{3,1},{4,6},{6,4},{5,7},{7,5},{8,10},{10,8},{9,1... | collective-permute-start | bytes 663560 | tf_op jit(solution)/shard_map/ppermute | solution.py:430
  (149 other events, 1448.2 us)
